TPU v7x, 256 devices: a whole 4x4x8 slice. The times are simulated.
256 devices in a mesh: img: 8 (over z_hi, core), txt: 32 (over y, x, z_lo).
Axes of the slice: x: 4, y: 4, z: 8 (z_hi: 4, z_lo: 2; z = z_hi * 2 + z_lo), core: 2. Of those that a mesh axis runs over, the one named last changes fastest.
Arguments:
- image_emb: float32 [8192, 1152], P(('img', 'txt')), may hold values from -6 to 6
- text_emb: float32 [8192, 1152], P(('img', 'txt')), may hold values from -6 to 6
- logit_scale: float32 [1], replicated, may hold values from 8 to 12
- logit_bias: float32 [1], replicated, may hold values from -4 to -2
Outputs:
- loss: float32 [1], replicated
- image_grad: float32 [8192, 1152], P(('img', 'txt'))
- text_grad: float32 [8192, 1152], P(('img', 'txt'))
All inputs are finite; a program needn't handle non-finite values.
Results may differ from a plain program's by a relative error of at most 0.0003.
Values sent between devices are 32-bit elements; how exact they have to be, the bound alone decides.
No kernel may reach another device: no remote copies, remote signals or barrier semaphores. Data moves between devices by JAX's collectives and lax.ppermute only.
A program may use at most 64 MiB of HBM per device.

v0:
```python
import jax
import jax.numpy as jnp
from jax import lax
from jax.sharding import PartitionSpec as P


def normalize(embed):
    inverse = lax.rsqrt(jnp.sum(embed * embed, axis=1, keepdims=True) + 1e-06)
    return (embed * inverse, inverse)


def tile_terms(image_rows, image_ids, text_block, text_ids, temper, offset):
    logits = temper * jnp.dot(image_rows, text_block.T, precision=lax.Precision.HIGHEST) + offset
    label = jnp.where(image_ids[:, None] == text_ids[None, :], 1.0, -1.0).astype(jnp.float32)
    total = jnp.sum(jax.nn.softplus(-label * logits))
    coef = -label * jax.nn.sigmoid(-label * logits)
    image_part = temper * jnp.dot(coef, text_block, precision=lax.Precision.HIGHEST)
    text_part = temper * jnp.dot(coef.T, image_rows, precision=lax.Precision.HIGHEST)
    return (total, image_part, text_part)


def on_device(image_emb, text_emb, logit_scale, logit_bias):
    image_unit, image_inv = normalize(image_emb)
    text_unit, text_inv = normalize(text_emb)
    temper = logit_scale[0]
    offset = logit_bias[0]
    rows_here = image_emb.shape[0]
    count_txt = lax.axis_size("txt")
    count_img = lax.axis_size("img")
    img_pos = lax.axis_index("img")
    txt_pos = lax.axis_index("txt")
    text_block = lax.all_gather(text_unit, "img", axis=0, tiled=True)
    cols = jnp.arange(text_block.shape[0], dtype=jnp.int32)
    text_ids = (cols // rows_here * count_txt + txt_pos) * rows_here + cols % rows_here
    image_block = lax.all_gather(image_unit, "txt", axis=0, tiled=True)
    image_ids = img_pos * count_txt * rows_here + jnp.arange(image_block.shape[0], dtype=jnp.int32)
    total, image_part, text_part = tile_terms(
        image_block, image_ids, text_block, text_ids, temper, offset
    )
    image_unit_grad = lax.psum_scatter(image_part, "txt", scatter_dimension=0, tiled=True)
    text_unit_grad = lax.psum_scatter(text_part, "img", scatter_dimension=0, tiled=True)
    grand = lax.psum(total, ("img", "txt"))
    pair_count = rows_here * count_img * count_txt
    loss = (grand / pair_count).reshape(1)
    image_grad = (
        image_unit_grad - image_unit * jnp.sum(image_unit * image_unit_grad, axis=1, keepdims=True)
    ) * image_inv
    text_grad = (
        text_unit_grad - text_unit * jnp.sum(text_unit * text_unit_grad, axis=1, keepdims=True)
    ) * text_inv
    return (loss, image_grad, text_grad)


def solution(mesh):
    return jax.shard_map(
        on_device,
        mesh=mesh,
        in_specs=(P(("img", "txt"), None), P(("img", "txt"), None), P(), P()),
        out_specs=(P(), P(("img", "txt"), None), P(("img", "txt"), None)),
        check_vma=False,
    )
```

profile of v0, /device:TPU:64, one launch (start us, length us, event | category | flops | bytes accessed | tf_op | source)
XLA Modules:
  0.0 457.7 jit_solution(16100951009210517958)
XLA Ops:
  7.2 0.0 all-gather.5.cloned.1.call-start
  7.2 1.0 multiply_reduce_fusion.2
  8.2 1.7 broadcast_multiply_fusion
  9.9 0.0 all-gather.5.cloned.1.call-update
  9.9 0.0 all-gather.3.cloned.1.call-start
  10.0 1.0 multiply_reduce_fusion.3
  11.0 1.7 broadcast_multiply_fusion.1
  12.7 0.0 all-gather.3.cloned.1.call-update
  12.7 0.0 reduce-scatter.5.cloned.1.call-start
  14.1 28.8 %all-gather.5.cloned.1.call-done = f32[256,1152]{1,0:T(8,128)} async-done(((f32[32,1152]{1,0:T(8,128)}), f32[256,1152]{1,0:T(8,128)}) %all-gather.5.cloned.1.call-update) | async-done | bytes 1179664 | tf_op jit(solution)/shard_map/all_gather | solution.py:32
  42.9 171.7 %all-gather.3.cloned.1.call-done = f32[1024,1152]{1,0:T(8,128)} async-done(((f32[32,1152]{1,0:T(8,128)}), f32[1024,1152]{1,0:T(8,128)}) %all-gather.3.cloned.1.call-update) | async-done | bytes 4718608 | tf_op jit(solution)/shard_map/all_gather | solution.py:35
  214.6 0.0 copy-start
  214.6 7.9 %fusion.2 = (f32[]{:T(128)}, f32[1024,256]{1,0:T(8,128)S(1)}) fusion(f32[]{:T(128)} %bitcast.10, f32[1024,1152]{1,0:T(8,128)} %all-gather.3.cloned.1.call-done, f32[256,1152]{1,0:T(8,128)} %all-gather.5.cloned.1.call-done, f32[]{:T(128)} %bitcast.7, s32[256]{0:T(256)S(1)} %fusion.5, s32[1024]{0:T(1024)S(1)} %iota_add_fusion), kind=kOutput, calls=%fused_computation.6 | convolution fusion | flops 3627286528 | bytes 6951948 | tf_op jit(solution)/shard_map/dot_general | solution.py:13
  222.5 0.0 copy-start.3
  222.5 0.0 copy-done
  222.5 5.7 %convolution_multiply_fusion.1 = f32[256,1152]{1,0:T(8,128)} fusion(f32[1024,1152]{1,0:T(8,128)S(1)} %copy-done, f32[]{:T(128)} %bitcast.9, f32[1024,256]{1,0:T(8,128)S(1)} %get-tuple-element.4, s32[256]{0:T(256)S(1)} %fusion.5, s32[1024]{0:T(1024)S(1)} %iota_add_fusion), kind=kOutput, calls=%fused_computation.2 | convolution fusion | flops 3626008576 | bytes 6951940 | tf_op jit(solution)/shard_map/dot_general | solution.py:18
  228.2 0.0 reduce-scatter.5.cloned.1.call-update
  228.2 0.0 reduce-scatter.3.cloned.1.call-start
  228.3 0.0 copy-done.3
  228.3 0.0 copy-start.1
  228.3 0.0 copy-start.2
  228.3 6.3 %convolution_multiply_fusion = f32[1024,1152]{1,0:T(8,128)} fusion(f32[256,1152]{1,0:T(8,128)S(1)} %copy-done.3, f32[]{:T(128)} %bitcast.8, f32[1024,256]{1,0:T(8,128)S(1)} %get-tuple-element.4, s32[256]{0:T(256)S(1)} %fusion.5, s32[1024]{0:T(1024)S(1)} %iota_add_fusion), kind=kOutput, calls=%fused_computation | convolution fusion | flops 3626893312 | bytes 6951940 | tf_op jit(solution)/shard_map/dot_general | solution.py:17
  234.6 0.0 reduce-scatter.3.cloned.1.call-update
  234.6 74.3 %psum.7 = f32[]{:T(128)} all-reduce(f32[]{:T(128)} %get-tuple-element.3), channel_id=1, replica_groups=mesh['img'=8,'txt'=32] {'img','txt'}, use_global_device_ids=true, to_apply=%region_3.4 | all-reduce | flops 1 | bytes 8 | tf_op jit(solution)/shard_map/psum | solution.py:42
  309.6 0.0 reduce-scatter.5.cloned.1.call-done
  309.6 0.0 copy-done.1
  309.6 1.1 multiply_reduce_fusion
  310.7 1.7 subtract_multiply_fusion
  312.4 134.9 %reduce-scatter.3.cloned.1.call-done = f32[32,1152]{1,0:T(8,128)} async-done(((f32[1024,1152]{1,0:T(8,128)}), f32[32,1152]{1,0:T(8,128)}) %reduce-scatter.3.cloned.1.call-update) | async-done | bytes 147472 | tf_op jit(solution)/shard_map/reduce_scatter | solution.py:40
  447.3 0.0 copy-done.2
  447.3 1.1 multiply_reduce_fusion.1
  448.4 1.7 subtract_multiply_fusion.1
  (4 shorter events, 0.0 us)
Async XLA Ops:
  7.2 35.7 %all-gather.5.cloned.1.call-start = ((), (), s32[]{:S(2)}) async-start(), calls=%async_computation.3 | async-start | bytes 1327104 | tf_op jit(solution)/shard_map/all_gather | solution.py:32
  9.9 204.6 %all-gather.3.cloned.1.call-start = ((), (), s32[]{:S(2)}) async-start(), calls=%async_computation.2 | async-start | bytes 4866048 | tf_op jit(solution)/shard_map/all_gather | solution.py:35
  12.7 296.9 %reduce-scatter.5.cloned.1.call-start = ((), (), s32[]{:S(2)}) async-start(), calls=%async_computation.5 | async-start | bytes 1327104 | tf_op jit(solution)/shard_map/reduce_scatter | solution.py:41
  214.6 7.9 %copy-start = (f32[1024,1152]{1,0:T(8,128)S(1)}, f32[1024,1152]{1,0:T(8,128)}, u32[]{:S(2)}) copy-start(f32[1024,1152]{1,0:T(8,128)} %all-gather.3.cloned.1.call-done) | copy-start | bytes 14155780
  222.5 5.8 %copy-start.3 = (f32[256,1152]{1,0:T(8,128)S(1)}, f32[256,1152]{1,0:T(8,128)}, u32[]{:S(2)}) copy-start(f32[256,1152]{1,0:T(8,128)} %all-gather.5.cloned.1.call-done) | copy-start | bytes 3538948
  228.2 219.1 %reduce-scatter.3.cloned.1.call-start = ((), (), s32[]{:S(2)}) async-start(), calls=%async_computation.4 | async-start | bytes 4866048 | tf_op jit(solution)/shard_map/reduce_scatter | solution.py:40
  228.3 81.3 %copy-start.1 = (f32[32,1152]{1,0:T(8,128)S(1)}, f32[32,1152]{1,0:T(8,128)}, u32[]{:S(2)}) copy-start(f32[32,1152]{1,0:T(8,128)} %param.5) | copy-start | bytes 442372
  228.3 219.0 %copy-start.2 = (f32[32,1152]{1,0:T(8,128)S(1)}, f32[32,1152]{1,0:T(8,128)}, u32[]{:S(2)}) copy-start(f32[32,1152]{1,0:T(8,128)} %param.4) | copy-start | bytes 442372
Sparse Core Ops, SparseCore 0:
  10.4 32.4 all-gather.4
  45.2 169.3 all-gather.2
  228.4 35.4 reduce-scatter.4
  266.3 180.9 reduce-scatter.2
where the time goes:
time: 458 us
  waiting for transfers between devices  335 us (73%)
  blocking collectives  74.3 us (16%)
  matrix products  19.9 us (4%)
  between operations  16.9 us (4%)
  other arithmetic  10.9 us (2%)
    all_gather x1, waiting for transfers between devices, on_device(): image_block = lax.all_gather(image_unit, 'txt', axis=0, tiled=True)  172 us
    reduce_scatter x1, waiting for transfers between devices, on_device(): lax.psum_scatter(image_part, 'txt', scatter_dimension=0, tiled=True)  135 us
    psum x1, blocking collectives, on_device(): grand = lax.psum(total, ('img', 'txt'))  74.3 us
    all_gather x1, waiting for transfers between devices, on_device(): text_block = lax.all_gather(text_unit, 'img', axis=0, tiled=True)  28.8 us
  transfers between devices with their start and end apart: 4, of which 3 were waited for; matrix products, arithmetic and copies ran while one was open for 3% of the time, Pallas kernels for 0%

commit v1 on v0

v1 whole, which is shorter than its diff:
```python
import itertools
import jax
import jax.numpy as jnp
from jax import lax
from jax.sharding import PartitionSpec as P

AXES = ("img", "txt")
NX, NY, NZ = 4, 4, 8
HIGH = lax.Precision.HIGH


def place(z, y, x, core):
    return ((z // 2) * 2 + core) * 32 + (y * NX + x) * 2 + z % 2


def pairs(target):
    out = []
    for z, y, x, core in itertools.product(range(NZ), range(NY), range(NX), range(2)):
        tz, ty, tx, tc = target(z, y, x, core)
        out.append((place(z, y, x, core), place(tz % NZ, ty % NY, tx % NX, tc)))
    return out


def send(value, target):
    return lax.ppermute(value, AXES, pairs(target))


def swap(value):
    return send(value, lambda z, y, x, core: (z, y, x, 1 - core))


def first(value, d):
    return send(value, lambda z, y, x, core: (z, y, x + d, core) if core == 0 else (z, y + d, x, core))


def second(value, d):
    return send(value, lambda z, y, x, core: (z, y + d, x, core) if core == 0 else (z, y, x + d, core))


def along_z(value, d):
    return send(value, lambda z, y, x, core: (z + d if core == 0 else z - d, y, x, core))


STEPS = (1, 3, 2)


def normalize(embed):
    inverse = lax.rsqrt(jnp.sum(embed * embed, axis=1, keepdims=True) + 1e-06)
    return (embed * inverse, inverse)


def gather_image(block):
    four = jnp.concatenate([block] + [first(block, d) for d in STEPS])
    return jnp.concatenate([four] + [second(four, d) for d in STEPS])


def gather_text(block):
    pair = jnp.concatenate([block, swap(block)])
    chain = []
    held = pair
    for step in range(4):
        held = along_z(held if step < 3 else held[: block.shape[0]], 1)
        chain.append(held)
    chain = jnp.concatenate(chain)
    return jnp.concatenate([pair, chain, swap(chain)])


def scatter_image(part, rows):
    four = [part[4 * rows * i : 4 * rows * (i + 1)] for i in range(4)]
    got = [second(four[i + 1], -d) for i, d in enumerate(STEPS)]
    total = four[0] + got[0] + got[1] + got[2]
    one = [total[rows * i : rows * (i + 1)] for i in range(4)]
    got = [first(one[i + 1], -d) for i, d in enumerate(STEPS)]
    return one[0] + got[0] + got[1] + got[2]


def scatter_text(part, rows):
    other = swap(jnp.concatenate([part[rows : 2 * rows], part[9 * rows :]]))
    own = part[:rows] + other[:rows]
    chain = part[2 * rows : 9 * rows] + other[rows:]
    held = along_z(chain[6 * rows :], -1)
    held = along_z(chain[4 * rows : 6 * rows] + jnp.concatenate([held, jnp.zeros_like(held)]), -1)
    held = along_z(chain[2 * rows : 4 * rows] + held, -1)
    held = along_z(chain[: 2 * rows] + held, -1)
    return own + held[:rows] + swap(held[rows:])


def sum_all(value):
    value = value + swap(value)
    for bit in (1, 2):
        value = value + send(value, lambda z, y, x, core: (z, y, x ^ bit, core))
        value = value + send(value, lambda z, y, x, core: (z, y ^ bit, x, core))
    for bit in (1, 2, 4):
        value = value + send(value, lambda z, y, x, core: (z ^ bit, y, x, core))
    return value


def on_device(image_emb, text_emb, logit_scale, logit_bias):
    rows = image_emb.shape[0]
    image_unit, image_inv = normalize(image_emb)
    text_unit, text_inv = normalize(text_emb)
    temper = logit_scale[0]
    offset = logit_bias[0]
    texts = gather_text(text_unit)
    images = gather_image(image_unit)

    logits = temper * jnp.dot(images, texts.T, precision=HIGH) + offset
    row = lax.broadcasted_iota(jnp.int32, logits.shape, 0)
    col = lax.broadcasted_iota(jnp.int32, logits.shape, 1)
    label = jnp.where((row == col) & (row < rows), 1.0, -1.0).astype(jnp.float32)
    total = jnp.sum(jax.nn.softplus(-label * logits))
    coef = -label * jax.nn.sigmoid(-label * logits)
    image_part = temper * jnp.dot(coef, texts, precision=HIGH)
    text_part = temper * jnp.dot(coef.T, images, precision=HIGH)

    text_unit_grad = scatter_text(text_part, rows)
    image_unit_grad = scatter_image(image_part, rows)
    loss = (sum_all(total.reshape(1)) / (rows * 2 * NX * NY * NZ)).reshape(1)
    image_grad = (
        image_unit_grad - image_unit * jnp.sum(image_unit * image_unit_grad, axis=1, keepdims=True)
    ) * image_inv
    text_grad = (
        text_unit_grad - text_unit * jnp.sum(text_unit * text_unit_grad, axis=1, keepdims=True)
    ) * text_inv
    return (loss, image_grad, text_grad)


def solution(mesh):
    return jax.shard_map(
        on_device,
        mesh=mesh,
        in_specs=(P(("img", "txt"), None), P(("img", "txt"), None), P(), P()),
        out_specs=(P(), P(("img", "txt"), None), P(("img", "txt"), None)),
        check_vma=False,
    )
```

time: 458 us -> 131 us (0.29)
  the two profiles are of different devices: /device:TPU:64 before, /device:TPU:8 now
where the time goes in v1:
time: 131 us; the launch traced here: 129 us
  waiting for transfers between devices  56.4 us (43%)
  starting transfers between devices  47.2 us (36%)
  between operations  9.06 us (7%)
  matrix products  8.84 us (7%)
  other arithmetic  6.55 us (5%)
    ppermute x32, waiting for transfers between devices, send(): return lax.ppermute(value, AXES, pairs(target))  56.4 us
    ppermute x32, starting transfers between devices, send(): return lax.ppermute(value, AXES, pairs(target))  47.2 us
    dot_general x1, matrix products, on_device(): logits = temper * jnp.dot(images, texts.T, precision=HIGH) + offset  3.61 us
    dot_general x1, matrix products, on_device(): text_part = temper * jnp.dot(coef.T, images, precision=HIGH)  2.68 us
  transfers between devices with their start and end apart: 32, of which 20 were waited for; matrix products, arithmetic and copies ran while one was open for 5% of the time, Pallas kernels for 0%

profile of v1, /device:TPU:8, one launch (start us, length us, event | category | flops | bytes accessed | tf_op | source)
XLA Modules:
  0.0 128.6 jit_solution(14285336227872592562)
XLA Ops:
  0.6 1.0 multiply_reduce_fusion.2
  1.7 1.0 constant_dynamic-update-slice_fusion.13
  2.8 1.0 multiply_reduce_fusion.3
  3.8 1.0 constant_dynamic-update-slice_fusion.6
  4.8 1.6 %collective-permute-start = (f32[32,1152]{1,0:T(8,128)S(1)}, f32[32,1152]{1,0:T(8,128)S(1)}, u32[]{:S(2)}, u32[]{:S(2)}) collective-permute-start(f32[32,1152]{1,0:T(8,128)S(1)} %get-tuple-element.10), channel_id=1, source_target_pairs={{0,2},{32,40},{2,4},{34,42},{4,6},{36,44},{6,0},{38,46},{8,10},{40... | collective-permute-start | bytes 442376 | tf_op jit(solution)/shard_map/ppermute | solution.py:25
  6.4 1.7 %collective-permute-start.1 = (f32[32,1152]{1,0:T(8,128)S(1)}, f32[32,1152]{1,0:T(8,128)S(1)}, u32[]{:S(2)}, u32[]{:S(2)}) collective-permute-start(f32[32,1152]{1,0:T(8,128)S(1)} %get-tuple-element.10), channel_id=1, source_target_pairs={{0,6},{32,56},{2,0},{34,58},{4,2},{36,60},{6,4},{38,62},{8,14},{40... | collective-permute-start | bytes 442376 | tf_op jit(solution)/shard_map/ppermute | solution.py:25
  8.1 1.8 %collective-permute-start.2 = (f32[32,1152]{1,0:T(8,128)S(1)}, f32[32,1152]{1,0:T(8,128)S(1)}, u32[]{:S(2)}, u32[]{:S(2)}) collective-permute-start(f32[32,1152]{1,0:T(8,128)S(1)} %get-tuple-element.10), channel_id=1, source_target_pairs={{0,4},{32,48},{2,6},{34,50},{4,0},{36,52},{6,2},{38,54},{8,12},{40... | collective-permute-start | bytes 442376 | tf_op jit(solution)/shard_map/ppermute | solution.py:25
  11.3 2.0 %collective-permute-start.7 = (f32[64,1152]{1,0:T(8,128)S(1)}, f32[64,1152]{1,0:T(8,128)S(1)}, u32[]{:S(2)}, u32[]{:S(2)}) collective-permute-start(f32[64,1152]{1,0:T(8,128)S(1)} %pad_maximum_fusion.3), channel_id=1, source_target_pairs={{0,1},{32,225},{2,3},{34,227},{4,5},{36,229},{6,7},{38,231},{8,9},... | collective-permute-start | bytes 884744 | tf_op jit(solution)/shard_map/ppermute | solution.py:25
  13.3 1.5 %collective-permute-done.2 = f32[32,1152]{1,0:T(8,128)S(1)} collective-permute-done((f32[32,1152]{1,0:T(8,128)S(1)}, f32[32,1152]{1,0:T(8,128)S(1)}, u32[]{:S(2)}, u32[]{:S(2)}) %collective-permute-start.2) | collective-permute-done | bytes 147488 | tf_op jit(solution)/shard_map/ppermute | solution.py:25
  14.8 1.7 %collective-permute-start.3 = (f32[128,1152]{1,0:T(8,128)S(1)}, f32[128,1152]{1,0:T(8,128)S(1)}, u32[]{:S(2)}, u32[]{:S(2)}) collective-permute-start(f32[128,1152]{1,0:T(8,128)S(1)} %pad_maximum_fusion.2), channel_id=1, source_target_pairs={{0,8},{32,34},{2,10},{34,36},{4,12},{36,38},{6,14},{38,32},{8,16},... | collective-permute-start | bytes 1769480 | tf_op jit(solution)/shard_map/ppermute | solution.py:25
  16.5 0.7 collective-permute-start.4
  17.2 2.0 %collective-permute-start.5 = (f32[128,1152]{1,0:T(8,128)S(1)}, f32[128,1152]{1,0:T(8,128)S(1)}, u32[]{:S(2)}, u32[]{:S(2)}) collective-permute-start(f32[128,1152]{1,0:T(8,128)S(1)} %pad_maximum_fusion.2), channel_id=1, source_target_pairs={{0,16},{32,36},{2,18},{34,38},{4,20},{36,32},{6,22},{38,34},{8,24}... | collective-permute-start | bytes 1769480 | tf_op jit(solution)/shard_map/ppermute | solution.py:25
  19.2 2.7 %collective-permute-done.7 = f32[64,1152]{1,0:T(8,128)S(1)} collective-permute-done((f32[64,1152]{1,0:T(8,128)S(1)}, f32[64,1152]{1,0:T(8,128)S(1)}, u32[]{:S(2)}, u32[]{:S(2)}) %collective-permute-start.7) | collective-permute-done | bytes 294944 | tf_op jit(solution)/shard_map/ppermute | solution.py:25
  22.0 7.9 %collective-permute-done.8 = f32[64,1152]{1,0:T(8,128)S(1)} collective-permute-done((f32[64,1152]{1,0:T(8,128)S(1)}, f32[64,1152]{1,0:T(8,128)S(1)}, u32[]{:S(2)}, u32[]{:S(2)}) %collective-permute-start.8) | collective-permute-done | bytes 294944 | tf_op jit(solution)/shard_map/ppermute | solution.py:25
  29.9 7.9 %collective-permute-done.9 = f32[64,1152]{1,0:T(8,128)S(1)} collective-permute-done((f32[64,1152]{1,0:T(8,128)S(1)}, f32[64,1152]{1,0:T(8,128)S(1)}, u32[]{:S(2)}, u32[]{:S(2)}) %collective-permute-start.9) | collective-permute-done | bytes 294944 | tf_op jit(solution)/shard_map/ppermute | solution.py:25
  38.0 6.3 %collective-permute-done.10 = f32[32,1152]{1,0:T(8,128)S(1)} collective-permute-done((f32[32,1152]{1,0:T(8,128)S(1)}, f32[32,1152]{1,0:T(8,128)S(1)}, u32[]{:S(2)}, u32[]{:S(2)}) %collective-permute-start.10) | collective-permute-done | bytes 147488 | tf_op jit(solution)/shard_map/ppermute | solution.py:25
  44.8 2.4 %collective-permute-done.11 = f32[224,1152]{1,0:T(8,128)S(1)} collective-permute-done((f32[224,1152]{1,0:T(8,128)S(1)}, f32[224,1152]{1,0:T(8,128)S(1)}, u32[]{:S(2)}, u32[]{:S(2)}) %collective-permute-start.11) | collective-permute-done | bytes 1032224 | tf_op jit(solution)/shard_map/ppermute | solution.py:25
  47.3 3.6 %fusion.2 = (f32[]{:T(128)}, f32[512,512]{1,0:T(8,128)S(1)}) fusion(f32[]{:T(128)} %bitcast.10, f32[512,1152]{1,0:T(8,128)S(1)} %constant_dynamic-update-slice_fusion, f32[512,1152]{1,0:T(8,128)S(1)} %constant_dynamic-update-slice_fusion.7, f32[]{:T(128)} %bitcast.7, pred[512]{0:T(512)(128)(4,1)S(1)} %iota_compare_fusion.1), kind=kOutput, calls=%fused_computation.7 | convolution fusion | flops 1815609344 | bytes 5767692 | tf_op jit(solution)/shard_map/dot_general | solution.py:107
  50.9 2.7 %convolution_multiply_fusion = f32[512,1152]{1,0:T(8,128)S(1)} fusion(f32[512,1152]{1,0:T(8,128)S(1)} %constant_dynamic-update-slice_fusion, f32[]{:T(128)} %bitcast.9, f32[512,512]{1,0:T(8,128)S(1)} %get-tuple-element.18, pred[512]{0:T(512)(128)(4,1)S(1)} %iota_compare_fusion.1), kind=kOutput, calls=%fused_computation | convolution fusion | flops 1814626304 | bytes 5767684 | tf_op jit(solution)/shard_map/dot_general | solution.py:114
  54.0 2.5 %convolution_multiply_fusion.1 = f32[512,1152]{1,0:T(8,128)S(1)} fusion(f32[512,1152]{1,0:T(8,128)S(1)} %constant_dynamic-update-slice_fusion.7, f32[]{:T(128)} %bitcast.8, f32[512,512]{1,0:T(8,128)S(1)} %get-tuple-element.18, pred[512]{0:T(512)(128)(4,1)S(1)} %iota_compare_fusion.1), kind=kOutput, calls=%fused_computation.1 | convolution fusion | flops 1814626304 | bytes 5767684 | tf_op jit(solution)/shard_map/dot_general | solution.py:113
  57.1 2.4 %collective-permute-start.22 = (f32[128,1152]{1,0:T(8,128)S(1)}, f32[128,1152]{1,0:T(8,128)S(1)}, u32[]{:S(2)}, u32[]{:S(2)}) collective-permute-start(f32[128,1152]{1,0:T(8,128)S(1)} %get-tuple-element.12), channel_id=1, source_target_pairs={{0,16},{32,36},{2,18},{34,38},{4,20},{36,32},{6,22},{38,34},{8,24}... | collective-permute-start | bytes 1769480 | tf_op jit(solution)/shard_map/ppermute | solution.py:25
  60.0 1.5 %collective-permute-start.20 = (f32[128,1152]{1,0:T(8,128)S(1)}, f32[128,1152]{1,0:T(8,128)S(1)}, u32[]{:S(2)}, u32[]{:S(2)}) collective-permute-start(f32[128,1152]{1,0:T(8,128)S(1)} %get-tuple-element.11), channel_id=1, source_target_pairs={{0,24},{32,38},{2,26},{34,32},{4,28},{36,34},{6,30},{38,36},{8,0},... | collective-permute-start | bytes 1769480 | tf_op jit(solution)/shard_map/ppermute | solution.py:25
  61.5 0.6 collective-permute-done.27
  62.2 1.5 %collective-permute-start.28 = (f32[64,1152]{1,0:T(8,128)S(1)}, f32[64,1152]{1,0:T(8,128)S(1)}, u32[]{:S(2)}, u32[]{:S(2)}) collective-permute-start(f32[64,1152]{1,0:T(8,128)S(1)} %slice_add_fusion.2), channel_id=1, source_target_pairs={{0,193},{32,33},{2,195},{34,35},{4,197},{36,37},{6,199},{38,39},{8... | collective-permute-start | bytes 884744 | tf_op jit(solution)/shard_map/ppermute | solution.py:25
  63.7 5.0 %collective-permute-done.22 = f32[128,1152]{1,0:T(8,128)S(1)} collective-permute-done((f32[128,1152]{1,0:T(8,128)S(1)}, f32[128,1152]{1,0:T(8,128)S(1)}, u32[]{:S(2)}, u32[]{:S(2)}) %collective-permute-start.22) | collective-permute-done | bytes 589856 | tf_op jit(solution)/shard_map/ppermute | solution.py:25
  68.7 6.4 %collective-permute-done.21 = f32[128,1152]{1,0:T(8,128)S(1)} collective-permute-done((f32[128,1152]{1,0:T(8,128)S(1)}, f32[128,1152]{1,0:T(8,128)S(1)}, u32[]{:S(2)}, u32[]{:S(2)}) %collective-permute-start.21) | collective-permute-done | bytes 589856 | tf_op jit(solution)/shard_map/ppermute | solution.py:25
  75.8 1.9 %collective-permute-start.25 = (f32[32,1152]{1,0:T(8,128)S(1)}, f32[32,1152]{1,0:T(8,128)S(1)}, u32[]{:S(2)}, u32[]{:S(2)}) collective-permute-start(f32[32,1152]{1,0:T(8,128)S(1)} %get-tuple-element.15), channel_id=1, source_target_pairs={{0,4},{32,48},{2,6},{34,50},{4,0},{36,52},{6,2},{38,54},{8,12},{40... | collective-permute-start | bytes 442376 | tf_op jit(solution)/shard_map/ppermute | solution.py:25
  78.3 2.6 %collective-permute-start.23 = (f32[32,1152]{1,0:T(8,128)S(1)}, f32[32,1152]{1,0:T(8,128)S(1)}, u32[]{:S(2)}, u32[]{:S(2)}) collective-permute-start(f32[32,1152]{1,0:T(8,128)S(1)} %get-tuple-element.14), channel_id=1, source_target_pairs={{0,6},{32,56},{2,0},{34,58},{4,2},{36,60},{6,4},{38,62},{8,14},{40... | collective-permute-start | bytes 442376 | tf_op jit(solution)/shard_map/ppermute | solution.py:25
  81.0 1.1 collective-permute-done.29
  82.1 1.7 %collective-permute-start.30 = (f32[64,1152]{1,0:T(8,128)S(1)}, f32[64,1152]{1,0:T(8,128)S(1)}, u32[]{:S(2)}, u32[]{:S(2)}) collective-permute-start(f32[64,1152]{1,0:T(8,128)S(1)} %slice_add_fusion.4), channel_id=1, source_target_pairs={{0,193},{32,33},{2,195},{34,35},{4,197},{36,37},{6,199},{38,39},{8... | collective-permute-start | bytes 884744 | tf_op jit(solution)/shard_map/ppermute | solution.py:25
  83.9 1.4 %collective-permute-done.12 = f32[1]{0:T(128)} collective-permute-done((f32[1]{0:T(128)}, f32[1]{0:T(128)}, u32[]{:S(2)}, u32[]{:S(2)}) %collective-permute-start.12) | collective-permute-done | bytes 36 | tf_op jit(solution)/shard_map/ppermute | solution.py:25
  86.5 1.8 %collective-permute-start.13 = (f32[1]{0:T(128)}, f32[1]{0:T(128)}, u32[]{:S(2)}, u32[]{:S(2)}) collective-permute-start(f32[1]{0:T(128)} %add.99), channel_id=1, source_target_pairs={{0,2},{32,34},{2,0},{34,32},{4,6},{36,38},{6,4},{38,36},{8,10},{40... | collective-permute-start | bytes 20 | tf_op jit(solution)/shard_map/ppermute | solution.py:25
  88.4 1.9 %collective-permute-done.13 = f32[1]{0:T(128)} collective-permute-done((f32[1]{0:T(128)}, f32[1]{0:T(128)}, u32[]{:S(2)}, u32[]{:S(2)}) %collective-permute-start.13) | collective-permute-done | bytes 36 | tf_op jit(solution)/shard_map/ppermute | solution.py:25
  90.9 2.7 %collective-permute-start.14 = (f32[1]{0:T(128)}, f32[1]{0:T(128)}, u32[]{:S(2)}, u32[]{:S(2)}) collective-permute-start(f32[1]{0:T(128)} %add.100), channel_id=1, source_target_pairs={{0,8},{32,40},{2,10},{34,42},{4,12},{36,44},{6,14},{38,46},{8,0},{... | collective-permute-start | bytes 20 | tf_op jit(solution)/shard_map/ppermute | solution.py:25
  93.6 1.0 collective-permute-done.14
  95.2 3.2 %collective-permute-start.15 = (f32[1]{0:T(128)}, f32[1]{0:T(128)}, u32[]{:S(2)}, u32[]{:S(2)}) collective-permute-start(f32[1]{0:T(128)} %add.101), channel_id=1, source_target_pairs={{0,4},{32,36},{2,6},{34,38},{4,0},{36,32},{6,2},{38,34},{8,12},{40... | collective-permute-start | bytes 20 | tf_op jit(solution)/shard_map/ppermute | solution.py:25
  98.4 2.0 %collective-permute-done.15 = f32[1]{0:T(128)} collective-permute-done((f32[1]{0:T(128)}, f32[1]{0:T(128)}, u32[]{:S(2)}, u32[]{:S(2)}) %collective-permute-start.15) | collective-permute-done | bytes 36 | tf_op jit(solution)/shard_map/ppermute | solution.py:25
  101.1 3.2 %collective-permute-start.16 = (f32[1]{0:T(128)}, f32[1]{0:T(128)}, u32[]{:S(2)}, u32[]{:S(2)}) collective-permute-start(f32[1]{0:T(128)} %add.102), channel_id=1, source_target_pairs={{0,16},{32,48},{2,18},{34,50},{4,20},{36,52},{6,22},{38,54},{8,24}... | collective-permute-start | bytes 20 | tf_op jit(solution)/shard_map/ppermute | solution.py:25
  104.3 2.0 %collective-permute-done.16 = f32[1]{0:T(128)} collective-permute-done((f32[1]{0:T(128)}, f32[1]{0:T(128)}, u32[]{:S(2)}, u32[]{:S(2)}) %collective-permute-start.16) | collective-permute-done | bytes 36 | tf_op jit(solution)/shard_map/ppermute | solution.py:25
  107.0 1.8 %collective-permute-start.17 = (f32[1]{0:T(128)}, f32[1]{0:T(128)}, u32[]{:S(2)}, u32[]{:S(2)}) collective-permute-start(f32[1]{0:T(128)} %add.103), channel_id=1, source_target_pairs={{0,1},{32,33},{2,3},{34,35},{4,5},{36,37},{6,7},{38,39},{8,9},{40,... | collective-permute-start | bytes 20 | tf_op jit(solution)/shard_map/ppermute | solution.py:25
  108.8 1.9 %collective-permute-done.17 = f32[1]{0:T(128)} collective-permute-done((f32[1]{0:T(128)}, f32[1]{0:T(128)}, u32[]{:S(2)}, u32[]{:S(2)}) %collective-permute-start.17) | collective-permute-done | bytes 36 | tf_op jit(solution)/shard_map/ppermute | solution.py:25
  111.3 3.2 %collective-permute-start.18 = (f32[1]{0:T(128)}, f32[1]{0:T(128)}, u32[]{:S(2)}, u32[]{:S(2)}) collective-permute-start(f32[1]{0:T(128)} %add.104), channel_id=1, source_target_pairs={{0,64},{32,96},{2,66},{34,98},{4,68},{36,100},{6,70},{38,102},{8,7... | collective-permute-start | bytes 20 | tf_op jit(solution)/shard_map/ppermute | solution.py:25
  114.5 1.4 %collective-permute-done.18 = f32[1]{0:T(128)} collective-permute-done((f32[1]{0:T(128)}, f32[1]{0:T(128)}, u32[]{:S(2)}, u32[]{:S(2)}) %collective-permute-start.18) | collective-permute-done | bytes 36 | tf_op jit(solution)/shard_map/ppermute | solution.py:25
  116.6 5.5 %collective-permute-start.19 = (f32[1]{0:T(128)}, f32[1]{0:T(128)}, u32[]{:S(2)}, u32[]{:S(2)}) collective-permute-start(f32[1]{0:T(128)} %add.105), channel_id=1, source_target_pairs={{0,128},{32,160},{2,130},{34,162},{4,132},{36,164},{6,134},{38,166... | collective-permute-start | bytes 20 | tf_op jit(solution)/shard_map/ppermute | solution.py:25
  122.1 2.1 %collective-permute-done.19 = f32[1]{0:T(128)} collective-permute-done((f32[1]{0:T(128)}, f32[1]{0:T(128)}, u32[]{:S(2)}, u32[]{:S(2)}) %collective-permute-start.19) | collective-permute-done | bytes 36 | tf_op jit(solution)/shard_map/ppermute | solution.py:25
  125.2 0.7 subtract_multiply_fusion.1
  125.9 0.6 collective-permute-done.31
  126.7 0.8 subtract_multiply_fusion
  (58 shorter events, 4.3 us)
Async XLA Ops:
  2.7 8.6 %collective-permute-start.6 = (f32[32,1152]{1,0:T(8,128)S(1)}, f32[32,1152]{1,0:T(8,128)S(1)}, u32[]{:S(2)}, u32[]{:S(2)}) collective-permute-start(f32[32,1152]{1,0:T(8,128)S(1)} %get-tuple-element.8), channel_id=1, source_target_pairs={{0,32},{32,0},{2,34},{34,2},{4,36},{36,4},{6,38},{38,6},{8,40},{40... | collective-permute-start | bytes 442376 | tf_op jit(solution)/shard_map/ppermute | solution.py:25
  4.8 8.5 %collective-permute-start = (f32[32,1152]{1,0:T(8,128)S(1)}, f32[32,1152]{1,0:T(8,128)S(1)}, u32[]{:S(2)}, u32[]{:S(2)}) collective-permute-start(f32[32,1152]{1,0:T(8,128)S(1)} %get-tuple-element.10), channel_id=1, source_target_pairs={{0,2},{32,40},{2,4},{34,42},{4,6},{36,44},{6,0},{38,46},{8,10},{40... | collective-permute-start | bytes 442376 | tf_op jit(solution)/shard_map/ppermute | solution.py:25
  6.4 6.9 %collective-permute-start.1 = (f32[32,1152]{1,0:T(8,128)S(1)}, f32[32,1152]{1,0:T(8,128)S(1)}, u32[]{:S(2)}, u32[]{:S(2)}) collective-permute-start(f32[32,1152]{1,0:T(8,128)S(1)} %get-tuple-element.10), channel_id=1, source_target_pairs={{0,6},{32,56},{2,0},{34,58},{4,2},{36,60},{6,4},{38,62},{8,14},{40... | collective-permute-start | bytes 442376 | tf_op jit(solution)/shard_map/ppermute | solution.py:25
  8.1 6.6 %collective-permute-start.2 = (f32[32,1152]{1,0:T(8,128)S(1)}, f32[32,1152]{1,0:T(8,128)S(1)}, u32[]{:S(2)}, u32[]{:S(2)}) collective-permute-start(f32[32,1152]{1,0:T(8,128)S(1)} %get-tuple-element.10), channel_id=1, source_target_pairs={{0,4},{32,48},{2,6},{34,50},{4,0},{36,52},{6,2},{38,54},{8,12},{40... | collective-permute-start | bytes 442376 | tf_op jit(solution)/shard_map/ppermute | solution.py:25
  11.3 10.6 %collective-permute-start.7 = (f32[64,1152]{1,0:T(8,128)S(1)}, f32[64,1152]{1,0:T(8,128)S(1)}, u32[]{:S(2)}, u32[]{:S(2)}) collective-permute-start(f32[64,1152]{1,0:T(8,128)S(1)} %pad_maximum_fusion.3), channel_id=1, source_target_pairs={{0,1},{32,225},{2,3},{34,227},{4,5},{36,229},{6,7},{38,231},{8,9},... | collective-permute-start | bytes 884744 | tf_op jit(solution)/shard_map/ppermute | solution.py:25
  14.8 23.1 %collective-permute-start.3 = (f32[128,1152]{1,0:T(8,128)S(1)}, f32[128,1152]{1,0:T(8,128)S(1)}, u32[]{:S(2)}, u32[]{:S(2)}) collective-permute-start(f32[128,1152]{1,0:T(8,128)S(1)} %pad_maximum_fusion.2), channel_id=1, source_target_pairs={{0,8},{32,34},{2,10},{34,36},{4,12},{36,38},{6,14},{38,32},{8,16},... | collective-permute-start | bytes 1769480 | tf_op jit(solution)/shard_map/ppermute | solution.py:25
  16.5 28.2 %collective-permute-start.4 = (f32[128,1152]{1,0:T(8,128)S(1)}, f32[128,1152]{1,0:T(8,128)S(1)}, u32[]{:S(2)}, u32[]{:S(2)}) collective-permute-start(f32[128,1152]{1,0:T(8,128)S(1)} %pad_maximum_fusion.2), channel_id=1, source_target_pairs={{0,24},{32,38},{2,26},{34,32},{4,28},{36,34},{6,30},{38,36},{8,0},... | collective-permute-start | bytes 1769480 | tf_op jit(solution)/shard_map/ppermute | solution.py:25
  17.2 27.5 %collective-permute-start.5 = (f32[128,1152]{1,0:T(8,128)S(1)}, f32[128,1152]{1,0:T(8,128)S(1)}, u32[]{:S(2)}, u32[]{:S(2)}) collective-permute-start(f32[128,1152]{1,0:T(8,128)S(1)} %pad_maximum_fusion.2), channel_id=1, source_target_pairs={{0,16},{32,36},{2,18},{34,38},{4,20},{36,32},{6,22},{38,34},{8,24}... | collective-permute-start | bytes 1769480 | tf_op jit(solution)/shard_map/ppermute | solution.py:25
  21.9 7.9 %collective-permute-start.8 = (f32[64,1152]{1,0:T(8,128)S(1)}, f32[64,1152]{1,0:T(8,128)S(1)}, u32[]{:S(2)}, u32[]{:S(2)}) collective-permute-start(f32[64,1152]{1,0:T(8,128)S(1)} %collective-permute-done.7), channel_id=1, source_target_pairs={{0,1},{32,225},{2,3},{34,227},{4,5},{36,229},{6,7},{38,231},{8,9},... | collective-permute-start | bytes 884744 | tf_op jit(solution)/shard_map/ppermute | solution.py:25
  29.9 7.9 %collective-permute-start.9 = (f32[64,1152]{1,0:T(8,128)S(1)}, f32[64,1152]{1,0:T(8,128)S(1)}, u32[]{:S(2)}, u32[]{:S(2)}) collective-permute-start(f32[64,1152]{1,0:T(8,128)S(1)} %collective-permute-done.8), channel_id=1, source_target_pairs={{0,1},{32,225},{2,3},{34,227},{4,5},{36,229},{6,7},{38,231},{8,9},... | collective-permute-start | bytes 884744 | tf_op jit(solution)/shard_map/ppermute | solution.py:25
  37.8 6.4 %collective-permute-start.10 = (f32[32,1152]{1,0:T(8,128)S(1)}, f32[32,1152]{1,0:T(8,128)S(1)}, u32[]{:S(2)}, u32[]{:S(2)}) collective-permute-start(f32[32,1152]{1,0:T(8,128)S(1)} %slice.84), channel_id=1, source_target_pairs={{0,1},{32,225},{2,3},{34,227},{4,5},{36,229},{6,7},{38,231},{8,9},... | collective-permute-start | bytes 442376 | tf_op jit(solution)/shard_map/ppermute | solution.py:25
  44.3 2.9 %collective-permute-start.11 = (f32[224,1152]{1,0:T(8,128)S(1)}, f32[224,1152]{1,0:T(8,128)S(1)}, u32[]{:S(2)}, u32[]{:S(2)}) collective-permute-start(f32[224,1152]{1,0:T(8,128)S(1)} %pad_maximum_fusion.1), channel_id=1, source_target_pairs={{0,32},{32,0},{2,34},{34,2},{4,36},{36,4},{6,38},{38,6},{8,40},{40... | collective-permute-start | bytes 3096584 | tf_op jit(solution)/shard_map/ppermute | solution.py:25
  53.8 2.9 %collective-permute-start.26 = (f32[256,1152]{1,0:T(8,128)S(1)}, f32[256,1152]{1,0:T(8,128)S(1)}, u32[]{:S(2)}, u32[]{:S(2)}) collective-permute-start(f32[256,1152]{1,0:T(8,128)S(1)} %pad_maximum_fusion), channel_id=1, source_target_pairs={{0,32},{32,0},{2,34},{34,2},{4,36},{36,4},{6,38},{38,6},{8,40},{40... | collective-permute-start | bytes 3538952 | tf_op jit(solution)/shard_map/ppermute | solution.py:25
  56.9 5.2 %collective-permute-start.27 = (f32[32,1152]{1,0:T(8,128)S(1)}, f32[32,1152]{1,0:T(8,128)S(1)}, u32[]{:S(2)}, u32[]{:S(2)}) collective-permute-start(f32[32,1152]{1,0:T(8,128)S(1)} %slice.102), channel_id=1, source_target_pairs={{0,193},{32,33},{2,195},{34,35},{4,197},{36,37},{6,199},{38,39},{8... | collective-permute-start | bytes 442376 | tf_op jit(solution)/shard_map/ppermute | solution.py:25
  57.1 11.6 %collective-permute-start.22 = (f32[128,1152]{1,0:T(8,128)S(1)}, f32[128,1152]{1,0:T(8,128)S(1)}, u32[]{:S(2)}, u32[]{:S(2)}) collective-permute-start(f32[128,1152]{1,0:T(8,128)S(1)} %get-tuple-element.12), channel_id=1, source_target_pairs={{0,16},{32,36},{2,18},{34,38},{4,20},{36,32},{6,22},{38,34},{8,24}... | collective-permute-start | bytes 1769480 | tf_op jit(solution)/shard_map/ppermute | solution.py:25
  59.5 15.6 %collective-permute-start.21 = (f32[128,1152]{1,0:T(8,128)S(1)}, f32[128,1152]{1,0:T(8,128)S(1)}, u32[]{:S(2)}, u32[]{:S(2)}) collective-permute-start(f32[128,1152]{1,0:T(8,128)S(1)} %get-tuple-element.13), channel_id=1, source_target_pairs={{0,8},{32,34},{2,10},{34,36},{4,12},{36,38},{6,14},{38,32},{8,16},... | collective-permute-start | bytes 1769480 | tf_op jit(solution)/shard_map/ppermute | solution.py:25
  60.0 15.0 %collective-permute-start.20 = (f32[128,1152]{1,0:T(8,128)S(1)}, f32[128,1152]{1,0:T(8,128)S(1)}, u32[]{:S(2)}, u32[]{:S(2)}) collective-permute-start(f32[128,1152]{1,0:T(8,128)S(1)} %get-tuple-element.11), channel_id=1, source_target_pairs={{0,24},{32,38},{2,26},{34,32},{4,28},{36,34},{6,30},{38,36},{8,0},... | collective-permute-start | bytes 1769480 | tf_op jit(solution)/shard_map/ppermute | solution.py:25
  62.2 13.1 %collective-permute-start.28 = (f32[64,1152]{1,0:T(8,128)S(1)}, f32[64,1152]{1,0:T(8,128)S(1)}, u32[]{:S(2)}, u32[]{:S(2)}) collective-permute-start(f32[64,1152]{1,0:T(8,128)S(1)} %slice_add_fusion.2), channel_id=1, source_target_pairs={{0,193},{32,33},{2,195},{34,35},{4,197},{36,37},{6,199},{38,39},{8... | collective-permute-start | bytes 884744 | tf_op jit(solution)/shard_map/ppermute | solution.py:25
  75.3 6.8 %collective-permute-start.29 = (f32[64,1152]{1,0:T(8,128)S(1)}, f32[64,1152]{1,0:T(8,128)S(1)}, u32[]{:S(2)}, u32[]{:S(2)}) collective-permute-start(f32[64,1152]{1,0:T(8,128)S(1)} %slice_add_fusion.3), channel_id=1, source_target_pairs={{0,193},{32,33},{2,195},{34,35},{4,197},{36,37},{6,199},{38,39},{8... | collective-permute-start | bytes 884744 | tf_op jit(solution)/shard_map/ppermute | solution.py:25
  75.8 49.0 %collective-permute-start.25 = (f32[32,1152]{1,0:T(8,128)S(1)}, f32[32,1152]{1,0:T(8,128)S(1)}, u32[]{:S(2)}, u32[]{:S(2)}) collective-permute-start(f32[32,1152]{1,0:T(8,128)S(1)} %get-tuple-element.15), channel_id=1, source_target_pairs={{0,4},{32,48},{2,6},{34,50},{4,0},{36,52},{6,2},{38,54},{8,12},{40... | collective-permute-start | bytes 442376 | tf_op jit(solution)/shard_map/ppermute | solution.py:25
  77.7 47.1 %collective-permute-start.24 = (f32[32,1152]{1,0:T(8,128)S(1)}, f32[32,1152]{1,0:T(8,128)S(1)}, u32[]{:S(2)}, u32[]{:S(2)}) collective-permute-start(f32[32,1152]{1,0:T(8,128)S(1)} %get-tuple-element.16), channel_id=1, source_target_pairs={{0,2},{32,40},{2,4},{34,42},{4,6},{36,44},{6,0},{38,46},{8,10},{40... | collective-permute-start | bytes 442376 | tf_op jit(solution)/shard_map/ppermute | solution.py:25
  78.3 46.6 %collective-permute-start.23 = (f32[32,1152]{1,0:T(8,128)S(1)}, f32[32,1152]{1,0:T(8,128)S(1)}, u32[]{:S(2)}, u32[]{:S(2)}) collective-permute-start(f32[32,1152]{1,0:T(8,128)S(1)} %get-tuple-element.14), channel_id=1, source_target_pairs={{0,6},{32,56},{2,0},{34,58},{4,2},{36,60},{6,4},{38,62},{8,14},{40... | collective-permute-start | bytes 442376 | tf_op jit(solution)/shard_map/ppermute | solution.py:25
  82.1 42.9 %collective-permute-start.30 = (f32[64,1152]{1,0:T(8,128)S(1)}, f32[64,1152]{1,0:T(8,128)S(1)}, u32[]{:S(2)}, u32[]{:S(2)}) collective-permute-start(f32[64,1152]{1,0:T(8,128)S(1)} %slice_add_fusion.4), channel_id=1, source_target_pairs={{0,193},{32,33},{2,195},{34,35},{4,197},{36,37},{6,199},{38,39},{8... | collective-permute-start | bytes 884744 | tf_op jit(solution)/shard_map/ppermute | solution.py:25
  83.9 1.4 %collective-permute-start.12 = (f32[1]{0:T(128)}, f32[1]{0:T(128)}, u32[]{:S(2)}, u32[]{:S(2)}) collective-permute-start(f32[1]{0:T(128)} %bitcast.2), channel_id=1, source_target_pairs={{0,32},{32,0},{2,34},{34,2},{4,36},{36,4},{6,38},{38,6},{8,40},{40... | collective-permute-start | bytes 20 | tf_op jit(solution)/shard_map/ppermute | solution.py:25
  86.5 3.7 %collective-permute-start.13 = (f32[1]{0:T(128)}, f32[1]{0:T(128)}, u32[]{:S(2)}, u32[]{:S(2)}) collective-permute-start(f32[1]{0:T(128)} %add.99), channel_id=1, source_target_pairs={{0,2},{32,34},{2,0},{34,32},{4,6},{36,38},{6,4},{38,36},{8,10},{40... | collective-permute-start | bytes 20 | tf_op jit(solution)/shard_map/ppermute | solution.py:25
  90.9 3.7 %collective-permute-start.14 = (f32[1]{0:T(128)}, f32[1]{0:T(128)}, u32[]{:S(2)}, u32[]{:S(2)}) collective-permute-start(f32[1]{0:T(128)} %add.100), channel_id=1, source_target_pairs={{0,8},{32,40},{2,10},{34,42},{4,12},{36,44},{6,14},{38,46},{8,0},{... | collective-permute-start | bytes 20 | tf_op jit(solution)/shard_map/ppermute | solution.py:25
  95.2 5.2 %collective-permute-start.15 = (f32[1]{0:T(128)}, f32[1]{0:T(128)}, u32[]{:S(2)}, u32[]{:S(2)}) collective-permute-start(f32[1]{0:T(128)} %add.101), channel_id=1, source_target_pairs={{0,4},{32,36},{2,6},{34,38},{4,0},{36,32},{6,2},{38,34},{8,12},{40... | collective-permute-start | bytes 20 | tf_op jit(solution)/shard_map/ppermute | solution.py:25
  101.1 5.2 %collective-permute-start.16 = (f32[1]{0:T(128)}, f32[1]{0:T(128)}, u32[]{:S(2)}, u32[]{:S(2)}) collective-permute-start(f32[1]{0:T(128)} %add.102), channel_id=1, source_target_pairs={{0,16},{32,48},{2,18},{34,50},{4,20},{36,52},{6,22},{38,54},{8,24}... | collective-permute-start | bytes 20 | tf_op jit(solution)/shard_map/ppermute | solution.py:25
  107.0 3.7 %collective-permute-start.17 = (f32[1]{0:T(128)}, f32[1]{0:T(128)}, u32[]{:S(2)}, u32[]{:S(2)}) collective-permute-start(f32[1]{0:T(128)} %add.103), channel_id=1, source_target_pairs={{0,1},{32,33},{2,3},{34,35},{4,5},{36,37},{6,7},{38,39},{8,9},{40,... | collective-permute-start | bytes 20 | tf_op jit(solution)/shard_map/ppermute | solution.py:25
  111.3 4.6 %collective-permute-start.18 = (f32[1]{0:T(128)}, f32[1]{0:T(128)}, u32[]{:S(2)}, u32[]{:S(2)}) collective-permute-start(f32[1]{0:T(128)} %add.104), channel_id=1, source_target_pairs={{0,64},{32,96},{2,66},{34,98},{4,68},{36,100},{6,70},{38,102},{8,7... | collective-permute-start | bytes 20 | tf_op jit(solution)/shard_map/ppermute | solution.py:25
  116.6 7.6 %collective-permute-start.19 = (f32[1]{0:T(128)}, f32[1]{0:T(128)}, u32[]{:S(2)}, u32[]{:S(2)}) collective-permute-start(f32[1]{0:T(128)} %add.105), channel_id=1, source_target_pairs={{0,128},{32,160},{2,130},{34,162},{4,132},{36,164},{6,134},{38,166... | collective-permute-start | bytes 20 | tf_op jit(solution)/shard_map/ppermute | solution.py:25
  125.1 1.5 %collective-permute-start.31 = (f32[32,1152]{1,0:T(8,128)S(1)}, f32[32,1152]{1,0:T(8,128)S(1)}, u32[]{:S(2)}, u32[]{:S(2)}) collective-permute-start(f32[32,1152]{1,0:T(8,128)S(1)} %slice.104), channel_id=1, source_target_pairs={{0,32},{32,0},{2,34},{34,2},{4,36},{36,4},{6,38},{38,6},{8,40},{40... | collective-permute-start | bytes 442376 | tf_op jit(solution)/shard_map/ppermute | solution.py:25

commit v2 on v1

v2 whole, which is shorter than its diff:
```python
import functools
import itertools
import jax
import jax.numpy as jnp
from jax import lax
from jax.experimental import pallas as pl
from jax.experimental.pallas import tpu as pltpu
from jax.sharding import PartitionSpec as P

AXES = ("img", "txt")
NX, NY, NZ = 4, 4, 8


def place(z, y, x, core):
    return ((z // 2) * 2 + core) * 32 + (y * NX + x) * 2 + z % 2


def pairs(target):
    out = []
    for z, y, x, core in itertools.product(range(NZ), range(NY), range(NX), range(2)):
        tz, ty, tx, tc = target(z, y, x, core)
        out.append((place(z, y, x, core), place(tz % NZ, ty % NY, tx % NX, tc)))
    return out


def send(value, target):
    return lax.ppermute(value, AXES, pairs(target))


def swap(value):
    return send(value, lambda z, y, x, core: (z, y, x, 1 - core))


def first(value, d):
    return send(value, lambda z, y, x, core: (z, y, x + d, core) if core == 0 else (z, y + d, x, core))


def second(value, d):
    return send(value, lambda z, y, x, core: (z, y + d, x, core) if core == 0 else (z, y, x + d, core))


def along_z(value, d):
    return send(value, lambda z, y, x, core: (z + d if core == 0 else z - d, y, x, core))


STEPS = (1, 3, 2)
SHEETS = [
    [place(z, k, x, 0) for z in range(NZ) for x in range(NX)] + [place(z, y, k, 1) for z in range(NZ) for y in range(NY)]
    for k in range(NX)
]


def after(values, *others):
    return lax.optimization_barrier((values, others))[0]


NT = (((1,), (1,)), ((), ()))
TN = (((0,), (0,)), ((), ()))
NN = (((1,), (0,)), ((), ()))
VMEM = pl.BlockSpec(memory_space=pltpu.VMEM)
SMEM = pl.BlockSpec(memory_space=pltpu.SMEM)
GRANT = pltpu.CompilerParams(vmem_limit_bytes=40 << 20)


def f32(*shape):
    return jax.ShapeDtypeStruct(shape, jnp.float32)


def b16(*shape):
    return jax.ShapeDtypeStruct(shape, jnp.bfloat16)


def halves(value):
    high = value.astype(jnp.bfloat16)
    return high, (value - high.astype(jnp.float32)).astype(jnp.bfloat16)


def dot3(a, b, dims):
    dot = functools.partial(lax.dot_general, dimension_numbers=dims, preferred_element_type=jnp.float32)
    return dot(a[0], b[0]) + (dot(a[0], b[1]) + dot(a[1], b[0]))


def unit_halves(refs, high, low):
    at = 0
    for ref in refs:
        rows = ref.shape[0]
        raw = ref[...]
        unit = raw * lax.rsqrt(jnp.sum(raw * raw, axis=1, keepdims=True) + 1e-06)
        high[at : at + rows, :], low[at : at + rows, :] = halves(unit)
        at += rows


def pair_terms(logits, own):
    if own:
        row = lax.broadcasted_iota(jnp.int32, logits.shape, 0)
        col = lax.broadcasted_iota(jnp.int32, logits.shape, 1)
        same = (row == col) & (row < own)
        logits = jnp.where(same, -logits, logits)
    small = jnp.exp(-jnp.abs(logits))
    loss = jnp.sum(jnp.maximum(logits, 0.0) + jnp.log1p(small))
    part = 1.0 / (1.0 + small)
    coef = jnp.where(logits >= 0, part, small * part)
    if own:
        coef = jnp.where(same, -coef, coef)
    return loss, coef


def near_kernel(own, scale, bias, *refs):
    i_refs, t_refs = refs[:4], refs[4:9]
    image_part, pay, own_part, one_part, two_part, ihi, ilo, loss, thi, tlo = refs[9:]
    unit_halves(i_refs, ihi, ilo)
    unit_halves(t_refs, thi, tlo)
    images = ihi[...], ilo[...]
    texts = thi[...], tlo[...]
    logits = scale[0] * dot3(images, texts, NT) + bias[0]
    total, coef = pair_terms(logits, own)
    loss[...] = jnp.full(loss.shape, total, jnp.float32)
    coef = halves(coef * scale[0])
    text_part = dot3(coef, images, TN)
    own_part[...] = text_part[:own]
    one_part[...] = text_part[2 * own : 4 * own]
    two_part[...] = text_part[4 * own : 6 * own]
    pay[: 4 * own, :] = text_part[6 * own :]
    pay[4 * own :, :] = text_part[own : 2 * own]
    image_part[...] = dot3(coef, texts, NN)


def far_kernel(scale, bias, ihi, ilo, loss_in, t0, t1, pay, rest, chi, clo, thi, tlo, loss):
    unit_halves((t0, t1), thi, tlo)
    images = ihi[...], ilo[...]
    texts = thi[...], tlo[...]
    logits = scale[0] * dot3(images, texts, NT) + bias[0]
    total, coef = pair_terms(logits, 0)
    loss[...] = loss_in[...] + total
    coef = halves(coef * scale[0])
    chi[...], clo[...] = coef
    text_part = dot3(coef, images, TN)
    count = t0.shape[0]
    rest[...] = text_part[:count]
    pay[...] = text_part[count:]


def last_kernel(chi, clo, thi, tlo, image_in, loss, out0, out1, out2, out3):
    part = dot3((chi[...], clo[...]), (thi[...], tlo[...]), NN) + image_in[...]
    rows = part.shape[0] // 4
    note = jnp.broadcast_to(loss[:, :1], (8, part.shape[1]))
    for k, out in enumerate((out0, out1, out2, out3)):
        out[:rows, :] = part[rows * k : rows * (k + 1)]
        out[rows:, :] = note


def sum_kernel(in0, in1, in2, in3, out0, out1, out2, out3, note):
    total = (in0[...] + in3[...]) + (in1[...] + in2[...])
    rows = (total.shape[0] - 8) // 4
    for k, out in enumerate((out0, out1, out2, out3)):
        out[...] = total[rows * k : rows * (k + 1)]
    note[...] = total[4 * rows :, :128]


def near_call(scale, bias, images, texts):
    own, width = texts[0].shape
    rows, cols = 16 * own, 10 * own
    return pl.pallas_call(
        functools.partial(near_kernel, own),
        out_shape=[f32(rows, width), f32(5 * own, width), f32(own, width), f32(2 * own, width), f32(2 * own, width)]
        + [b16(rows, width), b16(rows, width), f32(8, 128)],
        in_specs=[SMEM, SMEM] + [VMEM] * 9,
        out_specs=[VMEM] * 8,
        scratch_shapes=[pltpu.VMEM((cols, width), jnp.bfloat16)] * 2,
        cost_estimate=pl.CostEstimate(
            flops=18 * rows * cols * width, bytes_accessed=12 * rows * width, transcendentals=rows * cols
        ),
        compiler_params=GRANT,
    )(scale, bias, *images, *texts)


def far_call(scale, bias, ihi, ilo, loss, t0, t1):
    count = t0.shape[0]
    rows, width = ihi.shape
    return pl.pallas_call(
        far_kernel,
        out_shape=[f32(count, width), f32(count, width), b16(rows, 2 * count), b16(rows, 2 * count)]
        + [b16(2 * count, width), b16(2 * count, width), f32(8, 128)],
        in_specs=[SMEM, SMEM] + [VMEM] * 5,
        out_specs=[VMEM] * 7,
        cost_estimate=pl.CostEstimate(
            flops=24 * rows * count * width, bytes_accessed=8 * rows * width, transcendentals=2 * rows * count
        ),
        compiler_params=GRANT,
    )(scale, bias, ihi, ilo, loss, t0, t1)


def last_call(chi, clo, thi, tlo, image_part, loss):
    rows, width = image_part.shape
    return pl.pallas_call(
        last_kernel,
        out_shape=[f32(rows // 4 + 8, width)] * 4,
        in_specs=[VMEM] * 6,
        out_specs=[VMEM] * 4,
        cost_estimate=pl.CostEstimate(
            flops=6 * rows * chi.shape[1] * width, bytes_accessed=8 * rows * width, transcendentals=0
        ),
        compiler_params=GRANT,
    )(chi, clo, thi, tlo, image_part, loss)


def sum_call(parts):
    rows, width = parts[0].shape
    return pl.pallas_call(
        sum_kernel,
        out_shape=[f32((rows - 8) // 4, width)] * 4 + [f32(8, 128)],
        in_specs=[VMEM] * 4,
        out_specs=[VMEM] * 5,
        compiler_params=GRANT,
    )(*parts)


def normalize(embed):
    inverse = lax.rsqrt(jnp.sum(embed * embed, axis=1, keepdims=True) + 1e-06)
    return (embed * inverse, inverse)


def on_device(image_emb, text_emb, logit_scale, logit_bias):
    rows = image_emb.shape[0]
    other = swap(text_emb)
    four = [first(image_emb, d) for d in STEPS]
    pair = jnp.concatenate([text_emb, other])
    one = along_z(pair, 1)
    two = along_z(pair, 2)
    four = jnp.concatenate([image_emb] + four)
    images = [four] + [second(four, d) for d in STEPS]
    far = along_z(jnp.concatenate([one, two[:rows]]), 2)
    near_swap = swap(jnp.concatenate([one, two]))

    image_part, near_pay, own_part, one_part, two_part, ihi, ilo, loss = near_call(
        logit_scale, logit_bias, images, [text_emb, other, one, two, near_swap]
    )
    far = after(far, loss)
    far_swap = swap(far)
    near_back = swap(near_pay)
    far_pay, far_part, chi, clo, thi, tlo, loss = far_call(
        logit_scale, logit_bias, after(ihi, near_back), ilo, loss, far, far_swap
    )
    far_pay = swap(far_pay)
    four = last_call(chi, clo, thi, tlo, image_part, loss)
    far_pay = after(far_part + far_pay, four)
    back = along_z(far_pay, -2)
    four = after(four, far_pay)
    got = [second(four[i + 1], -d) for i, d in enumerate(STEPS)]
    one_part = one_part + near_back[: 2 * rows] + back[: 2 * rows]
    two_part = two_part + near_back[2 * rows : 4 * rows]
    two_part = jnp.concatenate([two_part[:rows] + back[2 * rows :], two_part[rows:]])
    back = along_z(one_part, -1) + along_z(two_part, -2)
    *four, note = sum_call([four[0]] + got)
    got = [first(four[i + 1], -d) for i, d in enumerate(STEPS)]
    notes = jnp.broadcast_to(note[:1, :128].reshape(1, 1, 128), (64, 1, 128))
    notes = lax.all_to_all(notes, AXES, 0, 0, axis_index_groups=SHEETS, tiled=True)
    loss = (jnp.sum(notes[:, 0, 0]) / (rows * 2 * NX * NY * NZ)).reshape(1)
    total = (four[0] + got[2]) + (got[0] + got[1])
    text_unit_grad = own_part + near_back[4 * rows :] + back[:rows] + swap(back[rows:])
    image_unit_grad = total

    image_unit, image_inv = normalize(image_emb)
    text_unit, text_inv = normalize(text_emb)
    image_grad = (
        image_unit_grad - image_unit * jnp.sum(image_unit * image_unit_grad, axis=1, keepdims=True)
    ) * image_inv
    text_grad = (
        text_unit_grad - text_unit * jnp.sum(text_unit * text_unit_grad, axis=1, keepdims=True)
    ) * text_inv
    return (loss, image_grad, text_grad)


def solution(mesh):
    return jax.shard_map(
        on_device,
        mesh=mesh,
        in_specs=(P(("img", "txt"), None), P(("img", "txt"), None), P(), P()),
        out_specs=(P(), P(("img", "txt"), None), P(("img", "txt"), None)),
        check_vma=False,
    )
```

time: 131 us -> 101 us (0.77)
  waiting for transfers between devices: 56.4 us -> 28.7 us
  Pallas kernels: 0 us -> 12 us
  matrix products: 8.84 us -> 0 us
  between operations: 9.06 us -> 3.91 us
  starting transfers between devices: 47.2 us -> 49 us
  other arithmetic: 6.55 us -> 4.95 us
    ppermute x32 -> x24, waiting for transfers between devices: 56.4 us -> 18.9 us  [send(): return lax.ppermute(value, AXES, pairs(target))]
    pallas_call x0 -> x4, Pallas kernels: none -> 12 us  [the longest x1 6.51 us: near_call(): pl.pallas_call(functools.partial(near_kernel, own), out_shape=[f32(rows,...]
    all_to_all x0 -> x1, waiting for transfers between devices: none -> 9.82 us  [on_device(): lax.all_to_all(notes, AXES, 0, 0, axis_index_groups=SHEETS, tiled=True)]
    dot_general x3 -> x0, matrix products: 8.84 us -> none  [the longest x1 3.61 us: on_device(): logits = temper * jnp.dot(images, texts.T, precision=HIGH) + offset]
    all_to_all x0 -> x1, starting transfers between devices: none -> 6.53 us  [on_device(): lax.all_to_all(notes, AXES, 0, 0, axis_index_groups=SHEETS, tiled=True)]
    ppermute x32 -> x24, starting transfers between devices: 47.2 us -> 42.5 us  [send(): return lax.ppermute(value, AXES, pairs(target))]
    unnamed x2 -> x0, other arithmetic: 2.02 us -> none
  transfers between devices with their start and end apart: 32 -> 25, of which waited for: 20 -> 9; matrix products, arithmetic and copies ran while one was open for 5% -> 5% of each run, Pallas kernels for 0% -> 8%
where the time goes in v2:
time: 101 us; the launch traced here: 99.3 us
  starting transfers between devices  49 us (49%)
  waiting for transfers between devices  28.7 us (28%)
  Pallas kernels  12 us (12%)
  other arithmetic  4.95 us (5%)
  between operations  3.91 us (4%)
    ppermute x24, starting transfers between devices, send(): return lax.ppermute(value, AXES, pairs(target))  42.5 us
    ppermute x24, waiting for transfers between devices, send(): return lax.ppermute(value, AXES, pairs(target))  18.9 us
    all_to_all x1, waiting for transfers between devices, on_device(): lax.all_to_all(notes, AXES, 0, 0, axis_index_groups=SHEETS, tiled=True)  9.82 us
    all_to_all x1, starting transfers between devices, on_device(): lax.all_to_all(notes, AXES, 0, 0, axis_index_groups=SHEETS, tiled=True)  6.53 us
    pallas_call x1, Pallas kernels, near_call(): pl.pallas_call(functools.partial(near_kernel, own), out_shape=[f32(rows,...  6.51 us
    pallas_call x1, Pallas kernels, far_call(): pl.pallas_call(far_kernel, out_shape=[f32(count, width), f32(count, width...  4.11 us
    reduce_sum x2, other arithmetic, normalize(): inverse = lax.rsqrt(jnp.sum(embed * embed, axis=1, keepdims=True) + 1e-06)  2.07 us
  transfers between devices with their start and end apart: 25, of which 9 were waited for; matrix products, arithmetic and copies ran while one was open for 5% of the time, Pallas kernels for 8%

profile of v2, /device:TPU:8, one launch (start us, length us, event | category | flops | bytes accessed | tf_op | source)
XLA Modules:
  0.0 99.3 jit_solution(14525708581142227073)
XLA Ops:
  0.6 1.6 %collective-permute-start = (f32[32,1152]{1,0:T(8,128)}, f32[32,1152]{1,0:T(8,128)S(1)}, u32[]{:S(2)}, u32[]{:S(2)}) collective-permute-start(f32[32,1152]{1,0:T(8,128)} %param.4), channel_id=1, source_target_pairs={{0,2},{32,40},{2,4},{34,42},{4,6},{36,44},{6,0},{38,46},{8,10},{40... | collective-permute-start | bytes 442376 | tf_op jit(solution)/shard_map/ppermute | solution.py:27
  2.2 1.7 %collective-permute-start.1 = (f32[32,1152]{1,0:T(8,128)}, f32[32,1152]{1,0:T(8,128)S(1)}, u32[]{:S(2)}, u32[]{:S(2)}) collective-permute-start(f32[32,1152]{1,0:T(8,128)} %param.4), channel_id=1, source_target_pairs={{0,6},{32,56},{2,0},{34,58},{4,2},{36,60},{6,4},{38,62},{8,14},{40... | collective-permute-start | bytes 442376 | tf_op jit(solution)/shard_map/ppermute | solution.py:27
  3.9 1.8 %collective-permute-start.2 = (f32[32,1152]{1,0:T(8,128)}, f32[32,1152]{1,0:T(8,128)S(1)}, u32[]{:S(2)}, u32[]{:S(2)}) collective-permute-start(f32[32,1152]{1,0:T(8,128)} %param.4), channel_id=1, source_target_pairs={{0,4},{32,48},{2,6},{34,50},{4,0},{36,52},{6,2},{38,54},{8,12},{40... | collective-permute-start | bytes 442376 | tf_op jit(solution)/shard_map/ppermute | solution.py:27
  5.8 1.0 %multiply_reduce_fusion.1 = (f32[32]{0:T(128)S(1)}, f32[64,1152]{1,0:T(8,128)S(1)}) fusion(f32[32,1152]{1,0:T(8,128)} %refs_4_.1), kind=kLoop, calls=%fused_computation.12 | loop fusion | flops 73695 | bytes 295424 | tf_op jit(solution)/shard_map/reduce_sum | solution.py:219
  6.8 1.0 %multiply_reduce_fusion.3 = (f32[32]{0:T(128)S(1)}, f32[128,1152]{1,0:T(8,128)S(1)}) fusion(f32[32,1152]{1,0:T(8,128)} %param.4), kind=kLoop, calls=%fused_computation.15 | loop fusion | flops 73695 | bytes 295424 | tf_op jit(solution)/shard_map/reduce_sum | solution.py:219
  7.9 2.0 %collective-permute-start.7 = (f32[64,1152]{1,0:T(8,128)S(1)}, f32[64,1152]{1,0:T(8,128)S(1)}, u32[]{:S(2)}, u32[]{:S(2)}) collective-permute-start(f32[64,1152]{1,0:T(8,128)S(1)} %constant_dynamic-update-slice_fusion.4), channel_id=1, source_target_pairs={{0,1},{32,225},{2,3},{34,227},{4,5},{36,229},{6,7},{38,231},{8,9},... | collective-permute-start | bytes 884744 | tf_op jit(solution)/shard_map/ppermute | solution.py:27
  9.8 3.3 %collective-permute-start.8 = (f32[64,1152]{1,0:T(8,128)S(1)}, f32[64,1152]{1,0:T(8,128)S(1)}, u32[]{:S(2)}, u32[]{:S(2)}) collective-permute-start(f32[64,1152]{1,0:T(8,128)S(1)} %constant_dynamic-update-slice_fusion.4), channel_id=1, source_target_pairs={{0,64},{32,224},{2,66},{34,226},{4,68},{36,228},{6,70},{38,230},{8... | collective-permute-start | bytes 884744 | tf_op jit(solution)/shard_map/ppermute | solution.py:27
  13.2 0.0 copy-start
  13.2 1.7 %collective-permute-start.3 = (f32[128,1152]{1,0:T(8,128)S(1)}, f32[128,1152]{1,0:T(8,128)S(1)}, u32[]{:S(2)}, u32[]{:S(2)}) collective-permute-start(f32[128,1152]{1,0:T(8,128)S(1)} %constant_dynamic-update-slice_fusion.refs_0_), channel_id=1, source_target_pairs={{0,8},{32,34},{2,10},{34,36},{4,12},{36,38},{6,14},{38,32},{8,16},... | collective-permute-start | bytes 1769480 | tf_op jit(solution)/shard_map/ppermute | solution.py:27
  14.9 0.5 collective-permute-start.4
  15.3 2.3 %collective-permute-start.5 = (f32[128,1152]{1,0:T(8,128)S(1)}, f32[128,1152]{1,0:T(8,128)S(1)}, u32[]{:S(2)}, u32[]{:S(2)}) collective-permute-start(f32[128,1152]{1,0:T(8,128)S(1)} %constant_dynamic-update-slice_fusion.refs_0_), channel_id=1, source_target_pairs={{0,16},{32,36},{2,18},{34,38},{4,20},{36,32},{6,22},{38,34},{8,24}... | collective-permute-start | bytes 1769480 | tf_op jit(solution)/shard_map/ppermute | solution.py:27
  17.6 0.9 collective-permute-done.7.refs_6_
  18.5 5.2 %collective-permute-done.8.refs_7_ = f32[64,1152]{1,0:T(8,128)S(1)} collective-permute-done((f32[64,1152]{1,0:T(8,128)S(1)}, f32[64,1152]{1,0:T(8,128)S(1)}, u32[]{:S(2)}, u32[]{:S(2)}) %collective-permute-start.8) | collective-permute-done | bytes 294944 | tf_op jit(solution)/shard_map/ppermute | solution.py:27
  23.7 0.4 collective-permute-start.9
  25.5 2.6 %collective-permute-start.11 = (f32[96,1152]{1,0:T(8,128)S(1)}, f32[96,1152]{1,0:T(8,128)S(1)}, u32[]{:S(2)}, u32[]{:S(2)}) collective-permute-start(f32[96,1152]{1,0:T(8,128)S(1)} %pad_maximum_fusion.1), channel_id=1, source_target_pairs={{0,64},{32,224},{2,66},{34,226},{4,68},{36,228},{6,70},{38,230},{8... | collective-permute-start | bytes 1327112 | tf_op jit(solution)/shard_map/ppermute | solution.py:27
  28.1 3.7 %collective-permute-done.5.refs_3_ = f32[128,1152]{1,0:T(8,128)S(1)} collective-permute-done((f32[128,1152]{1,0:T(8,128)S(1)}, f32[128,1152]{1,0:T(8,128)S(1)}, u32[]{:S(2)}, u32[]{:S(2)}) %collective-permute-start.5) | collective-permute-done | bytes 589856 | tf_op jit(solution)/shard_map/ppermute | solution.py:27
  31.8 6.5 %shard_map.67 = (f32[512,1152]{1,0:T(8,128)S(1)}, f32[160,1152]{1,0:T(8,128)S(1)}, f32[32,1152]{1,0:T(8,128)S(1)}, f32[64,1152]{1,0:T(8,128)S(1)}, f32[64,1152]{...) custom-call(f32[1]{0:T(128)S(6)} %copy.13.scale, ...), custom_call_target="tpu_custom_call" | custom-call | flops 3397386240 | bytes 7077888 | tf_op jit(solution)/shard_map/pallas_call | solution.py:163
  38.3 0.2 collective-permute-start.10
  38.5 1.2 %collective-permute-start.12 = (f32[96,1152]{1,0:T(8,128)S(1)}, f32[96,1152]{1,0:T(8,128)S(1)}, u32[]{:S(2)}, u32[]{:S(2)}) collective-permute-start(f32[96,1152]{1,0:T(8,128)S(1)} %collective-permute-done.11.t0), channel_id=1, source_target_pairs={{0,32},{32,0},{2,34},{34,2},{4,36},{36,4},{6,38},{38,6},{8,40},{40... | collective-permute-start | bytes 1327112 | tf_op jit(solution)/shard_map/ppermute | solution.py:27
  39.8 0.8 collective-permute-done.10
  40.6 0.6 collective-permute-done.12.t1
  41.2 4.1 %shard_map.68 = (f32[96,1152]{1,0:T(8,128)S(1)}, f32[96,1152]{1,0:T(8,128)S(1)}, bf16[512,192]{1,0:T(8,128)(2,1)S(1)}, bf16[512,192]{1,0:T(8,128)(2,1)S(1)}, bf1...) custom-call(f32[1]{0:T(128)S(6)} %copy.13.scale, f32[1]{0:T(128)S(6)} %copy.14.bias, ...), custom_call_target="tpu_custom_call" | custom-call | flops 1358954496 | bytes 4718592 | tf_op jit(solution)/shard_map/pallas_call | solution.py:180
  45.4 0.4 collective-permute-start.13
  45.8 1.2 %shard_map.69 = (f32[136,1152]{1,0:T(8,128)S(1)}, f32[136,1152]{1,0:T(8,128)S(1)}, f32[136,1152]{1,0:T(8,128)S(1)}, f32[136,1152]{1,0:T(8,128)S(1)}) custom-call(bf16[512,192]{1,0:T(8,128)(2,1)S(1)} %get-tuple-element.40.chi, bf16[512,192]{1,0:T(8,128)(2,1)S(1)} %get-tuple-element.41.clo, bf16[192,1152]{1,0:T(8,128)(2,1)S(1)} %get-tuple-element.42.thi, ...), custom_call_target="tpu_custom_call" | custom-call | flops 679477248 | bytes 4718592 | tf_op jit(solution)/shard_map/pallas_call | solution.py:195
  47.0 0.2 collective-permute-done.13
  47.3 4.3 %collective-permute-start.20 = (f32[96,1152]{1,0:T(8,128)S(1)}, f32[96,1152]{1,0:T(8,128)S(1)}, u32[]{:S(2)}, u32[]{:S(2)}) collective-permute-start(f32[96,1152]{1,0:T(8,128)S(1)} %add.52), channel_id=1, source_target_pairs={{0,192},{32,96},{2,194},{34,98},{4,196},{36,100},{6,198},{38,102},... | collective-permute-start | bytes 1327112 | tf_op jit(solution)/shard_map/ppermute | solution.py:27
  51.6 0.5 collective-permute-start.14
  52.1 1.6 %collective-permute-start.15 = (f32[136,1152]{1,0:T(8,128)S(1)}, f32[136,1152]{1,0:T(8,128)S(1)}, u32[]{:S(2)}, u32[]{:S(2)}) collective-permute-start(f32[136,1152]{1,0:T(8,128)S(1)} %get-tuple-element.55), channel_id=1, source_target_pairs={{0,8},{32,34},{2,10},{34,36},{4,12},{36,38},{6,14},{38,32},{8,16},... | collective-permute-start | bytes 1880072 | tf_op jit(solution)/shard_map/ppermute | solution.py:27
  53.7 3.8 %collective-permute-start.16 = (f32[136,1152]{1,0:T(8,128)S(1)}, f32[136,1152]{1,0:T(8,128)S(1)}, u32[]{:S(2)}, u32[]{:S(2)}) collective-permute-start(f32[136,1152]{1,0:T(8,128)S(1)} %get-tuple-element.56), channel_id=1, source_target_pairs={{0,16},{32,36},{2,18},{34,38},{4,20},{36,32},{6,22},{38,34},{8,24}... | collective-permute-start | bytes 1880072 | tf_op jit(solution)/shard_map/ppermute | solution.py:27
  57.5 4.8 %collective-permute-done.20 = f32[96,1152]{1,0:T(8,128)S(1)} collective-permute-done((f32[96,1152]{1,0:T(8,128)S(1)}, f32[96,1152]{1,0:T(8,128)S(1)}, u32[]{:S(2)}, u32[]{:S(2)}) %collective-permute-start.20) | collective-permute-done | bytes 442400 | tf_op jit(solution)/shard_map/ppermute | solution.py:27
  62.2 0.1 slice_add_fusion
  62.4 4.6 %collective-permute-start.22 = (f32[64,1152]{1,0:T(8,128)S(1)}, f32[64,1152]{1,0:T(8,128)S(1)}, u32[]{:S(2)}, u32[]{:S(2)}) collective-permute-start(f32[64,1152]{1,0:T(8,128)S(1)} %pad_maximum_fusion.2), channel_id=1, source_target_pairs={{0,192},{32,96},{2,194},{34,98},{4,196},{36,100},{6,198},{38,102},... | collective-permute-start | bytes 884744 | tf_op jit(solution)/shard_map/ppermute | solution.py:27
  67.0 2.6 %collective-permute-done.16.in3 = f32[136,1152]{1,0:T(8,128)S(1)} collective-permute-done((f32[136,1152]{1,0:T(8,128)S(1)}, f32[136,1152]{1,0:T(8,128)S(1)}, u32[]{:S(2)}, u32[]{:S(2)}) %collective-permute-start.16) | collective-permute-done | bytes 626720 | tf_op jit(solution)/shard_map/ppermute | solution.py:27
  69.6 0.1 shard_map.70
  69.8 0.0 copy-start.1
  69.8 1.8 %collective-permute-start.17 = (f32[32,1152]{1,0:T(8,128)S(1)}, f32[32,1152]{1,0:T(8,128)S(1)}, u32[]{:S(2)}, u32[]{:S(2)}) collective-permute-start(f32[32,1152]{1,0:T(8,128)S(1)} %get-tuple-element.59), channel_id=1, source_target_pairs={{0,4},{32,48},{2,6},{34,50},{4,0},{36,52},{6,2},{38,54},{8,12},{40... | collective-permute-start | bytes 442376 | tf_op jit(solution)/shard_map/ppermute | solution.py:27
  71.6 1.5 %collective-permute-start.18 = (f32[32,1152]{1,0:T(8,128)S(1)}, f32[32,1152]{1,0:T(8,128)S(1)}, u32[]{:S(2)}, u32[]{:S(2)}) collective-permute-start(f32[32,1152]{1,0:T(8,128)S(1)} %get-tuple-element.60), channel_id=1, source_target_pairs={{0,6},{32,56},{2,0},{34,58},{4,2},{36,60},{6,4},{38,62},{8,14},{40... | collective-permute-start | bytes 442376 | tf_op jit(solution)/shard_map/ppermute | solution.py:27
  73.1 0.5 collective-permute-start.19
  73.6 0.6 broadcast_in_dim.5
  74.3 6.5 %all-to-all-start = ((f32[64,1,128]{2,1,0:T(1,128)}), f32[64,1,128]{2,1,0:T(1,128)S(1)}, u32[]{:S(2)}, u32[]{:S(2)}) async-start(f32[64,1,128]{2,1,0:T(1,128)} %broadcast_in_dim.5), calls=%async_computation | async-start | bytes 65536 | tf_op jit(solution)/shard_map/all_to_all | solution.py:257
  80.8 9.8 %all-to-all-done = f32[64,1,128]{2,1,0:T(1,128)S(1)} async-done(((f32[64,1,128]{2,1,0:T(1,128)}), f32[64,1,128]{2,1,0:T(1,128)S(1)}, u32[]{:S(2)}, u32[]{:S(2)}) %all-to-all-start) | async-done | bytes 32800 | tf_op jit(solution)/shard_map/all_to_all | solution.py:257
  90.6 0.7 slice_reduce_fusion
  92.0 4.2 %collective-permute-start.23 = (f32[32,1152]{1,0:T(8,128)S(1)}, f32[32,1152]{1,0:T(8,128)S(1)}, u32[]{:S(2)}, u32[]{:S(2)}) collective-permute-start(f32[32,1152]{1,0:T(8,128)S(1)} %slice.58), channel_id=1, source_target_pairs={{0,32},{32,0},{2,34},{34,2},{4,36},{36,4},{6,38},{38,6},{8,40},{40... | collective-permute-start | bytes 442376 | tf_op jit(solution)/shard_map/ppermute | solution.py:27
  96.2 0.2 multiply_reduce_fusion.2
  96.4 0.8 subtract_multiply_fusion.1
  97.2 0.0 collective-permute-done.23
  97.2 0.2 multiply_reduce_fusion
  97.4 0.8 subtract_multiply_fusion
  (34 shorter events, 0.3 us)
Async XLA Ops:
  0.6 12.5 %collective-permute-start = (f32[32,1152]{1,0:T(8,128)}, f32[32,1152]{1,0:T(8,128)S(1)}, u32[]{:S(2)}, u32[]{:S(2)}) collective-permute-start(f32[32,1152]{1,0:T(8,128)} %param.4), channel_id=1, source_target_pairs={{0,2},{32,40},{2,4},{34,42},{4,6},{36,44},{6,0},{38,46},{8,10},{40... | collective-permute-start | bytes 442376 | tf_op jit(solution)/shard_map/ppermute | solution.py:27
  2.2 10.9 %collective-permute-start.1 = (f32[32,1152]{1,0:T(8,128)}, f32[32,1152]{1,0:T(8,128)S(1)}, u32[]{:S(2)}, u32[]{:S(2)}) collective-permute-start(f32[32,1152]{1,0:T(8,128)} %param.4), channel_id=1, source_target_pairs={{0,6},{32,56},{2,0},{34,58},{4,2},{36,60},{6,4},{38,62},{8,14},{40... | collective-permute-start | bytes 442376 | tf_op jit(solution)/shard_map/ppermute | solution.py:27
  3.9 9.2 %collective-permute-start.2 = (f32[32,1152]{1,0:T(8,128)}, f32[32,1152]{1,0:T(8,128)S(1)}, u32[]{:S(2)}, u32[]{:S(2)}) collective-permute-start(f32[32,1152]{1,0:T(8,128)} %param.4), channel_id=1, source_target_pairs={{0,4},{32,48},{2,6},{34,50},{4,0},{36,52},{6,2},{38,54},{8,12},{40... | collective-permute-start | bytes 442376 | tf_op jit(solution)/shard_map/ppermute | solution.py:27
  5.8 2.1 %collective-permute-start.6 = (f32[32,1152]{1,0:T(8,128)}, f32[32,1152]{1,0:T(8,128)S(1)}, u32[]{:S(2)}, u32[]{:S(2)}) collective-permute-start(f32[32,1152]{1,0:T(8,128)} %refs_4_.1), channel_id=1, source_target_pairs={{0,32},{32,0},{2,34},{34,2},{4,36},{36,4},{6,38},{38,6},{8,40},{40... | collective-permute-start | bytes 442376 | tf_op jit(solution)/shard_map/ppermute | solution.py:27
  7.9 10.6 %collective-permute-start.7 = (f32[64,1152]{1,0:T(8,128)S(1)}, f32[64,1152]{1,0:T(8,128)S(1)}, u32[]{:S(2)}, u32[]{:S(2)}) collective-permute-start(f32[64,1152]{1,0:T(8,128)S(1)} %constant_dynamic-update-slice_fusion.4), channel_id=1, source_target_pairs={{0,1},{32,225},{2,3},{34,227},{4,5},{36,229},{6,7},{38,231},{8,9},... | collective-permute-start | bytes 884744 | tf_op jit(solution)/shard_map/ppermute | solution.py:27
  9.8 13.8 %collective-permute-start.8 = (f32[64,1152]{1,0:T(8,128)S(1)}, f32[64,1152]{1,0:T(8,128)S(1)}, u32[]{:S(2)}, u32[]{:S(2)}) collective-permute-start(f32[64,1152]{1,0:T(8,128)S(1)} %constant_dynamic-update-slice_fusion.4), channel_id=1, source_target_pairs={{0,64},{32,224},{2,66},{34,226},{4,68},{36,228},{6,70},{38,230},{8... | collective-permute-start | bytes 884744 | tf_op jit(solution)/shard_map/ppermute | solution.py:27
  13.2 18.6 %copy-start = (f32[32,1152]{1,0:T(8,128)S(1)}, f32[32,1152]{1,0:T(8,128)}, u32[]{:S(2)}) copy-start(f32[32,1152]{1,0:T(8,128)} %refs_4_.1) | copy-start | bytes 442372
  13.2 14.9 %collective-permute-start.3 = (f32[128,1152]{1,0:T(8,128)S(1)}, f32[128,1152]{1,0:T(8,128)S(1)}, u32[]{:S(2)}, u32[]{:S(2)}) collective-permute-start(f32[128,1152]{1,0:T(8,128)S(1)} %constant_dynamic-update-slice_fusion.refs_0_), channel_id=1, source_target_pairs={{0,8},{32,34},{2,10},{34,36},{4,12},{36,38},{6,14},{38,32},{8,16},... | collective-permute-start | bytes 1769480 | tf_op jit(solution)/shard_map/ppermute | solution.py:27
  14.9 13.2 %collective-permute-start.4 = (f32[128,1152]{1,0:T(8,128)S(1)}, f32[128,1152]{1,0:T(8,128)S(1)}, u32[]{:S(2)}, u32[]{:S(2)}) collective-permute-start(f32[128,1152]{1,0:T(8,128)S(1)} %constant_dynamic-update-slice_fusion.refs_0_), channel_id=1, source_target_pairs={{0,24},{32,38},{2,26},{34,32},{4,28},{36,34},{6,30},{38,36},{8,0},... | collective-permute-start | bytes 1769480 | tf_op jit(solution)/shard_map/ppermute | solution.py:27
  15.3 16.5 %collective-permute-start.5 = (f32[128,1152]{1,0:T(8,128)S(1)}, f32[128,1152]{1,0:T(8,128)S(1)}, u32[]{:S(2)}, u32[]{:S(2)}) collective-permute-start(f32[128,1152]{1,0:T(8,128)S(1)} %constant_dynamic-update-slice_fusion.refs_0_), channel_id=1, source_target_pairs={{0,16},{32,36},{2,18},{34,38},{4,20},{36,32},{6,22},{38,34},{8,24}... | collective-permute-start | bytes 1769480 | tf_op jit(solution)/shard_map/ppermute | solution.py:27
  23.7 8.1 %collective-permute-start.9 = (f32[128,1152]{1,0:T(8,128)S(1)}, f32[128,1152]{1,0:T(8,128)S(1)}, u32[]{:S(2)}, u32[]{:S(2)}) collective-permute-start(f32[128,1152]{1,0:T(8,128)S(1)} %pad_maximum_fusion), channel_id=1, source_target_pairs={{0,32},{32,0},{2,34},{34,2},{4,36},{36,4},{6,38},{38,6},{8,40},{40... | collective-permute-start | bytes 1769480 | tf_op jit(solution)/shard_map/ppermute | solution.py:27
  25.5 13.1 %collective-permute-start.11 = (f32[96,1152]{1,0:T(8,128)S(1)}, f32[96,1152]{1,0:T(8,128)S(1)}, u32[]{:S(2)}, u32[]{:S(2)}) collective-permute-start(f32[96,1152]{1,0:T(8,128)S(1)} %pad_maximum_fusion.1), channel_id=1, source_target_pairs={{0,64},{32,224},{2,66},{34,226},{4,68},{36,228},{6,70},{38,230},{8... | collective-permute-start | bytes 1327112 | tf_op jit(solution)/shard_map/ppermute | solution.py:27
  38.3 2.3 %collective-permute-start.10 = (f32[160,1152]{1,0:T(8,128)S(1)}, f32[160,1152]{1,0:T(8,128)S(1)}, u32[]{:S(2)}, u32[]{:S(2)}) collective-permute-start(f32[160,1152]{1,0:T(8,128)S(1)} %get-tuple-element.35), channel_id=1, source_target_pairs={{0,32},{32,0},{2,34},{34,2},{4,36},{36,4},{6,38},{38,6},{8,40},{40... | collective-permute-start | bytes 2211848 | tf_op jit(solution)/shard_map/ppermute | solution.py:27
  38.5 2.7 %collective-permute-start.12 = (f32[96,1152]{1,0:T(8,128)S(1)}, f32[96,1152]{1,0:T(8,128)S(1)}, u32[]{:S(2)}, u32[]{:S(2)}) collective-permute-start(f32[96,1152]{1,0:T(8,128)S(1)} %collective-permute-done.11.t0), channel_id=1, source_target_pairs={{0,32},{32,0},{2,34},{34,2},{4,36},{36,4},{6,38},{38,6},{8,40},{40... | collective-permute-start | bytes 1327112 | tf_op jit(solution)/shard_map/ppermute | solution.py:27
  45.4 1.9 %collective-permute-start.13 = (f32[96,1152]{1,0:T(8,128)S(1)}, f32[96,1152]{1,0:T(8,128)S(1)}, u32[]{:S(2)}, u32[]{:S(2)}) collective-permute-start(f32[96,1152]{1,0:T(8,128)S(1)} %get-tuple-element.51), channel_id=1, source_target_pairs={{0,32},{32,0},{2,34},{34,2},{4,36},{36,4},{6,38},{38,6},{8,40},{40... | collective-permute-start | bytes 1327112 | tf_op jit(solution)/shard_map/ppermute | solution.py:27
  47.3 14.9 %collective-permute-start.20 = (f32[96,1152]{1,0:T(8,128)S(1)}, f32[96,1152]{1,0:T(8,128)S(1)}, u32[]{:S(2)}, u32[]{:S(2)}) collective-permute-start(f32[96,1152]{1,0:T(8,128)S(1)} %add.52), channel_id=1, source_target_pairs={{0,192},{32,96},{2,194},{34,98},{4,196},{36,100},{6,198},{38,102},... | collective-permute-start | bytes 1327112 | tf_op jit(solution)/shard_map/ppermute | solution.py:27
  51.6 15.4 %collective-permute-start.14 = (f32[136,1152]{1,0:T(8,128)S(1)}, f32[136,1152]{1,0:T(8,128)S(1)}, u32[]{:S(2)}, u32[]{:S(2)}) collective-permute-start(f32[136,1152]{1,0:T(8,128)S(1)} %get-tuple-element.54), channel_id=1, source_target_pairs={{0,24},{32,38},{2,26},{34,32},{4,28},{36,34},{6,30},{38,36},{8,0},... | collective-permute-start | bytes 1880072 | tf_op jit(solution)/shard_map/ppermute | solution.py:27
  52.1 14.9 %collective-permute-start.15 = (f32[136,1152]{1,0:T(8,128)S(1)}, f32[136,1152]{1,0:T(8,128)S(1)}, u32[]{:S(2)}, u32[]{:S(2)}) collective-permute-start(f32[136,1152]{1,0:T(8,128)S(1)} %get-tuple-element.55), channel_id=1, source_target_pairs={{0,8},{32,34},{2,10},{34,36},{4,12},{36,38},{6,14},{38,32},{8,16},... | collective-permute-start | bytes 1880072 | tf_op jit(solution)/shard_map/ppermute | solution.py:27
  53.7 16.0 %collective-permute-start.16 = (f32[136,1152]{1,0:T(8,128)S(1)}, f32[136,1152]{1,0:T(8,128)S(1)}, u32[]{:S(2)}, u32[]{:S(2)}) collective-permute-start(f32[136,1152]{1,0:T(8,128)S(1)} %get-tuple-element.56), channel_id=1, source_target_pairs={{0,16},{32,36},{2,18},{34,38},{4,20},{36,32},{6,22},{38,34},{8,24}... | collective-permute-start | bytes 1880072 | tf_op jit(solution)/shard_map/ppermute | solution.py:27
  62.4 29.6 %collective-permute-start.22 = (f32[64,1152]{1,0:T(8,128)S(1)}, f32[64,1152]{1,0:T(8,128)S(1)}, u32[]{:S(2)}, u32[]{:S(2)}) collective-permute-start(f32[64,1152]{1,0:T(8,128)S(1)} %pad_maximum_fusion.2), channel_id=1, source_target_pairs={{0,192},{32,96},{2,194},{34,98},{4,196},{36,100},{6,198},{38,102},... | collective-permute-start | bytes 884744 | tf_op jit(solution)/shard_map/ppermute | solution.py:27
  67.0 24.9 %collective-permute-start.21 = (f32[64,1152]{1,0:T(8,128)S(1)}, f32[64,1152]{1,0:T(8,128)S(1)}, u32[]{:S(2)}, u32[]{:S(2)}) collective-permute-start(f32[64,1152]{1,0:T(8,128)S(1)} %get-tuple-element.70), channel_id=1, source_target_pairs={{0,193},{32,33},{2,195},{34,35},{4,197},{36,37},{6,199},{38,39},{8... | collective-permute-start | bytes 884744 | tf_op jit(solution)/shard_map/ppermute | solution.py:27
  69.8 26.4 %copy-start.1 = (f32[32,1152]{1,0:T(8,128)S(1)}, f32[32,1152]{1,0:T(8,128)}, u32[]{:S(2)}) copy-start(f32[32,1152]{1,0:T(8,128)} %param.4) | copy-start | bytes 442372
  69.8 26.4 %collective-permute-start.17 = (f32[32,1152]{1,0:T(8,128)S(1)}, f32[32,1152]{1,0:T(8,128)S(1)}, u32[]{:S(2)}, u32[]{:S(2)}) collective-permute-start(f32[32,1152]{1,0:T(8,128)S(1)} %get-tuple-element.59), channel_id=1, source_target_pairs={{0,4},{32,48},{2,6},{34,50},{4,0},{36,52},{6,2},{38,54},{8,12},{40... | collective-permute-start | bytes 442376 | tf_op jit(solution)/shard_map/ppermute | solution.py:27
  71.6 24.6 %collective-permute-start.18 = (f32[32,1152]{1,0:T(8,128)S(1)}, f32[32,1152]{1,0:T(8,128)S(1)}, u32[]{:S(2)}, u32[]{:S(2)}) collective-permute-start(f32[32,1152]{1,0:T(8,128)S(1)} %get-tuple-element.60), channel_id=1, source_target_pairs={{0,6},{32,56},{2,0},{34,58},{4,2},{36,60},{6,4},{38,62},{8,14},{40... | collective-permute-start | bytes 442376 | tf_op jit(solution)/shard_map/ppermute | solution.py:27
  73.1 23.1 %collective-permute-start.19 = (f32[32,1152]{1,0:T(8,128)S(1)}, f32[32,1152]{1,0:T(8,128)S(1)}, u32[]{:S(2)}, u32[]{:S(2)}) collective-permute-start(f32[32,1152]{1,0:T(8,128)S(1)} %get-tuple-element.61), channel_id=1, source_target_pairs={{0,2},{32,40},{2,4},{34,42},{4,6},{36,44},{6,0},{38,46},{8,10},{40... | collective-permute-start | bytes 442376 | tf_op jit(solution)/shard_map/ppermute | solution.py:27
  74.3 16.4 %all-to-all-start = ((f32[64,1,128]{2,1,0:T(1,128)}), f32[64,1,128]{2,1,0:T(1,128)S(1)}, u32[]{:S(2)}, u32[]{:S(2)}) async-start(f32[64,1,128]{2,1,0:T(1,128)} %broadcast_in_dim.5), calls=%async_computation | async-start | bytes 65536 | tf_op jit(solution)/shard_map/all_to_all | solution.py:257
  92.0 5.2 %collective-permute-start.23 = (f32[32,1152]{1,0:T(8,128)S(1)}, f32[32,1152]{1,0:T(8,128)S(1)}, u32[]{:S(2)}, u32[]{:S(2)}) collective-permute-start(f32[32,1152]{1,0:T(8,128)S(1)} %slice.58), channel_id=1, source_target_pairs={{0,32},{32,0},{2,34},{34,2},{4,36},{36,4},{6,38},{38,6},{8,40},{40... | collective-permute-start | bytes 442376 | tf_op jit(solution)/shard_map/ppermute | solution.py:27

commit v3 on v2

v3 whole, which is shorter than its diff:
```python
import functools
import itertools
import jax
import jax.numpy as jnp
from jax import lax
from jax.experimental import pallas as pl
from jax.experimental.pallas import tpu as pltpu
from jax.sharding import PartitionSpec as P

AXES = ("img", "txt")
NX, NY, NZ = 4, 4, 8


def place(z, y, x, core):
    return ((z // 2) * 2 + core) * 32 + (y * NX + x) * 2 + z % 2


def pairs(target):
    out = []
    for z, y, x, core in itertools.product(range(NZ), range(NY), range(NX), range(2)):
        tz, ty, tx, tc = target(z, y, x, core)
        out.append((place(z, y, x, core), place(tz % NZ, ty % NY, tx % NX, tc)))
    return out


def send(value, target):
    return lax.ppermute(value, AXES, pairs(target))


def swap(value):
    return send(value, lambda z, y, x, core: (z, y, x, 1 - core))


def first(value, d):
    return send(value, lambda z, y, x, core: (z, y, x + d, core) if core == 0 else (z, y + d, x, core))


def second(value, d):
    return send(value, lambda z, y, x, core: (z, y + d, x, core) if core == 0 else (z, y, x + d, core))


def along_z(value, d):
    return send(value, lambda z, y, x, core: (z + d if core == 0 else z - d, y, x, core))


STEPS = (1, 3, 2)

def add_from(value, target):
    return value + send(value, target)


def after(values, *others):
    return lax.optimization_barrier((values, others))[0]


NT = (((1,), (1,)), ((), ()))
TN = (((0,), (0,)), ((), ()))
NN = (((1,), (0,)), ((), ()))
VMEM = pl.BlockSpec(memory_space=pltpu.VMEM)
SMEM = pl.BlockSpec(memory_space=pltpu.SMEM)
GRANT = pltpu.CompilerParams(vmem_limit_bytes=40 << 20)


def f32(*shape):
    return jax.ShapeDtypeStruct(shape, jnp.float32)


def b16(*shape):
    return jax.ShapeDtypeStruct(shape, jnp.bfloat16)


def halves(value):
    high = value.astype(jnp.bfloat16)
    return high, (value - high.astype(jnp.float32)).astype(jnp.bfloat16)


def dot3(a, b, dims):
    dot = functools.partial(lax.dot_general, dimension_numbers=dims, preferred_element_type=jnp.float32)
    return dot(a[0], b[0]) + (dot(a[0], b[1]) + dot(a[1], b[0]))


def unit_halves(refs, high, low):
    at = 0
    for ref in refs:
        rows = ref.shape[0]
        raw = ref[...]
        unit = raw * lax.rsqrt(jnp.sum(raw * raw, axis=1, keepdims=True) + 1e-06)
        high[at : at + rows, :], low[at : at + rows, :] = halves(unit)
        at += rows


def pair_terms(logits, own):
    if own:
        row = lax.broadcasted_iota(jnp.int32, logits.shape, 0)
        col = lax.broadcasted_iota(jnp.int32, logits.shape, 1)
        same = (row == col) & (row < own)
        logits = jnp.where(same, -logits, logits)
    small = jnp.exp(-jnp.abs(logits))
    loss = jnp.sum(jnp.maximum(logits, 0.0) + jnp.log1p(small))
    part = 1.0 / (1.0 + small)
    coef = jnp.where(logits >= 0, part, small * part)
    if own:
        coef = jnp.where(same, -coef, coef)
    return loss, coef


def two_parts(total):
    coarse = jnp.round(total * (1.0 / 128.0)) * 128.0
    fine = jnp.round((total - coarse) * 512.0) * (1.0 / 512.0)
    return jnp.where(lax.broadcasted_iota(jnp.int32, (8, 128), 1) < 64, coarse, fine)


def group_kernel(own, count, scale, bias, *refs):
    raws = refs[:count]
    if own:
        texts = refs[count : count + 4]
        image_part, ihi, ilo, text_part, loss, thi, tlo = refs[count + 4 :]
        unit_halves(texts, thi, tlo)
    else:
        thi, tlo, text_in, loss_in, image_part, ihi, ilo, text_part, loss = refs[count:]
    unit_halves(raws, ihi, ilo)
    images = ihi[...], ilo[...]
    texts = thi[...], tlo[...]
    logits = scale[0] * dot3(images, texts, NT) + bias[0]
    total, coef = pair_terms(logits, own)
    coef = halves(coef * scale[0])
    image_part[...] = dot3(coef, texts, NN)
    part = dot3(coef, images, TN)
    if own:
        text_part[...] = part
        loss[...] = jnp.full(loss.shape, total, jnp.float32)
    else:
        text_part[...] = text_in[...] + part
        loss[...] = loss_in[...] + total


def mid_kernel(scale, bias, h0, l0, h1, l1, loss_in, raw, ihi, ilo, part, chi, clo, thi, tlo, loss):
    rows = h0.shape[0]
    ihi[:rows, :], ilo[:rows, :] = h0[...], l0[...]
    ihi[rows:, :], ilo[rows:, :] = h1[...], l1[...]
    unit_halves((raw,), thi, tlo)
    images = ihi[...], ilo[...]
    logits = scale[0] * dot3(images, (thi[...], tlo[...]), NT) + bias[0]
    total, coef = pair_terms(logits, 0)
    loss[...] = loss_in[...] + total
    coef = halves(coef * scale[0])
    chi[...], clo[...] = coef
    part[...] = dot3(coef, images, TN)


def far_kernel(scale, bias, ihi, ilo, loss_in, raw, chi, clo, thi, tlo, loss):
    unit_halves((raw,), thi, tlo)
    logits = scale[0] * dot3((ihi[...], ilo[...]), (thi[...], tlo[...]), NT) + bias[0]
    total, coef = pair_terms(logits, 0)
    loss[...] = two_parts(loss_in[...] + total)
    chi[...], clo[...] = halves(coef * scale[0])


def last_kernel(ihi, ilo, mhi, mlo, uhi, ulo, chi, clo, thi, tlo, in0, in1, other, pay, *outs):
    coef = chi[...], clo[...]
    count = thi.shape[0]
    pay[:count, :] = dot3(coef, (ihi[...], ilo[...]), TN)
    pay[count:, :] = other[...]
    part = dot3((mhi[...], mlo[...]), (uhi[...], ulo[...]), NN) + dot3(coef, (thi[...], tlo[...]), NN)
    rows = in0.shape[0]
    outs[0][...] = in0[...] + part[:rows]
    for k, out in enumerate(outs[1:]):
        out[...] = in1[rows * k : rows * (k + 1), :] + part[rows * (k + 1) : rows * (k + 2)]


def sum_kernel(in0, in1, in2, in3, out0, out1, out2, out3):
    total = (in0[...] + in3[...]) + (in1[...] + in2[...])
    rows = (total.shape[0] - 8) // 4
    for k, out in enumerate((out0, out1, out2, out3)):
        out[:rows, :] = total[rows * k : rows * (k + 1)]
        out[rows:, :] = total[4 * rows :]


def cost(rows, cols, width, dots):
    return pl.CostEstimate(flops=6 * dots * rows * cols * width, bytes_accessed=4 * rows * width, transcendentals=0)


def group_call(scale, bias, raws, texts, start=None):
    width = raws[0].shape[1]
    rows = sum(raw.shape[0] for raw in raws)
    cols = sum(text.shape[0] for text in texts) if start is None else texts[0].shape[0]
    operands = [scale, bias, *raws, *texts, *(start or ())]
    shapes = [f32(rows, width), b16(rows, width), b16(rows, width), f32(cols, width), f32(8, 128)]
    if start is None:
        shapes += [b16(cols, width)] * 2
    return pl.pallas_call(
        functools.partial(group_kernel, texts[0].shape[0] if start is None else 0, len(raws)),
        out_shape=shapes,
        in_specs=[SMEM, SMEM] + [VMEM] * (len(operands) - 2),
        out_specs=[VMEM] * len(shapes),
        cost_estimate=cost(rows, cols, width, 3),
        compiler_params=GRANT,
    )(*operands)


def mid_call(scale, bias, images, loss, raw):
    count, width = raw.shape
    rows = images[0].shape[0] + images[2].shape[0]
    return pl.pallas_call(
        mid_kernel,
        out_shape=[b16(rows, width)] * 2
        + [f32(count, width)]
        + [b16(rows, count)] * 2
        + [b16(count, width)] * 2
        + [f32(8, 128)],
        in_specs=[SMEM, SMEM] + [VMEM] * 6,
        out_specs=[VMEM] * 8,
        cost_estimate=cost(rows, count, width, 2),
        compiler_params=GRANT,
    )(scale, bias, *images, loss, raw)


def far_call(scale, bias, ihi, ilo, loss, raw):
    count, width = raw.shape
    rows = ihi.shape[0]
    return pl.pallas_call(
        far_kernel,
        out_shape=[b16(rows, count)] * 2 + [b16(count, width)] * 2 + [f32(8, 128)],
        in_specs=[SMEM, SMEM] + [VMEM] * 4,
        out_specs=[VMEM] * 5,
        cost_estimate=cost(rows, count, width, 1),
        compiler_params=GRANT,
    )(scale, bias, ihi, ilo, loss, raw)


def last_call(images, mid, far, starts, other):
    rows, width = images[0].shape
    count = far[0].shape[1]
    return pl.pallas_call(
        last_kernel,
        out_shape=[f32(count + other.shape[0], width)] + [f32(rows // 4, width)] * 4,
        in_specs=[VMEM] * 13,
        out_specs=[VMEM] * 5,
        cost_estimate=cost(rows, count, width, 5),
        compiler_params=GRANT,
    )(*images, *mid, *far, *starts, other)


def sum_call(parts):
    rows, width = parts[0].shape
    return pl.pallas_call(
        sum_kernel,
        out_shape=[f32((rows - 8) // 4 + 8, width)] * 4,
        in_specs=[VMEM] * 4,
        out_specs=[VMEM] * 4,
        compiler_params=GRANT,
    )(*parts)


def normalize(embed):
    inverse = lax.rsqrt(jnp.sum(embed * embed, axis=1, keepdims=True) + 1e-06)
    return (embed * inverse, inverse)


def on_device(image_emb, text_emb, logit_scale, logit_bias):
    rows = image_emb.shape[0]
    other = swap(text_emb)
    four = [first(image_emb, d) for d in STEPS]
    pair = jnp.concatenate([text_emb, other])
    one = along_z(pair, 1)
    two = along_z(pair, 2)
    four = jnp.concatenate([image_emb] + four)
    images = [four] + [second(four, d) for d in STEPS]
    far = along_z(jnp.concatenate([one, two[:rows]]), 2)
    part0, hi0, lo0, *start, thi, tlo = group_call(logit_scale, logit_bias, images[:1], [text_emb, other, one, two])
    part1, hi1, lo1, text_part, loss = group_call(logit_scale, logit_bias, images[1:], (thi, tlo), start)
    rest = swap(after(jnp.concatenate([one, two, far]), loss))
    ihi, ilo, far_part, *mid, loss = mid_call(logit_scale, logit_bias, (hi0, lo0, hi1, lo1), loss, far)
    *last, loss = far_call(logit_scale, logit_bias, ihi, ilo, loss, rest)
    pay, *four = last_call((ihi, ilo), mid, last, (part0, part1), text_part[rows : 2 * rows])
    loss = add_from(loss, lambda z, y, x, core: (z ^ 1, y, x, core))
    note = jnp.concatenate([jnp.broadcast_to(loss[:, at : at + 1], (8, text_emb.shape[1] // 2)) for at in (0, 127)], 1)
    got = swap(jnp.concatenate([pay, note]))
    note = note + got[8 * rows :]
    back = along_z(far_part + got[4 * rows : 7 * rows], -2)
    one_part = text_part[2 * rows : 4 * rows] + got[: 2 * rows]
    two_part = text_part[4 * rows :] + got[2 * rows : 4 * rows]
    own_part = text_part[:rows] + got[7 * rows : 8 * rows]
    four = [jnp.concatenate([block, note]) for block in four]
    got = [second(four[i + 1], -d) for i, d in enumerate(STEPS)]
    one_part = one_part + back[: 2 * rows]
    two_part = jnp.concatenate([two_part[:rows] + back[2 * rows :], two_part[rows:]])
    back = along_z(one_part, -1) + along_z(two_part, -2)
    four = sum_call([four[0]] + got)
    got = [first(four[i + 1], -d) for i, d in enumerate(STEPS)]
    total = (four[0] + got[2]) + (got[0] + got[1])
    text_unit_grad = own_part + back[:rows] + swap(back[rows:])
    image_unit_grad = total[:rows]
    loss = jnp.concatenate([total[rows:, :64], total[rows:, -64:]], 1)
    beside = along_z(loss, -2)
    loss = loss + send(loss, lambda z, y, x, core: (z + 4, y, x, core))
    loss = loss + beside + swap(beside)
    loss = ((loss[0, 0] + loss[0, 127]) / (rows * 2 * NX * NY * NZ)).reshape(1)

    image_unit, image_inv = normalize(image_emb)
    text_unit, text_inv = normalize(text_emb)
    image_grad = (
        image_unit_grad - image_unit * jnp.sum(image_unit * image_unit_grad, axis=1, keepdims=True)
    ) * image_inv
    text_grad = (
        text_unit_grad - text_unit * jnp.sum(text_unit * text_unit_grad, axis=1, keepdims=True)
    ) * text_inv
    return (loss, image_grad, text_grad)


def solution(mesh):
    return jax.shard_map(
        on_device,
        mesh=mesh,
        in_specs=(P(("img", "txt"), None), P(("img", "txt"), None), P(), P()),
        out_specs=(P(), P(("img", "txt"), None), P(("img", "txt"), None)),
        check_vma=False,
    )
```

time: 101 us -> 98.6 us (0.976); the launches traced: 99.3 us -> 98.5 us
  starting transfers between devices: 49 us -> 36.7 us
  waiting for transfers between devices: 28.7 us -> 36.7 us
  Pallas kernels: 12 us -> 14.5 us
    ppermute x24 -> x26, waiting for transfers between devices: 18.9 us -> 36.7 us  [send(): return lax.ppermute(value, AXES, pairs(target))]
    all_to_all x1 -> x0, waiting for transfers between devices: 9.82 us -> none  [on_device(): lax.all_to_all(notes, AXES, 0, 0, axis_index_groups=SHEETS, tiled=True)]
    all_to_all x1 -> x0, starting transfers between devices: 6.53 us -> none  [on_device(): lax.all_to_all(notes, AXES, 0, 0, axis_index_groups=SHEETS, tiled=True)]
    ppermute x24 -> x26, starting transfers between devices: 42.5 us -> 36.7 us  [send(): return lax.ppermute(value, AXES, pairs(target))]
    pallas_call x4 -> x6, Pallas kernels: 12 us -> 14.5 us  [the longest x2 6.67 us: group_call(): pl.pallas_call(functools.partial(group_kernel, texts[0].shape[0] if start...]
  transfers between devices with their start and end apart: 25 -> 26, of which waited for: 9 -> 16; matrix products, arithmetic and copies ran while one was open for 5% -> 4% of each run, Pallas kernels for 8% -> 13%
where the time goes in v3:
time: 98.6 us; the launch traced here: 98.5 us
  starting transfers between devices  36.7 us (37%)
  waiting for transfers between devices  36.7 us (37%)
  Pallas kernels  14.5 us (15%)
  other arithmetic  4.92 us (5%)
  between operations  4.6 us (5%)
  local copies, waits for them, and re-layouts  1.07 us (1%)
    ppermute x26, waiting for transfers between devices, send(): return lax.ppermute(value, AXES, pairs(target))  36.7 us
    ppermute x26, starting transfers between devices, send(): return lax.ppermute(value, AXES, pairs(target))  36.7 us
    pallas_call x2, Pallas kernels, group_call(): pl.pallas_call(functools.partial(group_kernel, texts[0].shape[0] if start...  6.67 us
    pallas_call x1, Pallas kernels, last_call(): pl.pallas_call(last_kernel, out_shape=[f32(count + other.shape[0], width)...  3.11 us
    pallas_call x1, Pallas kernels, mid_call(): pl.pallas_call(mid_kernel, out_shape=[b16(rows, width)] * 2 + [f32(count,...  2.77 us
    reduce_sum x2, other arithmetic, normalize(): inverse = lax.rsqrt(jnp.sum(embed * embed, axis=1, keepdims=True) + 1e-06)  2.07 us
  transfers between devices with their start and end apart: 26, of which 16 were waited for; matrix products, arithmetic and copies ran while one was open for 4% of the time, Pallas kernels for 13%

profile of v3, /device:TPU:8, one launch (start us, length us, event | category | flops | bytes accessed | tf_op | source)
XLA Modules:
  0.0 98.5 jit_solution(12194241097449902069)
XLA Ops:
  0.6 3.1 %collective-permute-start.2 = (f32[32,1152]{1,0:T(8,128)}, f32[32,1152]{1,0:T(8,128)S(1)}, u32[]{:S(2)}, u32[]{:S(2)}) collective-permute-start(f32[32,1152]{1,0:T(8,128)} %param.4), channel_id=1, source_target_pairs={{0,4},{32,48},{2,6},{34,50},{4,0},{36,52},{6,2},{38,54},{8,12},{40... | collective-permute-start | bytes 442376 | tf_op jit(solution)/shard_map/ppermute | solution.py:27
  3.7 1.1 %collective-permute-start.1 = (f32[32,1152]{1,0:T(8,128)}, f32[32,1152]{1,0:T(8,128)S(1)}, u32[]{:S(2)}, u32[]{:S(2)}) collective-permute-start(f32[32,1152]{1,0:T(8,128)} %param.4), channel_id=1, source_target_pairs={{0,6},{32,56},{2,0},{34,58},{4,2},{36,60},{6,4},{38,62},{8,14},{40... | collective-permute-start | bytes 442376 | tf_op jit(solution)/shard_map/ppermute | solution.py:27
  4.9 0.9 collective-permute-start
  5.8 1.0 %multiply_reduce_fusion.1 = (f32[32]{0:T(128)S(1)}, f32[64,1152]{1,0:T(8,128)S(1)}) fusion(f32[32,1152]{1,0:T(8,128)} %refs_1_.1), kind=kLoop, calls=%fused_computation.19 | loop fusion | flops 73695 | bytes 295424 | tf_op jit(solution)/shard_map/reduce_sum | solution.py:256
  6.8 1.0 %multiply_reduce_fusion.3 = (f32[32]{0:T(128)S(1)}, f32[128,1152]{1,0:T(8,128)S(1)}) fusion(f32[32,1152]{1,0:T(8,128)} %param.4), kind=kLoop, calls=%fused_computation.22 | loop fusion | flops 73695 | bytes 295424 | tf_op jit(solution)/shard_map/reduce_sum | solution.py:256
  7.9 3.3 %collective-permute-start.5 = (f32[64,1152]{1,0:T(8,128)S(1)}, f32[64,1152]{1,0:T(8,128)S(1)}, u32[]{:S(2)}, u32[]{:S(2)}) collective-permute-start(f32[64,1152]{1,0:T(8,128)S(1)} %constant_dynamic-update-slice_fusion.4), channel_id=1, source_target_pairs={{0,64},{32,224},{2,66},{34,226},{4,68},{36,228},{6,70},{38,230},{8... | collective-permute-start | bytes 884744 | tf_op jit(solution)/shard_map/ppermute | solution.py:27
  11.2 1.9 %collective-permute-start.4 = (f32[64,1152]{1,0:T(8,128)S(1)}, f32[64,1152]{1,0:T(8,128)S(1)}, u32[]{:S(2)}, u32[]{:S(2)}) collective-permute-start(f32[64,1152]{1,0:T(8,128)S(1)} %constant_dynamic-update-slice_fusion.4), channel_id=1, source_target_pairs={{0,1},{32,225},{2,3},{34,227},{4,5},{36,229},{6,7},{38,231},{8,9},... | collective-permute-start | bytes 884744 | tf_op jit(solution)/shard_map/ppermute | solution.py:27
  13.2 2.4 %collective-permute-start.8 = (f32[128,1152]{1,0:T(8,128)S(1)}, f32[128,1152]{1,0:T(8,128)S(1)}, u32[]{:S(2)}, u32[]{:S(2)}) collective-permute-start(f32[128,1152]{1,0:T(8,128)S(1)} %constant_dynamic-update-slice_fusion.refs_0_), channel_id=1, source_target_pairs={{0,16},{32,36},{2,18},{34,38},{4,20},{36,32},{6,22},{38,34},{8,24}... | collective-permute-start | bytes 1769480 | tf_op jit(solution)/shard_map/ppermute | solution.py:27
  15.6 1.3 %collective-permute-start.7 = (f32[128,1152]{1,0:T(8,128)S(1)}, f32[128,1152]{1,0:T(8,128)S(1)}, u32[]{:S(2)}, u32[]{:S(2)}) collective-permute-start(f32[128,1152]{1,0:T(8,128)S(1)} %constant_dynamic-update-slice_fusion.refs_0_), channel_id=1, source_target_pairs={{0,24},{32,38},{2,26},{34,32},{4,28},{36,34},{6,30},{38,36},{8,0},... | collective-permute-start | bytes 1769480 | tf_op jit(solution)/shard_map/ppermute | solution.py:27
  17.0 0.7 collective-permute-start.6
  17.6 1.9 %collective-permute-done.5.refs_4_ = f32[64,1152]{1,0:T(8,128)S(1)} collective-permute-done((f32[64,1152]{1,0:T(8,128)S(1)}, f32[64,1152]{1,0:T(8,128)S(1)}, u32[]{:S(2)}, u32[]{:S(2)}) %collective-permute-start.5) | collective-permute-done | bytes 294944 | tf_op jit(solution)/shard_map/ppermute | solution.py:27
  19.6 5.3 %collective-permute-done.4.refs_3_ = f32[64,1152]{1,0:T(8,128)S(1)} collective-permute-done((f32[64,1152]{1,0:T(8,128)S(1)}, f32[64,1152]{1,0:T(8,128)S(1)}, u32[]{:S(2)}, u32[]{:S(2)}) %collective-permute-start.4) | collective-permute-done | bytes 294944 | tf_op jit(solution)/shard_map/ppermute | solution.py:27
  24.9 1.5 %collective-permute-start.9 = (f32[96,1152]{1,0:T(8,128)S(1)}, f32[96,1152]{1,0:T(8,128)S(1)}, u32[]{:S(2)}, u32[]{:S(2)}) collective-permute-start(f32[96,1152]{1,0:T(8,128)S(1)} %pad_maximum_fusion.6), channel_id=1, source_target_pairs={{0,64},{32,224},{2,66},{34,226},{4,68},{36,228},{6,70},{38,230},{8... | collective-permute-start | bytes 1327112 | tf_op jit(solution)/shard_map/ppermute | solution.py:27
  27.6 2.3 %shard_map.67 = (f32[128,1152]{1,0:T(8,128)S(1)}, bf16[128,1152]{1,0:T(8,128)(2,1)S(1)}, bf16[128,1152]{1,0:T(8,128)(2,1)S(1)}, f32[192,1152]{1,0:T(8,128)S(1)},...) custom-call(f32[1]{0:T(128)S(6)} %copy.11.scale, f32[1]{0:T(128)S(6)} %copy.12.bias, ...), custom_call_target="tpu_custom_call" | custom-call | flops 509607936 | bytes 589824 | tf_op jit(solution)/shard_map/pallas_call | solution.py:191
  29.9 1.1 %collective-permute-done.7.refs_1_ = f32[128,1152]{1,0:T(8,128)S(1)} collective-permute-done((f32[128,1152]{1,0:T(8,128)S(1)}, f32[128,1152]{1,0:T(8,128)S(1)}, u32[]{:S(2)}, u32[]{:S(2)}) %collective-permute-start.7) | collective-permute-done | bytes 589856 | tf_op jit(solution)/shard_map/ppermute | solution.py:27
  31.2 4.4 %shard_map.68 = (f32[384,1152]{1,0:T(8,128)S(1)}, bf16[384,1152]{1,0:T(8,128)(2,1)S(1)}, bf16[384,1152]{1,0:T(8,128)(2,1)S(1)}, f32[192,1152]{1,0:T(8,128)S(1)}, f32[8,128]{1,0:T(8,128)S(1)}) custom-call(f32[1]{0:T(128)S(6)} %copy.11.scale, f32[1]{0:T(128)S(6)} %copy.12.bias, f32[128,1152]{1,0:T(8,128)S(1)} %collective-permute-done.6.refs_0_, ...), custom_call_target="tpu_custom_call" | custom-call | flops 1528823808 | bytes 1769472 | tf_op jit(solution)/shard_map/pallas_call | solution.py:191
  35.6 3.8 %collective-permute-done.9.raw = f32[96,1152]{1,0:T(8,128)S(1)} collective-permute-done((f32[96,1152]{1,0:T(8,128)S(1)}, f32[96,1152]{1,0:T(8,128)S(1)}, u32[]{:S(2)}, u32[]{:S(2)}) %collective-permute-start.9) | collective-permute-done | bytes 442400 | tf_op jit(solution)/shard_map/ppermute | solution.py:27
  39.5 0.3 collective-permute-start.10
  39.8 2.8 %shard_map.69 = (bf16[512,1152]{1,0:T(8,128)(2,1)S(1)}, bf16[512,1152]{1,0:T(8,128)(2,1)S(1)}, f32[96,1152]{1,0:T(8,128)S(1)}, bf16[512,96]{1,0:T(8,128)(2,1)S(1...) custom-call(f32[1]{0:T(128)S(6)} %copy.11.scale, ...), custom_call_target="tpu_custom_call" | custom-call | flops 679477248 | bytes 2359296 | tf_op jit(solution)/shard_map/pallas_call | solution.py:204
  42.5 1.8 %shard_map.70 = (bf16[512,224]{1,0:T(8,128)(2,1)S(1)}, bf16[512,224]{1,0:T(8,128)(2,1)S(1)}, bf16[224,1152]{1,0:T(8,128)(2,1)S(1)}, bf16[224,1152]{1,0:T(8,128)(2,1)S(1)}, f32[8,128]{1,0:T(8,128)S(1)}) custom-call(f32[1]{0:T(128)S(6)} %copy.11.scale, f32[1]{0:T(128)S(6)} %copy.12.bias, bf16[512,1152]{1,0:T(8,128)(2,1)S(1)} %get-tuple-element.47.ihi, ...), custom_call_target="tpu_custom_call" | custom-call | flops 792723456 | bytes 2359296 | tf_op jit(solution)/shard_map/pallas_call | solution.py:221
  44.5 3.1 %shard_map.71 = (f32[256,1152]{1,0:T(8,128)S(1)}, f32[128,1152]{1,0:T(8,128)S(1)}, f32[128,1152]{1,0:T(8,128)S(1)}, f32[128,1152]{1,0:T(8,128)S(1)}, f32[128,1152]{1,0:T(8,128)S(1)}) custom-call(bf16[512,1152]{1,0:T(8,128)(2,1)S(1)} %get-tuple-element.47.ihi, bf16[512,1152]{1,0:T(8,128)(2,1)S(1)} %get-tuple-element.48.ilo, ...), custom_call_target="tpu_custom_call" | custom-call | flops 3963617280 | bytes 2359296 | tf_op jit(solution)/shard_map/pallas_call | solution.py:234
  47.6 0.5 collective-permute-done.11
  48.1 0.2 slice_reduce_fusion.1
  48.7 2.9 %collective-permute-done.12 = f32[264,1152]{1,0:T(8,128)S(1)} collective-permute-done((f32[264,1152]{1,0:T(8,128)S(1)}, f32[264,1152]{1,0:T(8,128)S(1)}, u32[]{:S(2)}, u32[]{:S(2)}) %collective-permute-start.12) | collective-permute-done | bytes 1216544 | tf_op jit(solution)/shard_map/ppermute | solution.py:27
  51.6 2.5 %collective-permute-start.22 = (f32[96,1152]{1,0:T(8,128)S(1)}, f32[96,1152]{1,0:T(8,128)S(1)}, u32[]{:S(2)}, u32[]{:S(2)}) collective-permute-start(f32[96,1152]{1,0:T(8,128)S(1)} %slice_add_fusion), channel_id=1, source_target_pairs={{0,192},{32,96},{2,194},{34,98},{4,196},{36,100},{6,198},{38,102},... | collective-permute-start | bytes 1327112 | tf_op jit(solution)/shard_map/ppermute | solution.py:27
  54.2 0.2 pad_maximum_fusion
  54.4 2.4 %collective-permute-start.15 = (f32[136,1152]{1,0:T(8,128)S(1)}, f32[136,1152]{1,0:T(8,128)S(1)}, u32[]{:S(2)}, u32[]{:S(2)}) collective-permute-start(f32[136,1152]{1,0:T(8,128)S(1)} %get-tuple-element.87), channel_id=1, source_target_pairs={{0,16},{32,36},{2,18},{34,38},{4,20},{36,32},{6,22},{38,34},{8,24}... | collective-permute-start | bytes 1880072 | tf_op jit(solution)/shard_map/ppermute | solution.py:27
  56.8 1.3 %collective-permute-start.13 = (f32[136,1152]{1,0:T(8,128)S(1)}, f32[136,1152]{1,0:T(8,128)S(1)}, u32[]{:S(2)}, u32[]{:S(2)}) collective-permute-start(f32[136,1152]{1,0:T(8,128)S(1)} %get-tuple-element.88), channel_id=1, source_target_pairs={{0,24},{32,38},{2,26},{34,32},{4,28},{36,34},{6,30},{38,36},{8,0},... | collective-permute-start | bytes 1880072 | tf_op jit(solution)/shard_map/ppermute | solution.py:27
  58.1 0.7 collective-permute-start.14
  58.8 6.9 %collective-permute-done.22 = f32[96,1152]{1,0:T(8,128)S(1)} collective-permute-done((f32[96,1152]{1,0:T(8,128)S(1)}, f32[96,1152]{1,0:T(8,128)S(1)}, u32[]{:S(2)}, u32[]{:S(2)}) %collective-permute-start.22) | collective-permute-done | bytes 442400 | tf_op jit(solution)/shard_map/ppermute | solution.py:27
  65.8 3.7 %collective-permute-start.24 = (f32[64,1152]{1,0:T(8,128)S(1)}, f32[64,1152]{1,0:T(8,128)S(1)}, u32[]{:S(2)}, u32[]{:S(2)}) collective-permute-start(f32[64,1152]{1,0:T(8,128)S(1)} %pad_maximum_fusion.7), channel_id=1, source_target_pairs={{0,192},{32,96},{2,194},{34,98},{4,196},{36,100},{6,198},{38,102},... | collective-permute-start | bytes 884744 | tf_op jit(solution)/shard_map/ppermute | solution.py:27
  69.6 1.5 %collective-permute-start.23 = (f32[64,1152]{1,0:T(8,128)S(1)}, f32[64,1152]{1,0:T(8,128)S(1)}, u32[]{:S(2)}, u32[]{:S(2)}) collective-permute-start(f32[64,1152]{1,0:T(8,128)S(1)} %get-tuple-element.78), channel_id=1, source_target_pairs={{0,193},{32,33},{2,195},{34,35},{4,197},{36,37},{6,199},{38,39},{8... | collective-permute-start | bytes 884744 | tf_op jit(solution)/shard_map/ppermute | solution.py:27
  71.1 1.9 %collective-permute-done.13.in1 = f32[136,1152]{1,0:T(8,128)S(1)} collective-permute-done((f32[136,1152]{1,0:T(8,128)S(1)}, f32[136,1152]{1,0:T(8,128)S(1)}, u32[]{:S(2)}, u32[]{:S(2)}) %collective-permute-start.13) | collective-permute-done | bytes 626720 | tf_op jit(solution)/shard_map/ppermute | solution.py:27
  73.3 1.4 %collective-permute-start.16 = (f32[40,1152]{1,0:T(8,128)S(1)}, f32[40,1152]{1,0:T(8,128)S(1)}, u32[]{:S(2)}, u32[]{:S(2)}) collective-permute-start(f32[40,1152]{1,0:T(8,128)S(1)} %get-tuple-element.69), channel_id=1, source_target_pairs={{0,4},{32,48},{2,6},{34,50},{4,0},{36,52},{6,2},{38,54},{8,12},{40... | collective-permute-start | bytes 552968 | tf_op jit(solution)/shard_map/ppermute | solution.py:27
  74.7 2.1 %collective-permute-start.17 = (f32[40,1152]{1,0:T(8,128)S(1)}, f32[40,1152]{1,0:T(8,128)S(1)}, u32[]{:S(2)}, u32[]{:S(2)}) collective-permute-start(f32[40,1152]{1,0:T(8,128)S(1)} %get-tuple-element.70), channel_id=1, source_target_pairs={{0,6},{32,56},{2,0},{34,58},{4,2},{36,60},{6,4},{38,62},{8,14},{40... | collective-permute-start | bytes 552968 | tf_op jit(solution)/shard_map/ppermute | solution.py:27
  76.9 2.2 %collective-permute-done.23 = f32[64,1152]{1,0:T(8,128)S(1)} collective-permute-done((f32[64,1152]{1,0:T(8,128)S(1)}, f32[64,1152]{1,0:T(8,128)S(1)}, u32[]{:S(2)}, u32[]{:S(2)}) %collective-permute-start.23) | collective-permute-done | bytes 294944 | tf_op jit(solution)/shard_map/ppermute | solution.py:27
  79.3 1.4 %collective-permute-done.16 = f32[40,1152]{1,0:T(8,128)S(1)} collective-permute-done((f32[40,1152]{1,0:T(8,128)S(1)}, f32[40,1152]{1,0:T(8,128)S(1)}, u32[]{:S(2)}, u32[]{:S(2)}) %collective-permute-start.16) | collective-permute-done | bytes 184352 | tf_op jit(solution)/shard_map/ppermute | solution.py:27
  80.7 1.6 %collective-permute-done.17 = f32[40,1152]{1,0:T(8,128)S(1)} collective-permute-done((f32[40,1152]{1,0:T(8,128)S(1)}, f32[40,1152]{1,0:T(8,128)S(1)}, u32[]{:S(2)}, u32[]{:S(2)}) %collective-permute-start.17) | collective-permute-done | bytes 184352 | tf_op jit(solution)/shard_map/ppermute | solution.py:27
  82.3 1.3 %collective-permute-done.18 = f32[40,1152]{1,0:T(8,128)S(1)} collective-permute-done((f32[40,1152]{1,0:T(8,128)S(1)}, f32[40,1152]{1,0:T(8,128)S(1)}, u32[]{:S(2)}, u32[]{:S(2)}) %collective-permute-start.18) | collective-permute-done | bytes 184352 | tf_op jit(solution)/shard_map/ppermute | solution.py:27
  83.8 3.1 %collective-permute-start.20 = (f32[8,128]{1,0:T(8,128)S(1)}, f32[8,128]{1,0:T(8,128)S(1)}, u32[]{:S(2)}, u32[]{:S(2)}) collective-permute-start(f32[8,128]{1,0:T(8,128)S(1)} %pad_maximum_fusion.9), channel_id=1, source_target_pairs={{0,192},{32,96},{2,194},{34,98},{4,196},{36,100},{6,198},{38,102},... | collective-permute-start | bytes 12296 | tf_op jit(solution)/shard_map/ppermute | solution.py:27
  86.9 1.0 collective-permute-start.19
  87.9 0.2 multiply_reduce_fusion.2
  88.0 0.3 collective-permute-done.20
  88.3 0.8 subtract_multiply_fusion.1
  89.1 5.3 %collective-permute-done.19 = f32[8,128]{1,0:T(8,128)S(1)} collective-permute-done((f32[8,128]{1,0:T(8,128)S(1)}, f32[8,128]{1,0:T(8,128)S(1)}, u32[]{:S(2)}, u32[]{:S(2)}) %collective-permute-start.19) | collective-permute-done | bytes 4128 | tf_op jit(solution)/shard_map/ppermute | solution.py:27
  94.5 0.6 fusion.3
  96.4 0.2 multiply_reduce_fusion
  96.6 0.8 subtract_multiply_fusion
  (49 shorter events, 1.9 us)
Async XLA Ops:
  0.6 12.6 %collective-permute-start.2 = (f32[32,1152]{1,0:T(8,128)}, f32[32,1152]{1,0:T(8,128)S(1)}, u32[]{:S(2)}, u32[]{:S(2)}) collective-permute-start(f32[32,1152]{1,0:T(8,128)} %param.4), channel_id=1, source_target_pairs={{0,4},{32,48},{2,6},{34,50},{4,0},{36,52},{6,2},{38,54},{8,12},{40... | collective-permute-start | bytes 442376 | tf_op jit(solution)/shard_map/ppermute | solution.py:27
  3.7 9.4 %collective-permute-start.1 = (f32[32,1152]{1,0:T(8,128)}, f32[32,1152]{1,0:T(8,128)S(1)}, u32[]{:S(2)}, u32[]{:S(2)}) collective-permute-start(f32[32,1152]{1,0:T(8,128)} %param.4), channel_id=1, source_target_pairs={{0,6},{32,56},{2,0},{34,58},{4,2},{36,60},{6,4},{38,62},{8,14},{40... | collective-permute-start | bytes 442376 | tf_op jit(solution)/shard_map/ppermute | solution.py:27
  4.9 8.3 %collective-permute-start = (f32[32,1152]{1,0:T(8,128)}, f32[32,1152]{1,0:T(8,128)S(1)}, u32[]{:S(2)}, u32[]{:S(2)}) collective-permute-start(f32[32,1152]{1,0:T(8,128)} %param.4), channel_id=1, source_target_pairs={{0,2},{32,40},{2,4},{34,42},{4,6},{36,44},{6,0},{38,46},{8,10},{40... | collective-permute-start | bytes 442376 | tf_op jit(solution)/shard_map/ppermute | solution.py:27
  5.8 2.1 %collective-permute-start.3 = (f32[32,1152]{1,0:T(8,128)}, f32[32,1152]{1,0:T(8,128)S(1)}, u32[]{:S(2)}, u32[]{:S(2)}) collective-permute-start(f32[32,1152]{1,0:T(8,128)} %refs_1_.1), channel_id=1, source_target_pairs={{0,32},{32,0},{2,34},{34,2},{4,36},{36,4},{6,38},{38,6},{8,40},{40... | collective-permute-start | bytes 442376 | tf_op jit(solution)/shard_map/ppermute | solution.py:27
  7.8 19.8 %copy-start = (f32[32,1152]{1,0:T(8,128)S(1)}, f32[32,1152]{1,0:T(8,128)}, u32[]{:S(2)}) copy-start(f32[32,1152]{1,0:T(8,128)} %refs_1_.1) | copy-start | bytes 442372
  7.9 11.7 %collective-permute-start.5 = (f32[64,1152]{1,0:T(8,128)S(1)}, f32[64,1152]{1,0:T(8,128)S(1)}, u32[]{:S(2)}, u32[]{:S(2)}) collective-permute-start(f32[64,1152]{1,0:T(8,128)S(1)} %constant_dynamic-update-slice_fusion.4), channel_id=1, source_target_pairs={{0,64},{32,224},{2,66},{34,226},{4,68},{36,228},{6,70},{38,230},{8... | collective-permute-start | bytes 884744 | tf_op jit(solution)/shard_map/ppermute | solution.py:27
  11.2 13.6 %collective-permute-start.4 = (f32[64,1152]{1,0:T(8,128)S(1)}, f32[64,1152]{1,0:T(8,128)S(1)}, u32[]{:S(2)}, u32[]{:S(2)}) collective-permute-start(f32[64,1152]{1,0:T(8,128)S(1)} %constant_dynamic-update-slice_fusion.4), channel_id=1, source_target_pairs={{0,1},{32,225},{2,3},{34,227},{4,5},{36,229},{6,7},{38,231},{8,9},... | collective-permute-start | bytes 884744 | tf_op jit(solution)/shard_map/ppermute | solution.py:27
  13.2 16.7 %collective-permute-start.8 = (f32[128,1152]{1,0:T(8,128)S(1)}, f32[128,1152]{1,0:T(8,128)S(1)}, u32[]{:S(2)}, u32[]{:S(2)}) collective-permute-start(f32[128,1152]{1,0:T(8,128)S(1)} %constant_dynamic-update-slice_fusion.refs_0_), channel_id=1, source_target_pairs={{0,16},{32,36},{2,18},{34,38},{4,20},{36,32},{6,22},{38,34},{8,24}... | collective-permute-start | bytes 1769480 | tf_op jit(solution)/shard_map/ppermute | solution.py:27
  15.6 15.4 %collective-permute-start.7 = (f32[128,1152]{1,0:T(8,128)S(1)}, f32[128,1152]{1,0:T(8,128)S(1)}, u32[]{:S(2)}, u32[]{:S(2)}) collective-permute-start(f32[128,1152]{1,0:T(8,128)S(1)} %constant_dynamic-update-slice_fusion.refs_0_), channel_id=1, source_target_pairs={{0,24},{32,38},{2,26},{34,32},{4,28},{36,34},{6,30},{38,36},{8,0},... | collective-permute-start | bytes 1769480 | tf_op jit(solution)/shard_map/ppermute | solution.py:27
  17.0 14.2 %collective-permute-start.6 = (f32[128,1152]{1,0:T(8,128)S(1)}, f32[128,1152]{1,0:T(8,128)S(1)}, u32[]{:S(2)}, u32[]{:S(2)}) collective-permute-start(f32[128,1152]{1,0:T(8,128)S(1)} %constant_dynamic-update-slice_fusion.refs_0_), channel_id=1, source_target_pairs={{0,8},{32,34},{2,10},{34,36},{4,12},{36,38},{6,14},{38,32},{8,16},... | collective-permute-start | bytes 1769480 | tf_op jit(solution)/shard_map/ppermute | solution.py:27
  24.9 14.5 %collective-permute-start.9 = (f32[96,1152]{1,0:T(8,128)S(1)}, f32[96,1152]{1,0:T(8,128)S(1)}, u32[]{:S(2)}, u32[]{:S(2)}) collective-permute-start(f32[96,1152]{1,0:T(8,128)S(1)} %pad_maximum_fusion.6), channel_id=1, source_target_pairs={{0,64},{32,224},{2,66},{34,226},{4,68},{36,228},{6,70},{38,230},{8... | collective-permute-start | bytes 1327112 | tf_op jit(solution)/shard_map/ppermute | solution.py:27
  39.5 3.1 %collective-permute-start.10 = (f32[224,1152]{1,0:T(8,128)S(1)}, f32[224,1152]{1,0:T(8,128)S(1)}, u32[]{:S(2)}, u32[]{:S(2)}) collective-permute-start(f32[224,1152]{1,0:T(8,128)S(1)} %pad_maximum_fusion.5), channel_id=1, source_target_pairs={{0,32},{32,0},{2,34},{34,2},{4,36},{36,4},{6,38},{38,6},{8,40},{40... | collective-permute-start | bytes 3096584 | tf_op jit(solution)/shard_map/ppermute | solution.py:27
  44.4 3.7 %collective-permute-start.11 = (f32[8,128]{1,0:T(8,128)S(1)}, f32[8,128]{1,0:T(8,128)S(1)}, u32[]{:S(2)}, u32[]{:S(2)}) collective-permute-start(f32[8,128]{1,0:T(8,128)S(1)} %get-tuple-element.63), channel_id=1, source_target_pairs={{0,1},{32,33},{2,3},{34,35},{4,5},{36,37},{6,7},{38,39},{8,9},{40,... | collective-permute-start | bytes 12296 | tf_op jit(solution)/shard_map/ppermute | solution.py:27
  48.6 3.0 %collective-permute-start.12 = (f32[264,1152]{1,0:T(8,128)S(1)}, f32[264,1152]{1,0:T(8,128)S(1)}, u32[]{:S(2)}, u32[]{:S(2)}) collective-permute-start(f32[264,1152]{1,0:T(8,128)S(1)} %pad_maximum_fusion.4), channel_id=1, source_target_pairs={{0,32},{32,0},{2,34},{34,2},{4,36},{36,4},{6,38},{38,6},{8,40},{40... | collective-permute-start | bytes 3649544 | tf_op jit(solution)/shard_map/ppermute | solution.py:27
  51.6 14.1 %collective-permute-start.22 = (f32[96,1152]{1,0:T(8,128)S(1)}, f32[96,1152]{1,0:T(8,128)S(1)}, u32[]{:S(2)}, u32[]{:S(2)}) collective-permute-start(f32[96,1152]{1,0:T(8,128)S(1)} %slice_add_fusion), channel_id=1, source_target_pairs={{0,192},{32,96},{2,194},{34,98},{4,196},{36,100},{6,198},{38,102},... | collective-permute-start | bytes 1327112 | tf_op jit(solution)/shard_map/ppermute | solution.py:27
  54.4 16.7 %collective-permute-start.15 = (f32[136,1152]{1,0:T(8,128)S(1)}, f32[136,1152]{1,0:T(8,128)S(1)}, u32[]{:S(2)}, u32[]{:S(2)}) collective-permute-start(f32[136,1152]{1,0:T(8,128)S(1)} %get-tuple-element.87), channel_id=1, source_target_pairs={{0,16},{32,36},{2,18},{34,38},{4,20},{36,32},{6,22},{38,34},{8,24}... | collective-permute-start | bytes 1880072 | tf_op jit(solution)/shard_map/ppermute | solution.py:27
  56.8 16.2 %collective-permute-start.13 = (f32[136,1152]{1,0:T(8,128)S(1)}, f32[136,1152]{1,0:T(8,128)S(1)}, u32[]{:S(2)}, u32[]{:S(2)}) collective-permute-start(f32[136,1152]{1,0:T(8,128)S(1)} %get-tuple-element.88), channel_id=1, source_target_pairs={{0,24},{32,38},{2,26},{34,32},{4,28},{36,34},{6,30},{38,36},{8,0},... | collective-permute-start | bytes 1880072 | tf_op jit(solution)/shard_map/ppermute | solution.py:27
  58.1 15.0 %collective-permute-start.14 = (f32[136,1152]{1,0:T(8,128)S(1)}, f32[136,1152]{1,0:T(8,128)S(1)}, u32[]{:S(2)}, u32[]{:S(2)}) collective-permute-start(f32[136,1152]{1,0:T(8,128)S(1)} %get-tuple-element.89), channel_id=1, source_target_pairs={{0,8},{32,34},{2,10},{34,36},{4,12},{36,38},{6,14},{38,32},{8,16},... | collective-permute-start | bytes 1880072 | tf_op jit(solution)/shard_map/ppermute | solution.py:27
  65.8 11.0 %collective-permute-start.24 = (f32[64,1152]{1,0:T(8,128)S(1)}, f32[64,1152]{1,0:T(8,128)S(1)}, u32[]{:S(2)}, u32[]{:S(2)}) collective-permute-start(f32[64,1152]{1,0:T(8,128)S(1)} %pad_maximum_fusion.7), channel_id=1, source_target_pairs={{0,192},{32,96},{2,194},{34,98},{4,196},{36,100},{6,198},{38,102},... | collective-permute-start | bytes 884744 | tf_op jit(solution)/shard_map/ppermute | solution.py:27
  69.6 9.5 %collective-permute-start.23 = (f32[64,1152]{1,0:T(8,128)S(1)}, f32[64,1152]{1,0:T(8,128)S(1)}, u32[]{:S(2)}, u32[]{:S(2)}) collective-permute-start(f32[64,1152]{1,0:T(8,128)S(1)} %get-tuple-element.78), channel_id=1, source_target_pairs={{0,193},{32,33},{2,195},{34,35},{4,197},{36,37},{6,199},{38,39},{8... | collective-permute-start | bytes 884744 | tf_op jit(solution)/shard_map/ppermute | solution.py:27
  73.3 14.6 %copy-start.1 = (f32[32,1152]{1,0:T(8,128)S(1)}, f32[32,1152]{1,0:T(8,128)}, u32[]{:S(2)}) copy-start(f32[32,1152]{1,0:T(8,128)} %param.4) | copy-start | bytes 442372
  73.3 7.3 %collective-permute-start.16 = (f32[40,1152]{1,0:T(8,128)S(1)}, f32[40,1152]{1,0:T(8,128)S(1)}, u32[]{:S(2)}, u32[]{:S(2)}) collective-permute-start(f32[40,1152]{1,0:T(8,128)S(1)} %get-tuple-element.69), channel_id=1, source_target_pairs={{0,4},{32,48},{2,6},{34,50},{4,0},{36,52},{6,2},{38,54},{8,12},{40... | collective-permute-start | bytes 552968 | tf_op jit(solution)/shard_map/ppermute | solution.py:27
  74.7 7.6 %collective-permute-start.17 = (f32[40,1152]{1,0:T(8,128)S(1)}, f32[40,1152]{1,0:T(8,128)S(1)}, u32[]{:S(2)}, u32[]{:S(2)}) collective-permute-start(f32[40,1152]{1,0:T(8,128)S(1)} %get-tuple-element.70), channel_id=1, source_target_pairs={{0,6},{32,56},{2,0},{34,58},{4,2},{36,60},{6,4},{38,62},{8,14},{40... | collective-permute-start | bytes 552968 | tf_op jit(solution)/shard_map/ppermute | solution.py:27
  76.9 6.7 %collective-permute-start.18 = (f32[40,1152]{1,0:T(8,128)S(1)}, f32[40,1152]{1,0:T(8,128)S(1)}, u32[]{:S(2)}, u32[]{:S(2)}) collective-permute-start(f32[40,1152]{1,0:T(8,128)S(1)} %get-tuple-element.71), channel_id=1, source_target_pairs={{0,2},{32,40},{2,4},{34,42},{4,6},{36,44},{6,0},{38,46},{8,10},{40... | collective-permute-start | bytes 552968 | tf_op jit(solution)/shard_map/ppermute | solution.py:27
  79.2 17.2 %collective-permute-start.25 = (f32[32,1152]{1,0:T(8,128)S(1)}, f32[32,1152]{1,0:T(8,128)S(1)}, u32[]{:S(2)}, u32[]{:S(2)}) collective-permute-start(f32[32,1152]{1,0:T(8,128)S(1)} %slice.106), channel_id=1, source_target_pairs={{0,32},{32,0},{2,34},{34,2},{4,36},{36,4},{6,38},{38,6},{8,40},{40... | collective-permute-start | bytes 442376 | tf_op jit(solution)/shard_map/ppermute | solution.py:27
  83.8 4.5 %collective-permute-start.20 = (f32[8,128]{1,0:T(8,128)S(1)}, f32[8,128]{1,0:T(8,128)S(1)}, u32[]{:S(2)}, u32[]{:S(2)}) collective-permute-start(f32[8,128]{1,0:T(8,128)S(1)} %pad_maximum_fusion.9), channel_id=1, source_target_pairs={{0,192},{32,96},{2,194},{34,98},{4,196},{36,100},{6,198},{38,102},... | collective-permute-start | bytes 12296 | tf_op jit(solution)/shard_map/ppermute | solution.py:27
  86.9 7.5 %collective-permute-start.19 = (f32[8,128]{1,0:T(8,128)S(1)}, f32[8,128]{1,0:T(8,128)S(1)}, u32[]{:S(2)}, u32[]{:S(2)}) collective-permute-start(f32[8,128]{1,0:T(8,128)S(1)} %pad_maximum_fusion.9), channel_id=1, source_target_pairs={{0,128},{32,160},{2,130},{34,162},{4,132},{36,164},{6,134},{38,166... | collective-permute-start | bytes 12296 | tf_op jit(solution)/shard_map/ppermute | solution.py:27
  88.3 6.1 %collective-permute-start.21 = (f32[8,128]{1,0:T(8,128)S(1)}, f32[8,128]{1,0:T(8,128)S(1)}, u32[]{:S(2)}, u32[]{:S(2)}) collective-permute-start(f32[8,128]{1,0:T(8,128)S(1)} %collective-permute-done.20), channel_id=1, source_target_pairs={{0,32},{32,0},{2,34},{34,2},{4,36},{36,4},{6,38},{38,6},{8,40},{40... | collective-permute-start | bytes 12296 | tf_op jit(solution)/shard_map/ppermute | solution.py:27

commit v4 on v3

--- a/solution.py
+++ b/solution.py
@@ -294,8 +294,6 @@
     loss = jnp.concatenate([total[rows:, :64], total[rows:, -64:]], 1)
     beside = along_z(loss, -2)
     loss = loss + send(loss, lambda z, y, x, core: (z + 4, y, x, core))
-    loss = loss + beside + swap(beside)
-    loss = ((loss[0, 0] + loss[0, 127]) / (rows * 2 * NX * NY * NZ)).reshape(1)
 
     image_unit, image_inv = normalize(image_emb)
     text_unit, text_inv = normalize(text_emb)
@@ -305,7 +303,8 @@
     text_grad = (
         text_unit_grad - text_unit * jnp.sum(text_unit * text_unit_grad, axis=1, keepdims=True)
     ) * text_inv
-    return (loss, image_grad, text_grad)
+    loss = loss + beside + swap(after(beside, (image_grad, text_grad)))
+    return ((loss[:1, 0] + loss[:1, 127]) / (rows * 2 * NX * NY * NZ), image_grad, text_grad)
 
 
 def solution(mesh):

time: 98.6 us -> 97.7 us (level)
  waiting for transfers between devices: 36.7 us -> 35.7 us
  transfers between devices with their start and end apart: 26 -> 26, of which waited for: 16 -> 15; matrix products, arithmetic and copies ran while one was open for 4% -> 5% of each run, Pallas kernels for 13% -> 13%
where the time goes in v4:
time: 97.7 us; the launch traced here: 97.5 us
  starting transfers between devices  36.7 us (38%)
  waiting for transfers between devices  35.7 us (37%)
  Pallas kernels  14.5 us (15%)
  other arithmetic  4.93 us (5%)
  between operations  4.64 us (5%)
  local copies, waits for them, and re-layouts  1.08 us (1%)
    ppermute x26, starting transfers between devices, send(): return lax.ppermute(value, AXES, pairs(target))  36.7 us
    ppermute x26, waiting for transfers between devices, send(): return lax.ppermute(value, AXES, pairs(target))  35.7 us
    pallas_call x2, Pallas kernels, group_call(): pl.pallas_call(functools.partial(group_kernel, texts[0].shape[0] if start...  6.67 us
    pallas_call x1, Pallas kernels, last_call(): pl.pallas_call(last_kernel, out_shape=[f32(count + other.shape[0], width)...  3.11 us
    pallas_call x1, Pallas kernels, mid_call(): pl.pallas_call(mid_kernel, out_shape=[b16(rows, width)] * 2 + [f32(count,...  2.77 us
    reduce_sum x2, other arithmetic, normalize(): inverse = lax.rsqrt(jnp.sum(embed * embed, axis=1, keepdims=True) + 1e-06)  2.07 us
  transfers between devices with their start and end apart: 26, of which 15 were waited for; matrix products, arithmetic and copies ran while one was open for 5% of the time, Pallas kernels for 13%

profile of v4, /device:TPU:8, one launch (start us, length us, event | category | flops | bytes accessed | tf_op | source)
XLA Modules:
  0.0 97.5 jit_solution(4220423150548894118)
XLA Ops:
  0.6 3.1 %collective-permute-start.2 = (f32[32,1152]{1,0:T(8,128)}, f32[32,1152]{1,0:T(8,128)S(1)}, u32[]{:S(2)}, u32[]{:S(2)}) collective-permute-start(f32[32,1152]{1,0:T(8,128)} %param.4), channel_id=1, source_target_pairs={{0,4},{32,48},{2,6},{34,50},{4,0},{36,52},{6,2},{38,54},{8,12},{40... | collective-permute-start | bytes 442376 | tf_op jit(solution)/shard_map/ppermute | solution.py:27
  3.7 1.1 %collective-permute-start.1 = (f32[32,1152]{1,0:T(8,128)}, f32[32,1152]{1,0:T(8,128)S(1)}, u32[]{:S(2)}, u32[]{:S(2)}) collective-permute-start(f32[32,1152]{1,0:T(8,128)} %param.4), channel_id=1, source_target_pairs={{0,6},{32,56},{2,0},{34,58},{4,2},{36,60},{6,4},{38,62},{8,14},{40... | collective-permute-start | bytes 442376 | tf_op jit(solution)/shard_map/ppermute | solution.py:27
  4.9 0.9 collective-permute-start
  5.8 1.0 %multiply_reduce_fusion.1 = (f32[32]{0:T(128)S(1)}, f32[64,1152]{1,0:T(8,128)S(1)}) fusion(f32[32,1152]{1,0:T(8,128)} %refs_1_.1), kind=kLoop, calls=%fused_computation.19 | loop fusion | flops 73695 | bytes 295424 | tf_op jit(solution)/shard_map/reduce_sum | solution.py:256
  6.8 1.0 %multiply_reduce_fusion.3 = (f32[32]{0:T(128)S(1)}, f32[128,1152]{1,0:T(8,128)S(1)}) fusion(f32[32,1152]{1,0:T(8,128)} %param.4), kind=kLoop, calls=%fused_computation.22 | loop fusion | flops 73695 | bytes 295424 | tf_op jit(solution)/shard_map/reduce_sum | solution.py:256
  7.9 3.3 %collective-permute-start.5 = (f32[64,1152]{1,0:T(8,128)S(1)}, f32[64,1152]{1,0:T(8,128)S(1)}, u32[]{:S(2)}, u32[]{:S(2)}) collective-permute-start(f32[64,1152]{1,0:T(8,128)S(1)} %constant_dynamic-update-slice_fusion.4), channel_id=1, source_target_pairs={{0,64},{32,224},{2,66},{34,226},{4,68},{36,228},{6,70},{38,230},{8... | collective-permute-start | bytes 884744 | tf_op jit(solution)/shard_map/ppermute | solution.py:27
  11.2 1.9 %collective-permute-start.4 = (f32[64,1152]{1,0:T(8,128)S(1)}, f32[64,1152]{1,0:T(8,128)S(1)}, u32[]{:S(2)}, u32[]{:S(2)}) collective-permute-start(f32[64,1152]{1,0:T(8,128)S(1)} %constant_dynamic-update-slice_fusion.4), channel_id=1, source_target_pairs={{0,1},{32,225},{2,3},{34,227},{4,5},{36,229},{6,7},{38,231},{8,9},... | collective-permute-start | bytes 884744 | tf_op jit(solution)/shard_map/ppermute | solution.py:27
  13.2 2.4 %collective-permute-start.8 = (f32[128,1152]{1,0:T(8,128)S(1)}, f32[128,1152]{1,0:T(8,128)S(1)}, u32[]{:S(2)}, u32[]{:S(2)}) collective-permute-start(f32[128,1152]{1,0:T(8,128)S(1)} %constant_dynamic-update-slice_fusion.refs_0_), channel_id=1, source_target_pairs={{0,16},{32,36},{2,18},{34,38},{4,20},{36,32},{6,22},{38,34},{8,24}... | collective-permute-start | bytes 1769480 | tf_op jit(solution)/shard_map/ppermute | solution.py:27
  15.6 1.3 %collective-permute-start.7 = (f32[128,1152]{1,0:T(8,128)S(1)}, f32[128,1152]{1,0:T(8,128)S(1)}, u32[]{:S(2)}, u32[]{:S(2)}) collective-permute-start(f32[128,1152]{1,0:T(8,128)S(1)} %constant_dynamic-update-slice_fusion.refs_0_), channel_id=1, source_target_pairs={{0,24},{32,38},{2,26},{34,32},{4,28},{36,34},{6,30},{38,36},{8,0},... | collective-permute-start | bytes 1769480 | tf_op jit(solution)/shard_map/ppermute | solution.py:27
  17.0 0.7 collective-permute-start.6
  17.6 1.9 %collective-permute-done.5.refs_4_ = f32[64,1152]{1,0:T(8,128)S(1)} collective-permute-done((f32[64,1152]{1,0:T(8,128)S(1)}, f32[64,1152]{1,0:T(8,128)S(1)}, u32[]{:S(2)}, u32[]{:S(2)}) %collective-permute-start.5) | collective-permute-done | bytes 294944 | tf_op jit(solution)/shard_map/ppermute | solution.py:27
  19.6 5.3 %collective-permute-done.4.refs_3_ = f32[64,1152]{1,0:T(8,128)S(1)} collective-permute-done((f32[64,1152]{1,0:T(8,128)S(1)}, f32[64,1152]{1,0:T(8,128)S(1)}, u32[]{:S(2)}, u32[]{:S(2)}) %collective-permute-start.4) | collective-permute-done | bytes 294944 | tf_op jit(solution)/shard_map/ppermute | solution.py:27
  24.9 1.5 %collective-permute-start.9 = (f32[96,1152]{1,0:T(8,128)S(1)}, f32[96,1152]{1,0:T(8,128)S(1)}, u32[]{:S(2)}, u32[]{:S(2)}) collective-permute-start(f32[96,1152]{1,0:T(8,128)S(1)} %pad_maximum_fusion.6), channel_id=1, source_target_pairs={{0,64},{32,224},{2,66},{34,226},{4,68},{36,228},{6,70},{38,230},{8... | collective-permute-start | bytes 1327112 | tf_op jit(solution)/shard_map/ppermute | solution.py:27
  27.6 2.3 %shard_map.67 = (f32[128,1152]{1,0:T(8,128)S(1)}, bf16[128,1152]{1,0:T(8,128)(2,1)S(1)}, bf16[128,1152]{1,0:T(8,128)(2,1)S(1)}, f32[192,1152]{1,0:T(8,128)S(1)},...) custom-call(f32[1]{0:T(128)S(6)} %copy.11.scale, f32[1]{0:T(128)S(6)} %copy.12.bias, ...), custom_call_target="tpu_custom_call" | custom-call | flops 509607936 | bytes 589824 | tf_op jit(solution)/shard_map/pallas_call | solution.py:191
  29.9 1.1 %collective-permute-done.7.refs_1_ = f32[128,1152]{1,0:T(8,128)S(1)} collective-permute-done((f32[128,1152]{1,0:T(8,128)S(1)}, f32[128,1152]{1,0:T(8,128)S(1)}, u32[]{:S(2)}, u32[]{:S(2)}) %collective-permute-start.7) | collective-permute-done | bytes 589856 | tf_op jit(solution)/shard_map/ppermute | solution.py:27
  31.2 4.4 %shard_map.68 = (f32[384,1152]{1,0:T(8,128)S(1)}, bf16[384,1152]{1,0:T(8,128)(2,1)S(1)}, bf16[384,1152]{1,0:T(8,128)(2,1)S(1)}, f32[192,1152]{1,0:T(8,128)S(1)}, f32[8,128]{1,0:T(8,128)S(1)}) custom-call(f32[1]{0:T(128)S(6)} %copy.11.scale, f32[1]{0:T(128)S(6)} %copy.12.bias, f32[128,1152]{1,0:T(8,128)S(1)} %collective-permute-done.6.refs_0_, ...), custom_call_target="tpu_custom_call" | custom-call | flops 1528823808 | bytes 1769472 | tf_op jit(solution)/shard_map/pallas_call | solution.py:191
  35.6 3.8 %collective-permute-done.9.raw = f32[96,1152]{1,0:T(8,128)S(1)} collective-permute-done((f32[96,1152]{1,0:T(8,128)S(1)}, f32[96,1152]{1,0:T(8,128)S(1)}, u32[]{:S(2)}, u32[]{:S(2)}) %collective-permute-start.9) | collective-permute-done | bytes 442400 | tf_op jit(solution)/shard_map/ppermute | solution.py:27
  39.5 0.3 collective-permute-start.10
  39.8 2.8 %shard_map.69 = (bf16[512,1152]{1,0:T(8,128)(2,1)S(1)}, bf16[512,1152]{1,0:T(8,128)(2,1)S(1)}, f32[96,1152]{1,0:T(8,128)S(1)}, bf16[512,96]{1,0:T(8,128)(2,1)S(1...) custom-call(f32[1]{0:T(128)S(6)} %copy.11.scale, ...), custom_call_target="tpu_custom_call" | custom-call | flops 679477248 | bytes 2359296 | tf_op jit(solution)/shard_map/pallas_call | solution.py:204
  42.5 1.8 %shard_map.70 = (bf16[512,224]{1,0:T(8,128)(2,1)S(1)}, bf16[512,224]{1,0:T(8,128)(2,1)S(1)}, bf16[224,1152]{1,0:T(8,128)(2,1)S(1)}, bf16[224,1152]{1,0:T(8,128)(2,1)S(1)}, f32[8,128]{1,0:T(8,128)S(1)}) custom-call(f32[1]{0:T(128)S(6)} %copy.11.scale, f32[1]{0:T(128)S(6)} %copy.12.bias, bf16[512,1152]{1,0:T(8,128)(2,1)S(1)} %get-tuple-element.48.ihi, ...), custom_call_target="tpu_custom_call" | custom-call | flops 792723456 | bytes 2359296 | tf_op jit(solution)/shard_map/pallas_call | solution.py:221
  44.5 3.1 %shard_map.71 = (f32[256,1152]{1,0:T(8,128)S(1)}, f32[128,1152]{1,0:T(8,128)S(1)}, f32[128,1152]{1,0:T(8,128)S(1)}, f32[128,1152]{1,0:T(8,128)S(1)}, f32[128,1152]{1,0:T(8,128)S(1)}) custom-call(bf16[512,1152]{1,0:T(8,128)(2,1)S(1)} %get-tuple-element.48.ihi, bf16[512,1152]{1,0:T(8,128)(2,1)S(1)} %get-tuple-element.49.ilo, ...), custom_call_target="tpu_custom_call" | custom-call | flops 3963617280 | bytes 2359296 | tf_op jit(solution)/shard_map/pallas_call | solution.py:234
  47.6 0.5 collective-permute-done.11
  48.1 0.2 slice_reduce_fusion.1
  48.7 2.9 %collective-permute-done.12 = f32[264,1152]{1,0:T(8,128)S(1)} collective-permute-done((f32[264,1152]{1,0:T(8,128)S(1)}, f32[264,1152]{1,0:T(8,128)S(1)}, u32[]{:S(2)}, u32[]{:S(2)}) %collective-permute-start.12) | collective-permute-done | bytes 1216544 | tf_op jit(solution)/shard_map/ppermute | solution.py:27
  51.6 2.5 %collective-permute-start.21 = (f32[96,1152]{1,0:T(8,128)S(1)}, f32[96,1152]{1,0:T(8,128)S(1)}, u32[]{:S(2)}, u32[]{:S(2)}) collective-permute-start(f32[96,1152]{1,0:T(8,128)S(1)} %slice_add_fusion), channel_id=1, source_target_pairs={{0,192},{32,96},{2,194},{34,98},{4,196},{36,100},{6,198},{38,102},... | collective-permute-start | bytes 1327112 | tf_op jit(solution)/shard_map/ppermute | solution.py:27
  54.2 0.2 pad_maximum_fusion
  54.4 2.4 %collective-permute-start.15 = (f32[136,1152]{1,0:T(8,128)S(1)}, f32[136,1152]{1,0:T(8,128)S(1)}, u32[]{:S(2)}, u32[]{:S(2)}) collective-permute-start(f32[136,1152]{1,0:T(8,128)S(1)} %get-tuple-element.89), channel_id=1, source_target_pairs={{0,16},{32,36},{2,18},{34,38},{4,20},{36,32},{6,22},{38,34},{8,24}... | collective-permute-start | bytes 1880072 | tf_op jit(solution)/shard_map/ppermute | solution.py:27
  56.8 1.3 %collective-permute-start.13 = (f32[136,1152]{1,0:T(8,128)S(1)}, f32[136,1152]{1,0:T(8,128)S(1)}, u32[]{:S(2)}, u32[]{:S(2)}) collective-permute-start(f32[136,1152]{1,0:T(8,128)S(1)} %get-tuple-element.90), channel_id=1, source_target_pairs={{0,24},{32,38},{2,26},{34,32},{4,28},{36,34},{6,30},{38,36},{8,0},... | collective-permute-start | bytes 1880072 | tf_op jit(solution)/shard_map/ppermute | solution.py:27
  58.1 0.7 collective-permute-start.14
  58.8 6.9 %collective-permute-done.21 = f32[96,1152]{1,0:T(8,128)S(1)} collective-permute-done((f32[96,1152]{1,0:T(8,128)S(1)}, f32[96,1152]{1,0:T(8,128)S(1)}, u32[]{:S(2)}, u32[]{:S(2)}) %collective-permute-start.21) | collective-permute-done | bytes 442400 | tf_op jit(solution)/shard_map/ppermute | solution.py:27
  65.8 3.7 %collective-permute-start.23 = (f32[64,1152]{1,0:T(8,128)S(1)}, f32[64,1152]{1,0:T(8,128)S(1)}, u32[]{:S(2)}, u32[]{:S(2)}) collective-permute-start(f32[64,1152]{1,0:T(8,128)S(1)} %pad_maximum_fusion.7), channel_id=1, source_target_pairs={{0,192},{32,96},{2,194},{34,98},{4,196},{36,100},{6,198},{38,102},... | collective-permute-start | bytes 884744 | tf_op jit(solution)/shard_map/ppermute | solution.py:27
  69.6 1.5 %collective-permute-start.22 = (f32[64,1152]{1,0:T(8,128)S(1)}, f32[64,1152]{1,0:T(8,128)S(1)}, u32[]{:S(2)}, u32[]{:S(2)}) collective-permute-start(f32[64,1152]{1,0:T(8,128)S(1)} %get-tuple-element.80), channel_id=1, source_target_pairs={{0,193},{32,33},{2,195},{34,35},{4,197},{36,37},{6,199},{38,39},{8... | collective-permute-start | bytes 884744 | tf_op jit(solution)/shard_map/ppermute | solution.py:27
  71.1 1.9 %collective-permute-done.13.in1 = f32[136,1152]{1,0:T(8,128)S(1)} collective-permute-done((f32[136,1152]{1,0:T(8,128)S(1)}, f32[136,1152]{1,0:T(8,128)S(1)}, u32[]{:S(2)}, u32[]{:S(2)}) %collective-permute-start.13) | collective-permute-done | bytes 626720 | tf_op jit(solution)/shard_map/ppermute | solution.py:27
  73.0 0.2 collective-permute-done.14.in2
  73.3 1.4 %collective-permute-start.16 = (f32[40,1152]{1,0:T(8,128)S(1)}, f32[40,1152]{1,0:T(8,128)S(1)}, u32[]{:S(2)}, u32[]{:S(2)}) collective-permute-start(f32[40,1152]{1,0:T(8,128)S(1)} %get-tuple-element.70), channel_id=1, source_target_pairs={{0,4},{32,48},{2,6},{34,50},{4,0},{36,52},{6,2},{38,54},{8,12},{40... | collective-permute-start | bytes 552968 | tf_op jit(solution)/shard_map/ppermute | solution.py:27
  74.7 2.1 %collective-permute-start.17 = (f32[40,1152]{1,0:T(8,128)S(1)}, f32[40,1152]{1,0:T(8,128)S(1)}, u32[]{:S(2)}, u32[]{:S(2)}) collective-permute-start(f32[40,1152]{1,0:T(8,128)S(1)} %get-tuple-element.71), channel_id=1, source_target_pairs={{0,6},{32,56},{2,0},{34,58},{4,2},{36,60},{6,4},{38,62},{8,14},{40... | collective-permute-start | bytes 552968 | tf_op jit(solution)/shard_map/ppermute | solution.py:27
  76.9 2.2 %collective-permute-done.22 = f32[64,1152]{1,0:T(8,128)S(1)} collective-permute-done((f32[64,1152]{1,0:T(8,128)S(1)}, f32[64,1152]{1,0:T(8,128)S(1)}, u32[]{:S(2)}, u32[]{:S(2)}) %collective-permute-start.22) | collective-permute-done | bytes 294944 | tf_op jit(solution)/shard_map/ppermute | solution.py:27
  79.3 1.4 %collective-permute-done.16 = f32[40,1152]{1,0:T(8,128)S(1)} collective-permute-done((f32[40,1152]{1,0:T(8,128)S(1)}, f32[40,1152]{1,0:T(8,128)S(1)}, u32[]{:S(2)}, u32[]{:S(2)}) %collective-permute-start.16) | collective-permute-done | bytes 184352 | tf_op jit(solution)/shard_map/ppermute | solution.py:27
  80.7 1.6 %collective-permute-done.17 = f32[40,1152]{1,0:T(8,128)S(1)} collective-permute-done((f32[40,1152]{1,0:T(8,128)S(1)}, f32[40,1152]{1,0:T(8,128)S(1)}, u32[]{:S(2)}, u32[]{:S(2)}) %collective-permute-start.17) | collective-permute-done | bytes 184352 | tf_op jit(solution)/shard_map/ppermute | solution.py:27
  82.3 1.3 %collective-permute-done.18 = f32[40,1152]{1,0:T(8,128)S(1)} collective-permute-done((f32[40,1152]{1,0:T(8,128)S(1)}, f32[40,1152]{1,0:T(8,128)S(1)}, u32[]{:S(2)}, u32[]{:S(2)}) %collective-permute-start.18) | collective-permute-done | bytes 184352 | tf_op jit(solution)/shard_map/ppermute | solution.py:27
  83.8 3.1 %collective-permute-start.20 = (f32[8,128]{1,0:T(8,128)S(1)}, f32[8,128]{1,0:T(8,128)S(1)}, u32[]{:S(2)}, u32[]{:S(2)}) collective-permute-start(f32[8,128]{1,0:T(8,128)S(1)} %pad_maximum_fusion.9), channel_id=1, source_target_pairs={{0,192},{32,96},{2,194},{34,98},{4,196},{36,100},{6,198},{38,102},... | collective-permute-start | bytes 12296 | tf_op jit(solution)/shard_map/ppermute | solution.py:27
  86.9 1.0 collective-permute-start.19
  87.9 0.2 multiply_reduce_fusion.2
  88.0 0.8 subtract_multiply_fusion.1
  88.8 0.2 multiply_reduce_fusion
  89.0 0.8 subtract_multiply_fusion
  89.8 4.6 %collective-permute-done.19 = f32[8,128]{1,0:T(8,128)S(1)} collective-permute-done((f32[8,128]{1,0:T(8,128)S(1)}, f32[8,128]{1,0:T(8,128)S(1)}, u32[]{:S(2)}, u32[]{:S(2)}) %collective-permute-start.19) | collective-permute-done | bytes 4128 | tf_op jit(solution)/shard_map/ppermute | solution.py:27
  94.5 0.6 fusion.3
  (49 shorter events, 1.7 us)
Async XLA Ops:
  0.6 12.6 %collective-permute-start.2 = (f32[32,1152]{1,0:T(8,128)}, f32[32,1152]{1,0:T(8,128)S(1)}, u32[]{:S(2)}, u32[]{:S(2)}) collective-permute-start(f32[32,1152]{1,0:T(8,128)} %param.4), channel_id=1, source_target_pairs={{0,4},{32,48},{2,6},{34,50},{4,0},{36,52},{6,2},{38,54},{8,12},{40... | collective-permute-start | bytes 442376 | tf_op jit(solution)/shard_map/ppermute | solution.py:27
  3.7 9.4 %collective-permute-start.1 = (f32[32,1152]{1,0:T(8,128)}, f32[32,1152]{1,0:T(8,128)S(1)}, u32[]{:S(2)}, u32[]{:S(2)}) collective-permute-start(f32[32,1152]{1,0:T(8,128)} %param.4), channel_id=1, source_target_pairs={{0,6},{32,56},{2,0},{34,58},{4,2},{36,60},{6,4},{38,62},{8,14},{40... | collective-permute-start | bytes 442376 | tf_op jit(solution)/shard_map/ppermute | solution.py:27
  4.9 8.3 %collective-permute-start = (f32[32,1152]{1,0:T(8,128)}, f32[32,1152]{1,0:T(8,128)S(1)}, u32[]{:S(2)}, u32[]{:S(2)}) collective-permute-start(f32[32,1152]{1,0:T(8,128)} %param.4), channel_id=1, source_target_pairs={{0,2},{32,40},{2,4},{34,42},{4,6},{36,44},{6,0},{38,46},{8,10},{40... | collective-permute-start | bytes 442376 | tf_op jit(solution)/shard_map/ppermute | solution.py:27
  5.8 2.1 %collective-permute-start.3 = (f32[32,1152]{1,0:T(8,128)}, f32[32,1152]{1,0:T(8,128)S(1)}, u32[]{:S(2)}, u32[]{:S(2)}) collective-permute-start(f32[32,1152]{1,0:T(8,128)} %refs_1_.1), channel_id=1, source_target_pairs={{0,32},{32,0},{2,34},{34,2},{4,36},{36,4},{6,38},{38,6},{8,40},{40... | collective-permute-start | bytes 442376 | tf_op jit(solution)/shard_map/ppermute | solution.py:27
  7.8 19.8 %copy-start = (f32[32,1152]{1,0:T(8,128)S(1)}, f32[32,1152]{1,0:T(8,128)}, u32[]{:S(2)}) copy-start(f32[32,1152]{1,0:T(8,128)} %refs_1_.1) | copy-start | bytes 442372
  7.9 11.7 %collective-permute-start.5 = (f32[64,1152]{1,0:T(8,128)S(1)}, f32[64,1152]{1,0:T(8,128)S(1)}, u32[]{:S(2)}, u32[]{:S(2)}) collective-permute-start(f32[64,1152]{1,0:T(8,128)S(1)} %constant_dynamic-update-slice_fusion.4), channel_id=1, source_target_pairs={{0,64},{32,224},{2,66},{34,226},{4,68},{36,228},{6,70},{38,230},{8... | collective-permute-start | bytes 884744 | tf_op jit(solution)/shard_map/ppermute | solution.py:27
  11.2 13.6 %collective-permute-start.4 = (f32[64,1152]{1,0:T(8,128)S(1)}, f32[64,1152]{1,0:T(8,128)S(1)}, u32[]{:S(2)}, u32[]{:S(2)}) collective-permute-start(f32[64,1152]{1,0:T(8,128)S(1)} %constant_dynamic-update-slice_fusion.4), channel_id=1, source_target_pairs={{0,1},{32,225},{2,3},{34,227},{4,5},{36,229},{6,7},{38,231},{8,9},... | collective-permute-start | bytes 884744 | tf_op jit(solution)/shard_map/ppermute | solution.py:27
  13.2 16.7 %collective-permute-start.8 = (f32[128,1152]{1,0:T(8,128)S(1)}, f32[128,1152]{1,0:T(8,128)S(1)}, u32[]{:S(2)}, u32[]{:S(2)}) collective-permute-start(f32[128,1152]{1,0:T(8,128)S(1)} %constant_dynamic-update-slice_fusion.refs_0_), channel_id=1, source_target_pairs={{0,16},{32,36},{2,18},{34,38},{4,20},{36,32},{6,22},{38,34},{8,24}... | collective-permute-start | bytes 1769480 | tf_op jit(solution)/shard_map/ppermute | solution.py:27
  15.6 15.4 %collective-permute-start.7 = (f32[128,1152]{1,0:T(8,128)S(1)}, f32[128,1152]{1,0:T(8,128)S(1)}, u32[]{:S(2)}, u32[]{:S(2)}) collective-permute-start(f32[128,1152]{1,0:T(8,128)S(1)} %constant_dynamic-update-slice_fusion.refs_0_), channel_id=1, source_target_pairs={{0,24},{32,38},{2,26},{34,32},{4,28},{36,34},{6,30},{38,36},{8,0},... | collective-permute-start | bytes 1769480 | tf_op jit(solution)/shard_map/ppermute | solution.py:27
  17.0 14.2 %collective-permute-start.6 = (f32[128,1152]{1,0:T(8,128)S(1)}, f32[128,1152]{1,0:T(8,128)S(1)}, u32[]{:S(2)}, u32[]{:S(2)}) collective-permute-start(f32[128,1152]{1,0:T(8,128)S(1)} %constant_dynamic-update-slice_fusion.refs_0_), channel_id=1, source_target_pairs={{0,8},{32,34},{2,10},{34,36},{4,12},{36,38},{6,14},{38,32},{8,16},... | collective-permute-start | bytes 1769480 | tf_op jit(solution)/shard_map/ppermute | solution.py:27
  24.9 14.5 %collective-permute-start.9 = (f32[96,1152]{1,0:T(8,128)S(1)}, f32[96,1152]{1,0:T(8,128)S(1)}, u32[]{:S(2)}, u32[]{:S(2)}) collective-permute-start(f32[96,1152]{1,0:T(8,128)S(1)} %pad_maximum_fusion.6), channel_id=1, source_target_pairs={{0,64},{32,224},{2,66},{34,226},{4,68},{36,228},{6,70},{38,230},{8... | collective-permute-start | bytes 1327112 | tf_op jit(solution)/shard_map/ppermute | solution.py:27
  39.5 3.1 %collective-permute-start.10 = (f32[224,1152]{1,0:T(8,128)S(1)}, f32[224,1152]{1,0:T(8,128)S(1)}, u32[]{:S(2)}, u32[]{:S(2)}) collective-permute-start(f32[224,1152]{1,0:T(8,128)S(1)} %pad_maximum_fusion.5), channel_id=1, source_target_pairs={{0,32},{32,0},{2,34},{34,2},{4,36},{36,4},{6,38},{38,6},{8,40},{40... | collective-permute-start | bytes 3096584 | tf_op jit(solution)/shard_map/ppermute | solution.py:27
  44.4 3.7 %collective-permute-start.11 = (f32[8,128]{1,0:T(8,128)S(1)}, f32[8,128]{1,0:T(8,128)S(1)}, u32[]{:S(2)}, u32[]{:S(2)}) collective-permute-start(f32[8,128]{1,0:T(8,128)S(1)} %get-tuple-element.64), channel_id=1, source_target_pairs={{0,1},{32,33},{2,3},{34,35},{4,5},{36,37},{6,7},{38,39},{8,9},{40,... | collective-permute-start | bytes 12296 | tf_op jit(solution)/shard_map/ppermute | solution.py:27
  48.6 3.0 %collective-permute-start.12 = (f32[264,1152]{1,0:T(8,128)S(1)}, f32[264,1152]{1,0:T(8,128)S(1)}, u32[]{:S(2)}, u32[]{:S(2)}) collective-permute-start(f32[264,1152]{1,0:T(8,128)S(1)} %pad_maximum_fusion.4), channel_id=1, source_target_pairs={{0,32},{32,0},{2,34},{34,2},{4,36},{36,4},{6,38},{38,6},{8,40},{40... | collective-permute-start | bytes 3649544 | tf_op jit(solution)/shard_map/ppermute | solution.py:27
  51.6 14.1 %collective-permute-start.21 = (f32[96,1152]{1,0:T(8,128)S(1)}, f32[96,1152]{1,0:T(8,128)S(1)}, u32[]{:S(2)}, u32[]{:S(2)}) collective-permute-start(f32[96,1152]{1,0:T(8,128)S(1)} %slice_add_fusion), channel_id=1, source_target_pairs={{0,192},{32,96},{2,194},{34,98},{4,196},{36,100},{6,198},{38,102},... | collective-permute-start | bytes 1327112 | tf_op jit(solution)/shard_map/ppermute | solution.py:27
  54.4 16.7 %collective-permute-start.15 = (f32[136,1152]{1,0:T(8,128)S(1)}, f32[136,1152]{1,0:T(8,128)S(1)}, u32[]{:S(2)}, u32[]{:S(2)}) collective-permute-start(f32[136,1152]{1,0:T(8,128)S(1)} %get-tuple-element.89), channel_id=1, source_target_pairs={{0,16},{32,36},{2,18},{34,38},{4,20},{36,32},{6,22},{38,34},{8,24}... | collective-permute-start | bytes 1880072 | tf_op jit(solution)/shard_map/ppermute | solution.py:27
  56.8 16.2 %collective-permute-start.13 = (f32[136,1152]{1,0:T(8,128)S(1)}, f32[136,1152]{1,0:T(8,128)S(1)}, u32[]{:S(2)}, u32[]{:S(2)}) collective-permute-start(f32[136,1152]{1,0:T(8,128)S(1)} %get-tuple-element.90), channel_id=1, source_target_pairs={{0,24},{32,38},{2,26},{34,32},{4,28},{36,34},{6,30},{38,36},{8,0},... | collective-permute-start | bytes 1880072 | tf_op jit(solution)/shard_map/ppermute | solution.py:27
  58.1 15.0 %collective-permute-start.14 = (f32[136,1152]{1,0:T(8,128)S(1)}, f32[136,1152]{1,0:T(8,128)S(1)}, u32[]{:S(2)}, u32[]{:S(2)}) collective-permute-start(f32[136,1152]{1,0:T(8,128)S(1)} %get-tuple-element.91), channel_id=1, source_target_pairs={{0,8},{32,34},{2,10},{34,36},{4,12},{36,38},{6,14},{38,32},{8,16},... | collective-permute-start | bytes 1880072 | tf_op jit(solution)/shard_map/ppermute | solution.py:27
  65.8 11.0 %collective-permute-start.23 = (f32[64,1152]{1,0:T(8,128)S(1)}, f32[64,1152]{1,0:T(8,128)S(1)}, u32[]{:S(2)}, u32[]{:S(2)}) collective-permute-start(f32[64,1152]{1,0:T(8,128)S(1)} %pad_maximum_fusion.7), channel_id=1, source_target_pairs={{0,192},{32,96},{2,194},{34,98},{4,196},{36,100},{6,198},{38,102},... | collective-permute-start | bytes 884744 | tf_op jit(solution)/shard_map/ppermute | solution.py:27
  69.6 9.5 %collective-permute-start.22 = (f32[64,1152]{1,0:T(8,128)S(1)}, f32[64,1152]{1,0:T(8,128)S(1)}, u32[]{:S(2)}, u32[]{:S(2)}) collective-permute-start(f32[64,1152]{1,0:T(8,128)S(1)} %get-tuple-element.80), channel_id=1, source_target_pairs={{0,193},{32,33},{2,195},{34,35},{4,197},{36,37},{6,199},{38,39},{8... | collective-permute-start | bytes 884744 | tf_op jit(solution)/shard_map/ppermute | solution.py:27
  73.3 14.6 %copy-start.1 = (f32[32,1152]{1,0:T(8,128)S(1)}, f32[32,1152]{1,0:T(8,128)}, u32[]{:S(2)}) copy-start(f32[32,1152]{1,0:T(8,128)} %param.4) | copy-start | bytes 442372
  73.3 7.3 %collective-permute-start.16 = (f32[40,1152]{1,0:T(8,128)S(1)}, f32[40,1152]{1,0:T(8,128)S(1)}, u32[]{:S(2)}, u32[]{:S(2)}) collective-permute-start(f32[40,1152]{1,0:T(8,128)S(1)} %get-tuple-element.70), channel_id=1, source_target_pairs={{0,4},{32,48},{2,6},{34,50},{4,0},{36,52},{6,2},{38,54},{8,12},{40... | collective-permute-start | bytes 552968 | tf_op jit(solution)/shard_map/ppermute | solution.py:27
  74.7 7.6 %collective-permute-start.17 = (f32[40,1152]{1,0:T(8,128)S(1)}, f32[40,1152]{1,0:T(8,128)S(1)}, u32[]{:S(2)}, u32[]{:S(2)}) collective-permute-start(f32[40,1152]{1,0:T(8,128)S(1)} %get-tuple-element.71), channel_id=1, source_target_pairs={{0,6},{32,56},{2,0},{34,58},{4,2},{36,60},{6,4},{38,62},{8,14},{40... | collective-permute-start | bytes 552968 | tf_op jit(solution)/shard_map/ppermute | solution.py:27
  76.9 6.7 %collective-permute-start.18 = (f32[40,1152]{1,0:T(8,128)S(1)}, f32[40,1152]{1,0:T(8,128)S(1)}, u32[]{:S(2)}, u32[]{:S(2)}) collective-permute-start(f32[40,1152]{1,0:T(8,128)S(1)} %get-tuple-element.72), channel_id=1, source_target_pairs={{0,2},{32,40},{2,4},{34,42},{4,6},{36,44},{6,0},{38,46},{8,10},{40... | collective-permute-start | bytes 552968 | tf_op jit(solution)/shard_map/ppermute | solution.py:27
  79.2 9.6 %collective-permute-start.24 = (f32[32,1152]{1,0:T(8,128)S(1)}, f32[32,1152]{1,0:T(8,128)S(1)}, u32[]{:S(2)}, u32[]{:S(2)}) collective-permute-start(f32[32,1152]{1,0:T(8,128)S(1)} %slice.106), channel_id=1, source_target_pairs={{0,32},{32,0},{2,34},{34,2},{4,36},{36,4},{6,38},{38,6},{8,40},{40... | collective-permute-start | bytes 442376 | tf_op jit(solution)/shard_map/ppermute | solution.py:27
  83.8 5.9 %collective-permute-start.20 = (f32[8,128]{1,0:T(8,128)S(1)}, f32[8,128]{1,0:T(8,128)S(1)}, u32[]{:S(2)}, u32[]{:S(2)}) collective-permute-start(f32[8,128]{1,0:T(8,128)S(1)} %pad_maximum_fusion.9), channel_id=1, source_target_pairs={{0,192},{32,96},{2,194},{34,98},{4,196},{36,100},{6,198},{38,102},... | collective-permute-start | bytes 12296 | tf_op jit(solution)/shard_map/ppermute | solution.py:27
  86.9 7.5 %collective-permute-start.19 = (f32[8,128]{1,0:T(8,128)S(1)}, f32[8,128]{1,0:T(8,128)S(1)}, u32[]{:S(2)}, u32[]{:S(2)}) collective-permute-start(f32[8,128]{1,0:T(8,128)S(1)} %pad_maximum_fusion.9), channel_id=1, source_target_pairs={{0,128},{32,160},{2,130},{34,162},{4,132},{36,164},{6,134},{38,166... | collective-permute-start | bytes 12296 | tf_op jit(solution)/shard_map/ppermute | solution.py:27
  89.8 4.6 %collective-permute-start.25 = (f32[8,128]{1,0:T(8,128)S(1)}, f32[8,128]{1,0:T(8,128)S(1)}, u32[]{:S(2)}, u32[]{:S(2)}) collective-permute-start(f32[8,128]{1,0:T(8,128)S(1)} %collective-permute-done.20), channel_id=1, source_target_pairs={{0,32},{32,0},{2,34},{34,2},{4,36},{36,4},{6,38},{38,6},{8,40},{40... | collective-permute-start | bytes 12296 | tf_op jit(solution)/shard_map/ppermute | solution.py:27

commit v5 on v4

--- a/solution.py
+++ b/solution.py
@@ -117,9 +117,12 @@
         image_part, ihi, ilo, text_part, loss, thi, tlo = refs[count + 4 :]
         unit_halves(texts, thi, tlo)
     else:
-        thi, tlo, text_in, loss_in, image_part, ihi, ilo, text_part, loss = refs[count:]
-    unit_halves(raws, ihi, ilo)
-    images = ihi[...], ilo[...]
+        thi, tlo, text_in, loss_in, high, low, image_part, ihi, ilo, text_part, loss = refs[count:]
+    before = ihi.shape[0] - image_part.shape[0]
+    if before:
+        ihi[:before, :], ilo[:before, :] = high[...], low[...]
+    unit_halves(raws, ihi.at[before:, :], ilo.at[before:, :])
+    images = ihi[before:, :], ilo[before:, :]
     texts = thi[...], tlo[...]
     logits = scale[0] * dot3(images, texts, NT) + bias[0]
     total, coef = pair_terms(logits, own)
@@ -134,34 +137,26 @@
         loss[...] = loss_in[...] + total
 
 
-def mid_kernel(scale, bias, h0, l0, h1, l1, loss_in, raw, ihi, ilo, part, chi, clo, thi, tlo, loss):
-    rows = h0.shape[0]
-    ihi[:rows, :], ilo[:rows, :] = h0[...], l0[...]
-    ihi[rows:, :], ilo[rows:, :] = h1[...], l1[...]
-    unit_halves((raw,), thi, tlo)
-    images = ihi[...], ilo[...]
-    logits = scale[0] * dot3(images, (thi[...], tlo[...]), NT) + bias[0]
-    total, coef = pair_terms(logits, 0)
-    loss[...] = loss_in[...] + total
-    coef = halves(coef * scale[0])
-    chi[...], clo[...] = coef
-    part[...] = dot3(coef, images, TN)
-
-
-def far_kernel(scale, bias, ihi, ilo, loss_in, raw, chi, clo, thi, tlo, loss):
+def far_kernel(final, scale, bias, ihi, ilo, loss_in, raw, chi, clo, thi, tlo, loss):
     unit_halves((raw,), thi, tlo)
     logits = scale[0] * dot3((ihi[...], ilo[...]), (thi[...], tlo[...]), NT) + bias[0]
     total, coef = pair_terms(logits, 0)
-    loss[...] = two_parts(loss_in[...] + total)
+    total = loss_in[...] + total
+    loss[...] = two_parts(total) if final else total
     chi[...], clo[...] = halves(coef * scale[0])
 
 
-def last_kernel(ihi, ilo, mhi, mlo, uhi, ulo, chi, clo, thi, tlo, in0, in1, other, pay, *outs):
-    coef = chi[...], clo[...]
-    count = thi.shape[0]
-    pay[:count, :] = dot3(coef, (ihi[...], ilo[...]), TN)
-    pay[count:, :] = other[...]
-    part = dot3((mhi[...], mlo[...]), (uhi[...], ulo[...]), NN) + dot3(coef, (thi[...], tlo[...]), NN)
+def text_kernel(ihi, ilo, chi, clo, *refs):
+    out = refs[-1]
+    count = chi.shape[1]
+    out[:count, :] = dot3((chi[...], clo[...]), (ihi[...], ilo[...]), TN)
+    if len(refs) > 1:
+        out[count:, :] = refs[0][...]
+
+
+def last_kernel(mhi, mlo, uhi, ulo, chi, clo, thi, tlo, in0, in1, *outs):
+    part = dot3((mhi[...], mlo[...]), (uhi[...], ulo[...]), NN)
+    part = part + dot3((chi[...], clo[...]), (thi[...], tlo[...]), NN)
     rows = in0.shape[0]
     outs[0][...] = in0[...] + part[:rows]
     for k, out in enumerate(outs[1:]):
@@ -185,7 +180,8 @@
     rows = sum(raw.shape[0] for raw in raws)
     cols = sum(text.shape[0] for text in texts) if start is None else texts[0].shape[0]
     operands = [scale, bias, *raws, *texts, *(start or ())]
-    shapes = [f32(rows, width), b16(rows, width), b16(rows, width), f32(cols, width), f32(8, 128)]
+    held = rows + (start[2].shape[0] if start else 0)
+    shapes = [f32(rows, width), b16(held, width), b16(held, width), f32(cols, width), f32(8, 128)]
     if start is None:
         shapes += [b16(cols, width)] * 2
     return pl.pallas_call(
@@ -198,47 +194,43 @@
     )(*operands)
 
 
-def mid_call(scale, bias, images, loss, raw):
+def far_call(scale, bias, images, loss, raw, final):
     count, width = raw.shape
-    rows = images[0].shape[0] + images[2].shape[0]
-    return pl.pallas_call(
-        mid_kernel,
-        out_shape=[b16(rows, width)] * 2
-        + [f32(count, width)]
-        + [b16(rows, count)] * 2
-        + [b16(count, width)] * 2
-        + [f32(8, 128)],
-        in_specs=[SMEM, SMEM] + [VMEM] * 6,
-        out_specs=[VMEM] * 8,
-        cost_estimate=cost(rows, count, width, 2),
-        compiler_params=GRANT,
-    )(scale, bias, *images, loss, raw)
-
-
-def far_call(scale, bias, ihi, ilo, loss, raw):
-    count, width = raw.shape
-    rows = ihi.shape[0]
-    return pl.pallas_call(
-        far_kernel,
+    rows = images[0].shape[0]
+    return pl.pallas_call(
+        functools.partial(far_kernel, final),
         out_shape=[b16(rows, count)] * 2 + [b16(count, width)] * 2 + [f32(8, 128)],
         in_specs=[SMEM, SMEM] + [VMEM] * 4,
         out_specs=[VMEM] * 5,
         cost_estimate=cost(rows, count, width, 1),
         compiler_params=GRANT,
-    )(scale, bias, ihi, ilo, loss, raw)
-
-
-def last_call(images, mid, far, starts, other):
+    )(scale, bias, *images, loss, raw)
+
+
+def text_call(images, coef, *more):
     rows, width = images[0].shape
-    count = far[0].shape[1]
+    count = coef[0].shape[1]
+    return pl.pallas_call(
+        text_kernel,
+        out_shape=f32(count + sum(block.shape[0] for block in more), width),
+        in_specs=[VMEM] * (4 + len(more)),
+        out_specs=VMEM,
+        cost_estimate=cost(rows, count, width, 1),
+        compiler_params=GRANT,
+    )(*images, *coef, *more)
+
+
+def last_call(mid, far, starts):
+    rows = mid[0].shape[0]
+    count, width = far[2].shape
     return pl.pallas_call(
         last_kernel,
-        out_shape=[f32(count + other.shape[0], width)] + [f32(rows // 4, width)] * 4,
-        in_specs=[VMEM] * 13,
-        out_specs=[VMEM] * 5,
-        cost_estimate=cost(rows, count, width, 5),
-        compiler_params=GRANT,
-    )(*images, *mid, *far, *starts, other)
+        out_shape=[f32(rows // 4, width)] * 4,
+        in_specs=[VMEM] * 10,
+        out_specs=[VMEM] * 4,
+        cost_estimate=cost(rows, count, width, 3),
+        compiler_params=GRANT,
+    )(*mid, *far, *starts)
 
 
 def sum_call(parts):
@@ -268,15 +260,20 @@
     images = [four] + [second(four, d) for d in STEPS]
     far = along_z(jnp.concatenate([one, two[:rows]]), 2)
     part0, hi0, lo0, *start, thi, tlo = group_call(logit_scale, logit_bias, images[:1], [text_emb, other, one, two])
-    part1, hi1, lo1, text_part, loss = group_call(logit_scale, logit_bias, images[1:], (thi, tlo), start)
+    part1, ihi, ilo, text_part, loss = group_call(logit_scale, logit_bias, images[1:], (thi, tlo), (*start, hi0, lo0))
     rest = swap(after(jnp.concatenate([one, two, far]), loss))
-    ihi, ilo, far_part, *mid, loss = mid_call(logit_scale, logit_bias, (hi0, lo0, hi1, lo1), loss, far)
-    *last, loss = far_call(logit_scale, logit_bias, ihi, ilo, loss, rest)
-    pay, *four = last_call((ihi, ilo), mid, last, (part0, part1), text_part[rows : 2 * rows])
+    images = ihi, ilo
+    *mid, loss = far_call(logit_scale, logit_bias, images, loss, far, False)
+    *last, loss = far_call(logit_scale, logit_bias, images, loss, rest, True)
     loss = add_from(loss, lambda z, y, x, core: (z ^ 1, y, x, core))
+    pay = text_call(images, last[:2], text_part[rows : 2 * rows])
+    four = last_call(mid, after(last, pay), (part0, part1))
+    got = swap(pay)
+    loss = after(loss, four)
+    loss = loss + swap(loss)
     note = jnp.concatenate([jnp.broadcast_to(loss[:, at : at + 1], (8, text_emb.shape[1] // 2)) for at in (0, 127)], 1)
-    got = swap(jnp.concatenate([pay, note]))
-    note = note + got[8 * rows :]
+    note = after(note, got)
+    far_part = text_call(images, after(mid[:2], four))
     back = along_z(far_part + got[4 * rows : 7 * rows], -2)
     one_part = text_part[2 * rows : 4 * rows] + got[: 2 * rows]
     two_part = text_part[4 * rows :] + got[2 * rows : 4 * rows]

time: 97.7 us -> 96.5 us (0.988)
  starting transfers between devices: 36.7 us -> 35.6 us
    ppermute x26 -> x27, starting transfers between devices: 36.7 us -> 35.6 us  [send(): return lax.ppermute(value, AXES, pairs(target))]
    ppermute x26 -> x27, waiting for transfers between devices: 35.7 us -> 36.1 us  [send(): return lax.ppermute(value, AXES, pairs(target))]
    pallas_call x3 -> x5, Pallas kernels: 7.7 us -> 7.36 us  [the longest x2 3.36 us: far_call(): pl.pallas_call(functools.partial(far_kernel, final), out_shape=[b16(rows,...]
  transfers between devices with their start and end apart: 26 -> 27, of which waited for: 15 -> 16; matrix products, arithmetic and copies ran while one was open for 5% -> 5% of each run, Pallas kernels for 13% -> 12%
where the time goes in v5:
time: 96.5 us; the launch traced here: 96.3 us
  waiting for transfers between devices  36.1 us (37%)
  starting transfers between devices  35.6 us (37%)
  Pallas kernels  14.3 us (15%)
  other arithmetic  4.73 us (5%)
  between operations  4.51 us (5%)
  local copies, waits for them, and re-layouts  1.07 us (1%)
    ppermute x27, waiting for transfers between devices, send(): return lax.ppermute(value, AXES, pairs(target))  36.1 us
    ppermute x27, starting transfers between devices, send(): return lax.ppermute(value, AXES, pairs(target))  35.6 us
    pallas_call x2, Pallas kernels, group_call(): pl.pallas_call(functools.partial(group_kernel, texts[0].shape[0] if start...  6.73 us
    pallas_call x2, Pallas kernels, far_call(): pl.pallas_call(functools.partial(far_kernel, final), out_shape=[b16(rows,...  3.36 us
    pallas_call x1, Pallas kernels, last_call(): pl.pallas_call(last_kernel, out_shape=[f32(rows // 4, width)] * 4, in_spe...  2.15 us
    reduce_sum x2, other arithmetic, normalize(): inverse = lax.rsqrt(jnp.sum(embed * embed, axis=1, keepdims=True) + 1e-06)  2.07 us
  transfers between devices with their start and end apart: 27, of which 16 were waited for; matrix products, arithmetic and copies ran while one was open for 5% of the time, Pallas kernels for 12%

profile of v5, /device:TPU:8, one launch (start us, length us, event | category | flops | bytes accessed | tf_op | source)
XLA Modules:
  0.0 96.3 jit_solution(11670689948719167119)
XLA Ops:
  0.6 3.1 %collective-permute-start.2 = (f32[32,1152]{1,0:T(8,128)}, f32[32,1152]{1,0:T(8,128)S(1)}, u32[]{:S(2)}, u32[]{:S(2)}) collective-permute-start(f32[32,1152]{1,0:T(8,128)} %param.4), channel_id=1, source_target_pairs={{0,4},{32,48},{2,6},{34,50},{4,0},{36,52},{6,2},{38,54},{8,12},{40... | collective-permute-start | bytes 442376 | tf_op jit(solution)/shard_map/ppermute | solution.py:27
  3.7 1.1 %collective-permute-start.1 = (f32[32,1152]{1,0:T(8,128)}, f32[32,1152]{1,0:T(8,128)S(1)}, u32[]{:S(2)}, u32[]{:S(2)}) collective-permute-start(f32[32,1152]{1,0:T(8,128)} %param.4), channel_id=1, source_target_pairs={{0,6},{32,56},{2,0},{34,58},{4,2},{36,60},{6,4},{38,62},{8,14},{40... | collective-permute-start | bytes 442376 | tf_op jit(solution)/shard_map/ppermute | solution.py:27
  4.9 0.9 collective-permute-start
  5.8 1.0 %multiply_reduce_fusion.1 = (f32[32]{0:T(128)S(1)}, f32[64,1152]{1,0:T(8,128)S(1)}) fusion(f32[32,1152]{1,0:T(8,128)} %refs_1_.1), kind=kLoop, calls=%fused_computation.18 | loop fusion | flops 73695 | bytes 295424 | tf_op jit(solution)/shard_map/reduce_sum | solution.py:248
  6.8 1.0 %multiply_reduce_fusion.3 = (f32[32]{0:T(128)S(1)}, f32[128,1152]{1,0:T(8,128)S(1)}) fusion(f32[32,1152]{1,0:T(8,128)} %param.4), kind=kLoop, calls=%fused_computation.21 | loop fusion | flops 73695 | bytes 295424 | tf_op jit(solution)/shard_map/reduce_sum | solution.py:248
  7.9 3.3 %collective-permute-start.8 = (f32[64,1152]{1,0:T(8,128)S(1)}, f32[64,1152]{1,0:T(8,128)S(1)}, u32[]{:S(2)}, u32[]{:S(2)}) collective-permute-start(f32[64,1152]{1,0:T(8,128)S(1)} %constant_dynamic-update-slice_fusion.4), channel_id=1, source_target_pairs={{0,64},{32,224},{2,66},{34,226},{4,68},{36,228},{6,70},{38,230},{8... | collective-permute-start | bytes 884744 | tf_op jit(solution)/shard_map/ppermute | solution.py:27
  11.2 1.9 %collective-permute-start.7 = (f32[64,1152]{1,0:T(8,128)S(1)}, f32[64,1152]{1,0:T(8,128)S(1)}, u32[]{:S(2)}, u32[]{:S(2)}) collective-permute-start(f32[64,1152]{1,0:T(8,128)S(1)} %constant_dynamic-update-slice_fusion.4), channel_id=1, source_target_pairs={{0,1},{32,225},{2,3},{34,227},{4,5},{36,229},{6,7},{38,231},{8,9},... | collective-permute-start | bytes 884744 | tf_op jit(solution)/shard_map/ppermute | solution.py:27
  13.2 2.4 %collective-permute-start.5 = (f32[128,1152]{1,0:T(8,128)S(1)}, f32[128,1152]{1,0:T(8,128)S(1)}, u32[]{:S(2)}, u32[]{:S(2)}) collective-permute-start(f32[128,1152]{1,0:T(8,128)S(1)} %constant_dynamic-update-slice_fusion.refs_0_), channel_id=1, source_target_pairs={{0,16},{32,36},{2,18},{34,38},{4,20},{36,32},{6,22},{38,34},{8,24}... | collective-permute-start | bytes 1769480 | tf_op jit(solution)/shard_map/ppermute | solution.py:27
  15.6 1.3 %collective-permute-start.4 = (f32[128,1152]{1,0:T(8,128)S(1)}, f32[128,1152]{1,0:T(8,128)S(1)}, u32[]{:S(2)}, u32[]{:S(2)}) collective-permute-start(f32[128,1152]{1,0:T(8,128)S(1)} %constant_dynamic-update-slice_fusion.refs_0_), channel_id=1, source_target_pairs={{0,24},{32,38},{2,26},{34,32},{4,28},{36,34},{6,30},{38,36},{8,0},... | collective-permute-start | bytes 1769480 | tf_op jit(solution)/shard_map/ppermute | solution.py:27
  17.0 0.7 collective-permute-start.3
  17.6 1.9 %collective-permute-done.8.refs_4_ = f32[64,1152]{1,0:T(8,128)S(1)} collective-permute-done((f32[64,1152]{1,0:T(8,128)S(1)}, f32[64,1152]{1,0:T(8,128)S(1)}, u32[]{:S(2)}, u32[]{:S(2)}) %collective-permute-start.8) | collective-permute-done | bytes 294944 | tf_op jit(solution)/shard_map/ppermute | solution.py:27
  19.6 5.3 %collective-permute-done.7.refs_3_ = f32[64,1152]{1,0:T(8,128)S(1)} collective-permute-done((f32[64,1152]{1,0:T(8,128)S(1)}, f32[64,1152]{1,0:T(8,128)S(1)}, u32[]{:S(2)}, u32[]{:S(2)}) %collective-permute-start.7) | collective-permute-done | bytes 294944 | tf_op jit(solution)/shard_map/ppermute | solution.py:27
  24.9 1.5 %collective-permute-start.9 = (f32[96,1152]{1,0:T(8,128)S(1)}, f32[96,1152]{1,0:T(8,128)S(1)}, u32[]{:S(2)}, u32[]{:S(2)}) collective-permute-start(f32[96,1152]{1,0:T(8,128)S(1)} %pad_maximum_fusion.5), channel_id=1, source_target_pairs={{0,64},{32,224},{2,66},{34,226},{4,68},{36,228},{6,70},{38,230},{8... | collective-permute-start | bytes 1327112 | tf_op jit(solution)/shard_map/ppermute | solution.py:27
  27.6 2.3 %shard_map.67 = (f32[128,1152]{1,0:T(8,128)S(1)}, bf16[128,1152]{1,0:T(8,128)(2,1)S(1)}, bf16[128,1152]{1,0:T(8,128)(2,1)S(1)}, f32[192,1152]{1,0:T(8,128)S(1)},...) custom-call(f32[1]{0:T(128)S(6)} %copy.11.scale, f32[1]{0:T(128)S(6)} %copy.12.bias, ...), custom_call_target="tpu_custom_call" | custom-call | flops 509607936 | bytes 589824 | tf_op jit(solution)/shard_map/pallas_call | solution.py:187
  29.9 1.1 %collective-permute-done.4.refs_1_ = f32[128,1152]{1,0:T(8,128)S(1)} collective-permute-done((f32[128,1152]{1,0:T(8,128)S(1)}, f32[128,1152]{1,0:T(8,128)S(1)}, u32[]{:S(2)}, u32[]{:S(2)}) %collective-permute-start.4) | collective-permute-done | bytes 589856 | tf_op jit(solution)/shard_map/ppermute | solution.py:27
  31.2 4.4 %shard_map.68 = (f32[384,1152]{1,0:T(8,128)S(1)}, bf16[512,1152]{1,0:T(8,128)(2,1)S(1)}, bf16[512,1152]{1,0:T(8,128)(2,1)S(1)}, f32[192,1152]{1,0:T(8,128)S(1)}, f32[8,128]{1,0:T(8,128)S(1)}) custom-call(f32[1]{0:T(128)S(6)} %copy.11.scale, f32[1]{0:T(128)S(6)} %copy.12.bias, f32[128,1152]{1,0:T(8,128)S(1)} %collective-permute-done.3.refs_0_, ...), custom_call_target="tpu_custom_call" | custom-call | flops 1528823808 | bytes 1769472 | tf_op jit(solution)/shard_map/pallas_call | solution.py:187
  35.6 3.8 %collective-permute-done.9.raw = f32[96,1152]{1,0:T(8,128)S(1)} collective-permute-done((f32[96,1152]{1,0:T(8,128)S(1)}, f32[96,1152]{1,0:T(8,128)S(1)}, u32[]{:S(2)}, u32[]{:S(2)}) %collective-permute-start.9) | collective-permute-done | bytes 442400 | tf_op jit(solution)/shard_map/ppermute | solution.py:27
  39.5 0.3 collective-permute-start.10
  39.8 1.5 %shard_map.69 = (bf16[512,96]{1,0:T(8,128)(2,1)S(1)}, bf16[512,96]{1,0:T(8,128)(2,1)S(1)}, bf16[96,1152]{1,0:T(8,128)(2,1)S(1)}, bf16[96,1152]{1,0:T(8,128)(2,1)S(1)}, f32[8,128]{1,0:T(8,128)S(1)}) custom-call(f32[1]{0:T(128)S(6)} %copy.11.scale, f32[1]{0:T(128)S(6)} %copy.12.bias, bf16[512,1152]{1,0:T(8,128)(2,1)S(1)} %get-tuple-element.49.ihi, ...), custom_call_target="tpu_custom_call" | custom-call | flops 339738624 | bytes 2359296 | tf_op jit(solution)/shard_map/pallas_call | solution.py:200
  41.3 1.1 %collective-permute-done.10.raw = f32[224,1152]{1,0:T(8,128)S(1)} collective-permute-done((f32[224,1152]{1,0:T(8,128)S(1)}, f32[224,1152]{1,0:T(8,128)S(1)}, u32[]{:S(2)}, u32[]{:S(2)}) %collective-permute-start.10) | collective-permute-done | bytes 1032224 | tf_op jit(solution)/shard_map/ppermute | solution.py:27
  42.4 1.8 %shard_map.70 = (bf16[512,224]{1,0:T(8,128)(2,1)S(1)}, bf16[512,224]{1,0:T(8,128)(2,1)S(1)}, bf16[224,1152]{1,0:T(8,128)(2,1)S(1)}, bf16[224,1152]{1,0:T(8,128)(2,1)S(1)}, f32[8,128]{1,0:T(8,128)S(1)}) custom-call(f32[1]{0:T(128)S(6)} %copy.11.scale, f32[1]{0:T(128)S(6)} %copy.12.bias, bf16[512,1152]{1,0:T(8,128)(2,1)S(1)} %get-tuple-element.49.ihi, ...), custom_call_target="tpu_custom_call" | custom-call | flops 792723456 | bytes 2359296 | tf_op jit(solution)/shard_map/pallas_call | solution.py:200
  44.2 1.1 %shard_map.71 = f32[256,1152]{1,0:T(8,128)S(1)} custom-call(bf16[512,1152]{1,0:T(8,128)(2,1)S(1)} %get-tuple-element.49.ihi, bf16[512,1152]{1,0:T(8,128)(2,1)S(1)} %get-tuple-element.50.ilo, bf16[512,224]{1,0:T(8,128)(2,1)S(1)} %get-tuple-element.63.chi, bf16[512,224]{1,0:T(8,128)(2,1)S(1)} %get-tuple-element.64.clo, f32[32,1152]{1,0:T(8,128)S(1)} %slice.67.refs_0_), custom_call_target="tpu_custom_call" | custom-call | flops 792723456 | bytes 2359296 | tf_op jit(solution)/shard_map/pallas_call | solution.py:213
  45.3 0.2 collective-permute-start.13
  45.5 2.1 %shard_map.72 = (f32[128,1152]{1,0:T(8,128)S(1)}, f32[128,1152]{1,0:T(8,128)S(1)}, f32[128,1152]{1,0:T(8,128)S(1)}, f32[128,1152]{1,0:T(8,128)S(1)}) custom-call(bf16[512,96]{1,0:T(8,128)(2,1)S(1)} %get-tuple-element.80.mhi.chi, bf16[512,96]{1,0:T(8,128)(2,1)S(1)} %get-tuple-element.81.mlo.clo, bf16[96,1152]{1,0:T(8,128)(2,1)S(1)} %get-tuple-element.54.uhi, ...), custom_call_target="tpu_custom_call" | custom-call | flops 2378170368 | bytes 2359296 | tf_op jit(solution)/shard_map/pallas_call | solution.py:226
  47.7 1.5 %collective-permute-done.11 = f32[8,128]{1,0:T(8,128)S(1)} collective-permute-done((f32[8,128]{1,0:T(8,128)S(1)}, f32[8,128]{1,0:T(8,128)S(1)}, u32[]{:S(2)}, u32[]{:S(2)}) %collective-permute-start.11) | collective-permute-done | bytes 4128 | tf_op jit(solution)/shard_map/ppermute | solution.py:27
  49.1 0.8 shard_map.74
  49.9 0.4 collective-permute-done.12
  50.6 2.5 %collective-permute-start.22 = (f32[96,1152]{1,0:T(8,128)S(1)}, f32[96,1152]{1,0:T(8,128)S(1)}, u32[]{:S(2)}, u32[]{:S(2)}) collective-permute-start(f32[96,1152]{1,0:T(8,128)S(1)} %slice_add_fusion), channel_id=1, source_target_pairs={{0,192},{32,96},{2,194},{34,98},{4,196},{36,100},{6,198},{38,102},... | collective-permute-start | bytes 1327112 | tf_op jit(solution)/shard_map/ppermute | solution.py:27
  53.5 2.4 %collective-permute-start.16 = (f32[136,1152]{1,0:T(8,128)S(1)}, f32[136,1152]{1,0:T(8,128)S(1)}, u32[]{:S(2)}, u32[]{:S(2)}) collective-permute-start(f32[136,1152]{1,0:T(8,128)S(1)} %get-tuple-element.97), channel_id=1, source_target_pairs={{0,16},{32,36},{2,18},{34,38},{4,20},{36,32},{6,22},{38,34},{8,24}... | collective-permute-start | bytes 1880072 | tf_op jit(solution)/shard_map/ppermute | solution.py:27
  55.9 1.3 %collective-permute-start.14 = (f32[136,1152]{1,0:T(8,128)S(1)}, f32[136,1152]{1,0:T(8,128)S(1)}, u32[]{:S(2)}, u32[]{:S(2)}) collective-permute-start(f32[136,1152]{1,0:T(8,128)S(1)} %get-tuple-element.98), channel_id=1, source_target_pairs={{0,24},{32,38},{2,26},{34,32},{4,28},{36,34},{6,30},{38,36},{8,0},... | collective-permute-start | bytes 1880072 | tf_op jit(solution)/shard_map/ppermute | solution.py:27
  57.2 0.7 collective-permute-start.15
  57.9 6.7 %collective-permute-done.22 = f32[96,1152]{1,0:T(8,128)S(1)} collective-permute-done((f32[96,1152]{1,0:T(8,128)S(1)}, f32[96,1152]{1,0:T(8,128)S(1)}, u32[]{:S(2)}, u32[]{:S(2)}) %collective-permute-start.22) | collective-permute-done | bytes 442400 | tf_op jit(solution)/shard_map/ppermute | solution.py:27
  64.8 3.7 %collective-permute-start.24 = (f32[64,1152]{1,0:T(8,128)S(1)}, f32[64,1152]{1,0:T(8,128)S(1)}, u32[]{:S(2)}, u32[]{:S(2)}) collective-permute-start(f32[64,1152]{1,0:T(8,128)S(1)} %pad_maximum_fusion.6), channel_id=1, source_target_pairs={{0,192},{32,96},{2,194},{34,98},{4,196},{36,100},{6,198},{38,102},... | collective-permute-start | bytes 884744 | tf_op jit(solution)/shard_map/ppermute | solution.py:27
  68.5 3.6 %collective-permute-done.14.in1 = f32[136,1152]{1,0:T(8,128)S(1)} collective-permute-done((f32[136,1152]{1,0:T(8,128)S(1)}, f32[136,1152]{1,0:T(8,128)S(1)}, u32[]{:S(2)}, u32[]{:S(2)}) %collective-permute-start.14) | collective-permute-done | bytes 626720 | tf_op jit(solution)/shard_map/ppermute | solution.py:27
  72.4 1.2 %collective-permute-start.17 = (f32[40,1152]{1,0:T(8,128)S(1)}, f32[40,1152]{1,0:T(8,128)S(1)}, u32[]{:S(2)}, u32[]{:S(2)}) collective-permute-start(f32[40,1152]{1,0:T(8,128)S(1)} %get-tuple-element.77), channel_id=1, source_target_pairs={{0,4},{32,48},{2,6},{34,50},{4,0},{36,52},{6,2},{38,54},{8,12},{40... | collective-permute-start | bytes 552968 | tf_op jit(solution)/shard_map/ppermute | solution.py:27
  73.7 2.1 %collective-permute-start.18 = (f32[40,1152]{1,0:T(8,128)S(1)}, f32[40,1152]{1,0:T(8,128)S(1)}, u32[]{:S(2)}, u32[]{:S(2)}) collective-permute-start(f32[40,1152]{1,0:T(8,128)S(1)} %get-tuple-element.78), channel_id=1, source_target_pairs={{0,6},{32,56},{2,0},{34,58},{4,2},{36,60},{6,4},{38,62},{8,14},{40... | collective-permute-start | bytes 552968 | tf_op jit(solution)/shard_map/ppermute | solution.py:27
  75.8 0.9 collective-permute-done.23
  76.7 0.8 collective-permute-start.25
  77.5 2.0 %collective-permute-done.17 = f32[40,1152]{1,0:T(8,128)S(1)} collective-permute-done((f32[40,1152]{1,0:T(8,128)S(1)}, f32[40,1152]{1,0:T(8,128)S(1)}, u32[]{:S(2)}, u32[]{:S(2)}) %collective-permute-start.17) | collective-permute-done | bytes 184352 | tf_op jit(solution)/shard_map/ppermute | solution.py:27
  79.6 1.7 %collective-permute-done.18 = f32[40,1152]{1,0:T(8,128)S(1)} collective-permute-done((f32[40,1152]{1,0:T(8,128)S(1)}, f32[40,1152]{1,0:T(8,128)S(1)}, u32[]{:S(2)}, u32[]{:S(2)}) %collective-permute-start.18) | collective-permute-done | bytes 184352 | tf_op jit(solution)/shard_map/ppermute | solution.py:27
  81.2 1.3 %collective-permute-done.19 = f32[40,1152]{1,0:T(8,128)S(1)} collective-permute-done((f32[40,1152]{1,0:T(8,128)S(1)}, f32[40,1152]{1,0:T(8,128)S(1)}, u32[]{:S(2)}, u32[]{:S(2)}) %collective-permute-start.19) | collective-permute-done | bytes 184352 | tf_op jit(solution)/shard_map/ppermute | solution.py:27
  82.7 3.1 %collective-permute-start.21 = (f32[8,128]{1,0:T(8,128)S(1)}, f32[8,128]{1,0:T(8,128)S(1)}, u32[]{:S(2)}, u32[]{:S(2)}) collective-permute-start(f32[8,128]{1,0:T(8,128)S(1)} %pad_maximum_fusion.8), channel_id=1, source_target_pairs={{0,192},{32,96},{2,194},{34,98},{4,196},{36,100},{6,198},{38,102},... | collective-permute-start | bytes 12296 | tf_op jit(solution)/shard_map/ppermute | solution.py:27
  85.8 1.0 %collective-permute-start.20 = (f32[8,128]{1,0:T(8,128)S(1)}, f32[8,128]{1,0:T(8,128)S(1)}, u32[]{:S(2)}, u32[]{:S(2)}) collective-permute-start(f32[8,128]{1,0:T(8,128)S(1)} %pad_maximum_fusion.8), channel_id=1, source_target_pairs={{0,128},{32,160},{2,130},{34,162},{4,132},{36,164},{6,134},{38,166... | collective-permute-start | bytes 12296 | tf_op jit(solution)/shard_map/ppermute | solution.py:27
  86.8 0.2 multiply_reduce_fusion.2
  87.0 0.8 subtract_multiply_fusion.1
  87.9 0.8 subtract_multiply_fusion
  88.7 4.6 %collective-permute-done.20 = f32[8,128]{1,0:T(8,128)S(1)} collective-permute-done((f32[8,128]{1,0:T(8,128)S(1)}, f32[8,128]{1,0:T(8,128)S(1)}, u32[]{:S(2)}, u32[]{:S(2)}) %collective-permute-start.20) | collective-permute-done | bytes 4128 | tf_op jit(solution)/shard_map/ppermute | solution.py:27
  93.4 0.6 fusion.3
  (52 shorter events, 2.0 us)
Async XLA Ops:
  0.6 12.6 %collective-permute-start.2 = (f32[32,1152]{1,0:T(8,128)}, f32[32,1152]{1,0:T(8,128)S(1)}, u32[]{:S(2)}, u32[]{:S(2)}) collective-permute-start(f32[32,1152]{1,0:T(8,128)} %param.4), channel_id=1, source_target_pairs={{0,4},{32,48},{2,6},{34,50},{4,0},{36,52},{6,2},{38,54},{8,12},{40... | collective-permute-start | bytes 442376 | tf_op jit(solution)/shard_map/ppermute | solution.py:27
  3.7 9.4 %collective-permute-start.1 = (f32[32,1152]{1,0:T(8,128)}, f32[32,1152]{1,0:T(8,128)S(1)}, u32[]{:S(2)}, u32[]{:S(2)}) collective-permute-start(f32[32,1152]{1,0:T(8,128)} %param.4), channel_id=1, source_target_pairs={{0,6},{32,56},{2,0},{34,58},{4,2},{36,60},{6,4},{38,62},{8,14},{40... | collective-permute-start | bytes 442376 | tf_op jit(solution)/shard_map/ppermute | solution.py:27
  4.9 8.3 %collective-permute-start = (f32[32,1152]{1,0:T(8,128)}, f32[32,1152]{1,0:T(8,128)S(1)}, u32[]{:S(2)}, u32[]{:S(2)}) collective-permute-start(f32[32,1152]{1,0:T(8,128)} %param.4), channel_id=1, source_target_pairs={{0,2},{32,40},{2,4},{34,42},{4,6},{36,44},{6,0},{38,46},{8,10},{40... | collective-permute-start | bytes 442376 | tf_op jit(solution)/shard_map/ppermute | solution.py:27
  5.8 2.1 %collective-permute-start.6 = (f32[32,1152]{1,0:T(8,128)}, f32[32,1152]{1,0:T(8,128)S(1)}, u32[]{:S(2)}, u32[]{:S(2)}) collective-permute-start(f32[32,1152]{1,0:T(8,128)} %refs_1_.1), channel_id=1, source_target_pairs={{0,32},{32,0},{2,34},{34,2},{4,36},{36,4},{6,38},{38,6},{8,40},{40... | collective-permute-start | bytes 442376 | tf_op jit(solution)/shard_map/ppermute | solution.py:27
  7.8 19.8 %copy-start = (f32[32,1152]{1,0:T(8,128)S(1)}, f32[32,1152]{1,0:T(8,128)}, u32[]{:S(2)}) copy-start(f32[32,1152]{1,0:T(8,128)} %refs_1_.1) | copy-start | bytes 442372
  7.9 11.7 %collective-permute-start.8 = (f32[64,1152]{1,0:T(8,128)S(1)}, f32[64,1152]{1,0:T(8,128)S(1)}, u32[]{:S(2)}, u32[]{:S(2)}) collective-permute-start(f32[64,1152]{1,0:T(8,128)S(1)} %constant_dynamic-update-slice_fusion.4), channel_id=1, source_target_pairs={{0,64},{32,224},{2,66},{34,226},{4,68},{36,228},{6,70},{38,230},{8... | collective-permute-start | bytes 884744 | tf_op jit(solution)/shard_map/ppermute | solution.py:27
  11.2 13.6 %collective-permute-start.7 = (f32[64,1152]{1,0:T(8,128)S(1)}, f32[64,1152]{1,0:T(8,128)S(1)}, u32[]{:S(2)}, u32[]{:S(2)}) collective-permute-start(f32[64,1152]{1,0:T(8,128)S(1)} %constant_dynamic-update-slice_fusion.4), channel_id=1, source_target_pairs={{0,1},{32,225},{2,3},{34,227},{4,5},{36,229},{6,7},{38,231},{8,9},... | collective-permute-start | bytes 884744 | tf_op jit(solution)/shard_map/ppermute | solution.py:27
  13.2 16.7 %collective-permute-start.5 = (f32[128,1152]{1,0:T(8,128)S(1)}, f32[128,1152]{1,0:T(8,128)S(1)}, u32[]{:S(2)}, u32[]{:S(2)}) collective-permute-start(f32[128,1152]{1,0:T(8,128)S(1)} %constant_dynamic-update-slice_fusion.refs_0_), channel_id=1, source_target_pairs={{0,16},{32,36},{2,18},{34,38},{4,20},{36,32},{6,22},{38,34},{8,24}... | collective-permute-start | bytes 1769480 | tf_op jit(solution)/shard_map/ppermute | solution.py:27
  15.6 15.4 %collective-permute-start.4 = (f32[128,1152]{1,0:T(8,128)S(1)}, f32[128,1152]{1,0:T(8,128)S(1)}, u32[]{:S(2)}, u32[]{:S(2)}) collective-permute-start(f32[128,1152]{1,0:T(8,128)S(1)} %constant_dynamic-update-slice_fusion.refs_0_), channel_id=1, source_target_pairs={{0,24},{32,38},{2,26},{34,32},{4,28},{36,34},{6,30},{38,36},{8,0},... | collective-permute-start | bytes 1769480 | tf_op jit(solution)/shard_map/ppermute | solution.py:27
  17.0 14.2 %collective-permute-start.3 = (f32[128,1152]{1,0:T(8,128)S(1)}, f32[128,1152]{1,0:T(8,128)S(1)}, u32[]{:S(2)}, u32[]{:S(2)}) collective-permute-start(f32[128,1152]{1,0:T(8,128)S(1)} %constant_dynamic-update-slice_fusion.refs_0_), channel_id=1, source_target_pairs={{0,8},{32,34},{2,10},{34,36},{4,12},{36,38},{6,14},{38,32},{8,16},... | collective-permute-start | bytes 1769480 | tf_op jit(solution)/shard_map/ppermute | solution.py:27
  24.9 14.5 %collective-permute-start.9 = (f32[96,1152]{1,0:T(8,128)S(1)}, f32[96,1152]{1,0:T(8,128)S(1)}, u32[]{:S(2)}, u32[]{:S(2)}) collective-permute-start(f32[96,1152]{1,0:T(8,128)S(1)} %pad_maximum_fusion.5), channel_id=1, source_target_pairs={{0,64},{32,224},{2,66},{34,226},{4,68},{36,228},{6,70},{38,230},{8... | collective-permute-start | bytes 1327112 | tf_op jit(solution)/shard_map/ppermute | solution.py:27
  39.5 2.9 %collective-permute-start.10 = (f32[224,1152]{1,0:T(8,128)S(1)}, f32[224,1152]{1,0:T(8,128)S(1)}, u32[]{:S(2)}, u32[]{:S(2)}) collective-permute-start(f32[224,1152]{1,0:T(8,128)S(1)} %pad_maximum_fusion.4), channel_id=1, source_target_pairs={{0,32},{32,0},{2,34},{34,2},{4,36},{36,4},{6,38},{38,6},{8,40},{40... | collective-permute-start | bytes 3096584 | tf_op jit(solution)/shard_map/ppermute | solution.py:27
  45.3 5.2 %collective-permute-start.13 = (f32[256,1152]{1,0:T(8,128)S(1)}, f32[256,1152]{1,0:T(8,128)S(1)}, u32[]{:S(2)}, u32[]{:S(2)}) collective-permute-start(f32[256,1152]{1,0:T(8,128)S(1)} %shard_map.71), channel_id=1, source_target_pairs={{0,32},{32,0},{2,34},{34,2},{4,36},{36,4},{6,38},{38,6},{8,40},{40... | collective-permute-start | bytes 3538952 | tf_op jit(solution)/shard_map/ppermute | solution.py:27
  45.5 3.6 %collective-permute-start.11 = (f32[8,128]{1,0:T(8,128)S(1)}, f32[8,128]{1,0:T(8,128)S(1)}, u32[]{:S(2)}, u32[]{:S(2)}) collective-permute-start(f32[8,128]{1,0:T(8,128)S(1)} %get-tuple-element.70), channel_id=1, source_target_pairs={{0,1},{32,33},{2,3},{34,35},{4,5},{36,37},{6,7},{38,39},{8,9},{40,... | collective-permute-start | bytes 12296 | tf_op jit(solution)/shard_map/ppermute | solution.py:27
  49.1 1.2 %collective-permute-start.12 = (f32[8,128]{1,0:T(8,128)S(1)}, f32[8,128]{1,0:T(8,128)S(1)}, u32[]{:S(2)}, u32[]{:S(2)}) collective-permute-start(f32[8,128]{1,0:T(8,128)S(1)} %add.71), channel_id=1, source_target_pairs={{0,32},{32,0},{2,34},{34,2},{4,36},{36,4},{6,38},{38,6},{8,40},{40... | collective-permute-start | bytes 12296 | tf_op jit(solution)/shard_map/ppermute | solution.py:27
  50.6 14.1 %collective-permute-start.22 = (f32[96,1152]{1,0:T(8,128)S(1)}, f32[96,1152]{1,0:T(8,128)S(1)}, u32[]{:S(2)}, u32[]{:S(2)}) collective-permute-start(f32[96,1152]{1,0:T(8,128)S(1)} %slice_add_fusion), channel_id=1, source_target_pairs={{0,192},{32,96},{2,194},{34,98},{4,196},{36,100},{6,198},{38,102},... | collective-permute-start | bytes 1327112 | tf_op jit(solution)/shard_map/ppermute | solution.py:27
  53.5 15.0 %collective-permute-start.16 = (f32[136,1152]{1,0:T(8,128)S(1)}, f32[136,1152]{1,0:T(8,128)S(1)}, u32[]{:S(2)}, u32[]{:S(2)}) collective-permute-start(f32[136,1152]{1,0:T(8,128)S(1)} %get-tuple-element.97), channel_id=1, source_target_pairs={{0,16},{32,36},{2,18},{34,38},{4,20},{36,32},{6,22},{38,34},{8,24}... | collective-permute-start | bytes 1880072 | tf_op jit(solution)/shard_map/ppermute | solution.py:27
  55.9 16.2 %collective-permute-start.14 = (f32[136,1152]{1,0:T(8,128)S(1)}, f32[136,1152]{1,0:T(8,128)S(1)}, u32[]{:S(2)}, u32[]{:S(2)}) collective-permute-start(f32[136,1152]{1,0:T(8,128)S(1)} %get-tuple-element.98), channel_id=1, source_target_pairs={{0,24},{32,38},{2,26},{34,32},{4,28},{36,34},{6,30},{38,36},{8,0},... | collective-permute-start | bytes 1880072 | tf_op jit(solution)/shard_map/ppermute | solution.py:27
  57.2 15.0 %collective-permute-start.15 = (f32[136,1152]{1,0:T(8,128)S(1)}, f32[136,1152]{1,0:T(8,128)S(1)}, u32[]{:S(2)}, u32[]{:S(2)}) collective-permute-start(f32[136,1152]{1,0:T(8,128)S(1)} %get-tuple-element.99), channel_id=1, source_target_pairs={{0,8},{32,34},{2,10},{34,36},{4,12},{36,38},{6,14},{38,32},{8,16},... | collective-permute-start | bytes 1880072 | tf_op jit(solution)/shard_map/ppermute | solution.py:27
  64.8 11.0 %collective-permute-start.24 = (f32[64,1152]{1,0:T(8,128)S(1)}, f32[64,1152]{1,0:T(8,128)S(1)}, u32[]{:S(2)}, u32[]{:S(2)}) collective-permute-start(f32[64,1152]{1,0:T(8,128)S(1)} %pad_maximum_fusion.6), channel_id=1, source_target_pairs={{0,192},{32,96},{2,194},{34,98},{4,196},{36,100},{6,198},{38,102},... | collective-permute-start | bytes 884744 | tf_op jit(solution)/shard_map/ppermute | solution.py:27
  68.5 8.2 %collective-permute-start.23 = (f32[64,1152]{1,0:T(8,128)S(1)}, f32[64,1152]{1,0:T(8,128)S(1)}, u32[]{:S(2)}, u32[]{:S(2)}) collective-permute-start(f32[64,1152]{1,0:T(8,128)S(1)} %get-tuple-element.88), channel_id=1, source_target_pairs={{0,193},{32,33},{2,195},{34,35},{4,197},{36,37},{6,199},{38,39},{8... | collective-permute-start | bytes 884744 | tf_op jit(solution)/shard_map/ppermute | solution.py:27
  72.4 14.3 %copy-start.1 = (f32[32,1152]{1,0:T(8,128)S(1)}, f32[32,1152]{1,0:T(8,128)}, u32[]{:S(2)}) copy-start(f32[32,1152]{1,0:T(8,128)} %param.4) | copy-start | bytes 442372
  72.4 7.1 %collective-permute-start.17 = (f32[40,1152]{1,0:T(8,128)S(1)}, f32[40,1152]{1,0:T(8,128)S(1)}, u32[]{:S(2)}, u32[]{:S(2)}) collective-permute-start(f32[40,1152]{1,0:T(8,128)S(1)} %get-tuple-element.77), channel_id=1, source_target_pairs={{0,4},{32,48},{2,6},{34,50},{4,0},{36,52},{6,2},{38,54},{8,12},{40... | collective-permute-start | bytes 552968 | tf_op jit(solution)/shard_map/ppermute | solution.py:27
  73.7 7.6 %collective-permute-start.18 = (f32[40,1152]{1,0:T(8,128)S(1)}, f32[40,1152]{1,0:T(8,128)S(1)}, u32[]{:S(2)}, u32[]{:S(2)}) collective-permute-start(f32[40,1152]{1,0:T(8,128)S(1)} %get-tuple-element.78), channel_id=1, source_target_pairs={{0,6},{32,56},{2,0},{34,58},{4,2},{36,60},{6,4},{38,62},{8,14},{40... | collective-permute-start | bytes 552968 | tf_op jit(solution)/shard_map/ppermute | solution.py:27
  75.8 6.7 %collective-permute-start.19 = (f32[40,1152]{1,0:T(8,128)S(1)}, f32[40,1152]{1,0:T(8,128)S(1)}, u32[]{:S(2)}, u32[]{:S(2)}) collective-permute-start(f32[40,1152]{1,0:T(8,128)S(1)} %get-tuple-element.79), channel_id=1, source_target_pairs={{0,2},{32,40},{2,4},{34,42},{4,6},{36,44},{6,0},{38,46},{8,10},{40... | collective-permute-start | bytes 552968 | tf_op jit(solution)/shard_map/ppermute | solution.py:27
  76.7 11.0 %collective-permute-start.25 = (f32[32,1152]{1,0:T(8,128)S(1)}, f32[32,1152]{1,0:T(8,128)S(1)}, u32[]{:S(2)}, u32[]{:S(2)}) collective-permute-start(f32[32,1152]{1,0:T(8,128)S(1)} %slice.101), channel_id=1, source_target_pairs={{0,32},{32,0},{2,34},{34,2},{4,36},{36,4},{6,38},{38,6},{8,40},{40... | collective-permute-start | bytes 442376 | tf_op jit(solution)/shard_map/ppermute | solution.py:27
  82.7 5.9 %collective-permute-start.21 = (f32[8,128]{1,0:T(8,128)S(1)}, f32[8,128]{1,0:T(8,128)S(1)}, u32[]{:S(2)}, u32[]{:S(2)}) collective-permute-start(f32[8,128]{1,0:T(8,128)S(1)} %pad_maximum_fusion.8), channel_id=1, source_target_pairs={{0,192},{32,96},{2,194},{34,98},{4,196},{36,100},{6,198},{38,102},... | collective-permute-start | bytes 12296 | tf_op jit(solution)/shard_map/ppermute | solution.py:27
  85.8 7.5 %collective-permute-start.20 = (f32[8,128]{1,0:T(8,128)S(1)}, f32[8,128]{1,0:T(8,128)S(1)}, u32[]{:S(2)}, u32[]{:S(2)}) collective-permute-start(f32[8,128]{1,0:T(8,128)S(1)} %pad_maximum_fusion.8), channel_id=1, source_target_pairs={{0,128},{32,160},{2,130},{34,162},{4,132},{36,164},{6,134},{38,166... | collective-permute-start | bytes 12296 | tf_op jit(solution)/shard_map/ppermute | solution.py:27
  88.7 4.6 %collective-permute-start.26 = (f32[8,128]{1,0:T(8,128)S(1)}, f32[8,128]{1,0:T(8,128)S(1)}, u32[]{:S(2)}, u32[]{:S(2)}) collective-permute-start(f32[8,128]{1,0:T(8,128)S(1)} %collective-permute-done.21), channel_id=1, source_target_pairs={{0,32},{32,0},{2,34},{34,2},{4,36},{36,4},{6,38},{38,6},{8,40},{40... | collective-permute-start | bytes 12296 | tf_op jit(solution)/shard_map/ppermute | solution.py:27

commit v6 on v5

--- a/solution.py
+++ b/solution.py
@@ -265,7 +265,7 @@
     images = ihi, ilo
     *mid, loss = far_call(logit_scale, logit_bias, images, loss, far, False)
     *last, loss = far_call(logit_scale, logit_bias, images, loss, rest, True)
-    loss = add_from(loss, lambda z, y, x, core: (z ^ 1, y, x, core))
+    loss = add_from(loss, lambda z, y, x, core: (z ^ 4, y, x, core))
     pay = text_call(images, last[:2], text_part[rows : 2 * rows])
     four = last_call(mid, after(last, pay), (part0, part1))
     got = swap(pay)
@@ -289,8 +289,8 @@
     text_unit_grad = own_part + back[:rows] + swap(back[rows:])
     image_unit_grad = total[:rows]
     loss = jnp.concatenate([total[rows:, :64], total[rows:, -64:]], 1)
-    beside = along_z(loss, -2)
-    loss = loss + send(loss, lambda z, y, x, core: (z + 4, y, x, core))
+    beside = along_z(loss, -1)
+    loss = loss + along_z(loss, -2)
 
     image_unit, image_inv = normalize(image_emb)
     text_unit, text_inv = normalize(text_emb)

time: 96.5 us -> 97.7 us (1.012); the launches traced: 96.3 us -> 96.1 us
  waiting for transfers between devices: 36.1 us -> 32.5 us
  starting transfers between devices: 35.6 us -> 39.1 us
    ppermute x27, waiting for transfers between devices: 36.1 us -> 32.5 us  [send(): return lax.ppermute(value, AXES, pairs(target))]
    ppermute x27, starting transfers between devices: 35.6 us -> 39.1 us  [send(): return lax.ppermute(value, AXES, pairs(target))]
where the time goes in v6:
time: 97.7 us; the launch traced here: 96.1 us
  starting transfers between devices  39.1 us (40%)
  waiting for transfers between devices  32.5 us (33%)
  Pallas kernels  14.3 us (15%)
  other arithmetic  4.73 us (5%)
  between operations  4.52 us (5%)
  local copies, waits for them, and re-layouts  1.07 us (1%)
    ppermute x27, starting transfers between devices, send(): return lax.ppermute(value, AXES, pairs(target))  39.1 us
    ppermute x27, waiting for transfers between devices, send(): return lax.ppermute(value, AXES, pairs(target))  32.5 us
    pallas_call x2, Pallas kernels, group_call(): pl.pallas_call(functools.partial(group_kernel, texts[0].shape[0] if start...  6.73 us
    pallas_call x2, Pallas kernels, far_call(): pl.pallas_call(functools.partial(far_kernel, final), out_shape=[b16(rows,...  3.36 us
    pallas_call x1, Pallas kernels, last_call(): pl.pallas_call(last_kernel, out_shape=[f32(rows // 4, width)] * 4, in_spe...  2.14 us
    reduce_sum x2, other arithmetic, normalize(): inverse = lax.rsqrt(jnp.sum(embed * embed, axis=1, keepdims=True) + 1e-06)  2.07 us
  transfers between devices with their start and end apart: 27, of which 16 were waited for; matrix products, arithmetic and copies ran while one was open for 5% of the time, Pallas kernels for 12%

profile of v6, /device:TPU:8, one launch (start us, length us, event | category | flops | bytes accessed | tf_op | source)
XLA Modules:
  0.0 96.1 jit_solution(3558786915209008506)
XLA Ops:
  0.6 3.1 %collective-permute-start.2 = (f32[32,1152]{1,0:T(8,128)}, f32[32,1152]{1,0:T(8,128)S(1)}, u32[]{:S(2)}, u32[]{:S(2)}) collective-permute-start(f32[32,1152]{1,0:T(8,128)} %param.4), channel_id=1, source_target_pairs={{0,4},{32,48},{2,6},{34,50},{4,0},{36,52},{6,2},{38,54},{8,12},{40... | collective-permute-start | bytes 442376 | tf_op jit(solution)/shard_map/ppermute | solution.py:27
  3.7 1.1 %collective-permute-start.1 = (f32[32,1152]{1,0:T(8,128)}, f32[32,1152]{1,0:T(8,128)S(1)}, u32[]{:S(2)}, u32[]{:S(2)}) collective-permute-start(f32[32,1152]{1,0:T(8,128)} %param.4), channel_id=1, source_target_pairs={{0,6},{32,56},{2,0},{34,58},{4,2},{36,60},{6,4},{38,62},{8,14},{40... | collective-permute-start | bytes 442376 | tf_op jit(solution)/shard_map/ppermute | solution.py:27
  4.9 0.9 collective-permute-start
  5.8 1.0 %multiply_reduce_fusion.1 = (f32[32]{0:T(128)S(1)}, f32[64,1152]{1,0:T(8,128)S(1)}) fusion(f32[32,1152]{1,0:T(8,128)} %refs_1_.1), kind=kLoop, calls=%fused_computation.18 | loop fusion | flops 73695 | bytes 295424 | tf_op jit(solution)/shard_map/reduce_sum | solution.py:248
  6.8 1.0 %multiply_reduce_fusion.3 = (f32[32]{0:T(128)S(1)}, f32[128,1152]{1,0:T(8,128)S(1)}) fusion(f32[32,1152]{1,0:T(8,128)} %param.4), kind=kLoop, calls=%fused_computation.21 | loop fusion | flops 73695 | bytes 295424 | tf_op jit(solution)/shard_map/reduce_sum | solution.py:248
  7.9 3.3 %collective-permute-start.8 = (f32[64,1152]{1,0:T(8,128)S(1)}, f32[64,1152]{1,0:T(8,128)S(1)}, u32[]{:S(2)}, u32[]{:S(2)}) collective-permute-start(f32[64,1152]{1,0:T(8,128)S(1)} %constant_dynamic-update-slice_fusion.4), channel_id=1, source_target_pairs={{0,64},{32,224},{2,66},{34,226},{4,68},{36,228},{6,70},{38,230},{8... | collective-permute-start | bytes 884744 | tf_op jit(solution)/shard_map/ppermute | solution.py:27
  11.2 1.9 %collective-permute-start.7 = (f32[64,1152]{1,0:T(8,128)S(1)}, f32[64,1152]{1,0:T(8,128)S(1)}, u32[]{:S(2)}, u32[]{:S(2)}) collective-permute-start(f32[64,1152]{1,0:T(8,128)S(1)} %constant_dynamic-update-slice_fusion.4), channel_id=1, source_target_pairs={{0,1},{32,225},{2,3},{34,227},{4,5},{36,229},{6,7},{38,231},{8,9},... | collective-permute-start | bytes 884744 | tf_op jit(solution)/shard_map/ppermute | solution.py:27
  13.2 2.4 %collective-permute-start.5 = (f32[128,1152]{1,0:T(8,128)S(1)}, f32[128,1152]{1,0:T(8,128)S(1)}, u32[]{:S(2)}, u32[]{:S(2)}) collective-permute-start(f32[128,1152]{1,0:T(8,128)S(1)} %constant_dynamic-update-slice_fusion.refs_0_), channel_id=1, source_target_pairs={{0,16},{32,36},{2,18},{34,38},{4,20},{36,32},{6,22},{38,34},{8,24}... | collective-permute-start | bytes 1769480 | tf_op jit(solution)/shard_map/ppermute | solution.py:27
  15.6 1.3 %collective-permute-start.4 = (f32[128,1152]{1,0:T(8,128)S(1)}, f32[128,1152]{1,0:T(8,128)S(1)}, u32[]{:S(2)}, u32[]{:S(2)}) collective-permute-start(f32[128,1152]{1,0:T(8,128)S(1)} %constant_dynamic-update-slice_fusion.refs_0_), channel_id=1, source_target_pairs={{0,24},{32,38},{2,26},{34,32},{4,28},{36,34},{6,30},{38,36},{8,0},... | collective-permute-start | bytes 1769480 | tf_op jit(solution)/shard_map/ppermute | solution.py:27
  17.0 0.7 collective-permute-start.3
  17.6 1.9 %collective-permute-done.8.refs_4_ = f32[64,1152]{1,0:T(8,128)S(1)} collective-permute-done((f32[64,1152]{1,0:T(8,128)S(1)}, f32[64,1152]{1,0:T(8,128)S(1)}, u32[]{:S(2)}, u32[]{:S(2)}) %collective-permute-start.8) | collective-permute-done | bytes 294944 | tf_op jit(solution)/shard_map/ppermute | solution.py:27
  19.6 5.3 %collective-permute-done.7.refs_3_ = f32[64,1152]{1,0:T(8,128)S(1)} collective-permute-done((f32[64,1152]{1,0:T(8,128)S(1)}, f32[64,1152]{1,0:T(8,128)S(1)}, u32[]{:S(2)}, u32[]{:S(2)}) %collective-permute-start.7) | collective-permute-done | bytes 294944 | tf_op jit(solution)/shard_map/ppermute | solution.py:27
  24.9 1.5 %collective-permute-start.9 = (f32[96,1152]{1,0:T(8,128)S(1)}, f32[96,1152]{1,0:T(8,128)S(1)}, u32[]{:S(2)}, u32[]{:S(2)}) collective-permute-start(f32[96,1152]{1,0:T(8,128)S(1)} %pad_maximum_fusion.5), channel_id=1, source_target_pairs={{0,64},{32,224},{2,66},{34,226},{4,68},{36,228},{6,70},{38,230},{8... | collective-permute-start | bytes 1327112 | tf_op jit(solution)/shard_map/ppermute | solution.py:27
  27.6 2.3 %shard_map.67 = (f32[128,1152]{1,0:T(8,128)S(1)}, bf16[128,1152]{1,0:T(8,128)(2,1)S(1)}, bf16[128,1152]{1,0:T(8,128)(2,1)S(1)}, f32[192,1152]{1,0:T(8,128)S(1)},...) custom-call(f32[1]{0:T(128)S(6)} %copy.11.scale, f32[1]{0:T(128)S(6)} %copy.12.bias, ...), custom_call_target="tpu_custom_call" | custom-call | flops 509607936 | bytes 589824 | tf_op jit(solution)/shard_map/pallas_call | solution.py:187
  29.9 1.1 %collective-permute-done.4.refs_1_ = f32[128,1152]{1,0:T(8,128)S(1)} collective-permute-done((f32[128,1152]{1,0:T(8,128)S(1)}, f32[128,1152]{1,0:T(8,128)S(1)}, u32[]{:S(2)}, u32[]{:S(2)}) %collective-permute-start.4) | collective-permute-done | bytes 589856 | tf_op jit(solution)/shard_map/ppermute | solution.py:27
  31.2 4.4 %shard_map.68 = (f32[384,1152]{1,0:T(8,128)S(1)}, bf16[512,1152]{1,0:T(8,128)(2,1)S(1)}, bf16[512,1152]{1,0:T(8,128)(2,1)S(1)}, f32[192,1152]{1,0:T(8,128)S(1)}, f32[8,128]{1,0:T(8,128)S(1)}) custom-call(f32[1]{0:T(128)S(6)} %copy.11.scale, f32[1]{0:T(128)S(6)} %copy.12.bias, f32[128,1152]{1,0:T(8,128)S(1)} %collective-permute-done.3.refs_0_, ...), custom_call_target="tpu_custom_call" | custom-call | flops 1528823808 | bytes 1769472 | tf_op jit(solution)/shard_map/pallas_call | solution.py:187
  35.6 3.8 %collective-permute-done.9.raw = f32[96,1152]{1,0:T(8,128)S(1)} collective-permute-done((f32[96,1152]{1,0:T(8,128)S(1)}, f32[96,1152]{1,0:T(8,128)S(1)}, u32[]{:S(2)}, u32[]{:S(2)}) %collective-permute-start.9) | collective-permute-done | bytes 442400 | tf_op jit(solution)/shard_map/ppermute | solution.py:27
  39.5 0.3 collective-permute-start.10
  39.8 1.5 %shard_map.69 = (bf16[512,96]{1,0:T(8,128)(2,1)S(1)}, bf16[512,96]{1,0:T(8,128)(2,1)S(1)}, bf16[96,1152]{1,0:T(8,128)(2,1)S(1)}, bf16[96,1152]{1,0:T(8,128)(2,1)S(1)}, f32[8,128]{1,0:T(8,128)S(1)}) custom-call(f32[1]{0:T(128)S(6)} %copy.11.scale, f32[1]{0:T(128)S(6)} %copy.12.bias, bf16[512,1152]{1,0:T(8,128)(2,1)S(1)} %get-tuple-element.49.ihi, ...), custom_call_target="tpu_custom_call" | custom-call | flops 339738624 | bytes 2359296 | tf_op jit(solution)/shard_map/pallas_call | solution.py:200
  41.3 1.1 %collective-permute-done.10.raw = f32[224,1152]{1,0:T(8,128)S(1)} collective-permute-done((f32[224,1152]{1,0:T(8,128)S(1)}, f32[224,1152]{1,0:T(8,128)S(1)}, u32[]{:S(2)}, u32[]{:S(2)}) %collective-permute-start.10) | collective-permute-done | bytes 1032224 | tf_op jit(solution)/shard_map/ppermute | solution.py:27
  42.4 1.8 %shard_map.70 = (bf16[512,224]{1,0:T(8,128)(2,1)S(1)}, bf16[512,224]{1,0:T(8,128)(2,1)S(1)}, bf16[224,1152]{1,0:T(8,128)(2,1)S(1)}, bf16[224,1152]{1,0:T(8,128)(2,1)S(1)}, f32[8,128]{1,0:T(8,128)S(1)}) custom-call(f32[1]{0:T(128)S(6)} %copy.11.scale, f32[1]{0:T(128)S(6)} %copy.12.bias, bf16[512,1152]{1,0:T(8,128)(2,1)S(1)} %get-tuple-element.49.ihi, ...), custom_call_target="tpu_custom_call" | custom-call | flops 792723456 | bytes 2359296 | tf_op jit(solution)/shard_map/pallas_call | solution.py:200
  44.2 1.1 %shard_map.71 = f32[256,1152]{1,0:T(8,128)S(1)} custom-call(bf16[512,1152]{1,0:T(8,128)(2,1)S(1)} %get-tuple-element.49.ihi, bf16[512,1152]{1,0:T(8,128)(2,1)S(1)} %get-tuple-element.50.ilo, bf16[512,224]{1,0:T(8,128)(2,1)S(1)} %get-tuple-element.63.chi, bf16[512,224]{1,0:T(8,128)(2,1)S(1)} %get-tuple-element.64.clo, f32[32,1152]{1,0:T(8,128)S(1)} %slice.67.refs_0_), custom_call_target="tpu_custom_call" | custom-call | flops 792723456 | bytes 2359296 | tf_op jit(solution)/shard_map/pallas_call | solution.py:213
  45.3 0.2 collective-permute-start.13
  45.5 5.0 %collective-permute-start.11 = (f32[8,128]{1,0:T(8,128)S(1)}, f32[8,128]{1,0:T(8,128)S(1)}, u32[]{:S(2)}, u32[]{:S(2)}) collective-permute-start(f32[8,128]{1,0:T(8,128)S(1)} %get-tuple-element.70), channel_id=1, source_target_pairs={{0,128},{32,160},{2,130},{34,162},{4,132},{36,164},{6,134},{38,166... | collective-permute-start | bytes 12296 | tf_op jit(solution)/shard_map/ppermute | solution.py:27
  50.5 2.1 %shard_map.72 = (f32[128,1152]{1,0:T(8,128)S(1)}, f32[128,1152]{1,0:T(8,128)S(1)}, f32[128,1152]{1,0:T(8,128)S(1)}, f32[128,1152]{1,0:T(8,128)S(1)}) custom-call(bf16[512,96]{1,0:T(8,128)(2,1)S(1)} %get-tuple-element.80.mhi.chi, bf16[512,96]{1,0:T(8,128)(2,1)S(1)} %get-tuple-element.81.mlo.clo, bf16[96,1152]{1,0:T(8,128)(2,1)S(1)} %get-tuple-element.54.uhi, ...), custom_call_target="tpu_custom_call" | custom-call | flops 2378170368 | bytes 2359296 | tf_op jit(solution)/shard_map/pallas_call | solution.py:226
  52.7 0.4 collective-permute-done.11
  53.1 0.8 shard_map.74
  53.8 0.4 collective-permute-done.12
  54.5 2.5 %collective-permute-start.22 = (f32[96,1152]{1,0:T(8,128)S(1)}, f32[96,1152]{1,0:T(8,128)S(1)}, u32[]{:S(2)}, u32[]{:S(2)}) collective-permute-start(f32[96,1152]{1,0:T(8,128)S(1)} %slice_add_fusion), channel_id=1, source_target_pairs={{0,192},{32,96},{2,194},{34,98},{4,196},{36,100},{6,198},{38,102},... | collective-permute-start | bytes 1327112 | tf_op jit(solution)/shard_map/ppermute | solution.py:27
  57.4 2.4 %collective-permute-start.16 = (f32[136,1152]{1,0:T(8,128)S(1)}, f32[136,1152]{1,0:T(8,128)S(1)}, u32[]{:S(2)}, u32[]{:S(2)}) collective-permute-start(f32[136,1152]{1,0:T(8,128)S(1)} %get-tuple-element.97), channel_id=1, source_target_pairs={{0,16},{32,36},{2,18},{34,38},{4,20},{36,32},{6,22},{38,34},{8,24}... | collective-permute-start | bytes 1880072 | tf_op jit(solution)/shard_map/ppermute | solution.py:27
  59.8 1.3 %collective-permute-start.14 = (f32[136,1152]{1,0:T(8,128)S(1)}, f32[136,1152]{1,0:T(8,128)S(1)}, u32[]{:S(2)}, u32[]{:S(2)}) collective-permute-start(f32[136,1152]{1,0:T(8,128)S(1)} %get-tuple-element.98), channel_id=1, source_target_pairs={{0,24},{32,38},{2,26},{34,32},{4,28},{36,34},{6,30},{38,36},{8,0},... | collective-permute-start | bytes 1880072 | tf_op jit(solution)/shard_map/ppermute | solution.py:27
  61.1 0.7 collective-permute-start.15
  61.8 6.4 %collective-permute-done.22 = f32[96,1152]{1,0:T(8,128)S(1)} collective-permute-done((f32[96,1152]{1,0:T(8,128)S(1)}, f32[96,1152]{1,0:T(8,128)S(1)}, u32[]{:S(2)}, u32[]{:S(2)}) %collective-permute-start.22) | collective-permute-done | bytes 442400 | tf_op jit(solution)/shard_map/ppermute | solution.py:27
  68.4 3.5 %collective-permute-start.24 = (f32[64,1152]{1,0:T(8,128)S(1)}, f32[64,1152]{1,0:T(8,128)S(1)}, u32[]{:S(2)}, u32[]{:S(2)}) collective-permute-start(f32[64,1152]{1,0:T(8,128)S(1)} %pad_maximum_fusion.6), channel_id=1, source_target_pairs={{0,192},{32,96},{2,194},{34,98},{4,196},{36,100},{6,198},{38,102},... | collective-permute-start | bytes 884744 | tf_op jit(solution)/shard_map/ppermute | solution.py:27
  71.9 4.1 %collective-permute-done.14.in1 = f32[136,1152]{1,0:T(8,128)S(1)} collective-permute-done((f32[136,1152]{1,0:T(8,128)S(1)}, f32[136,1152]{1,0:T(8,128)S(1)}, u32[]{:S(2)}, u32[]{:S(2)}) %collective-permute-start.14) | collective-permute-done | bytes 626720 | tf_op jit(solution)/shard_map/ppermute | solution.py:27
  76.3 1.2 %collective-permute-start.17 = (f32[40,1152]{1,0:T(8,128)S(1)}, f32[40,1152]{1,0:T(8,128)S(1)}, u32[]{:S(2)}, u32[]{:S(2)}) collective-permute-start(f32[40,1152]{1,0:T(8,128)S(1)} %get-tuple-element.77), channel_id=1, source_target_pairs={{0,4},{32,48},{2,6},{34,50},{4,0},{36,52},{6,2},{38,54},{8,12},{40... | collective-permute-start | bytes 552968 | tf_op jit(solution)/shard_map/ppermute | solution.py:27
  77.6 2.1 %collective-permute-start.18 = (f32[40,1152]{1,0:T(8,128)S(1)}, f32[40,1152]{1,0:T(8,128)S(1)}, u32[]{:S(2)}, u32[]{:S(2)}) collective-permute-start(f32[40,1152]{1,0:T(8,128)S(1)} %get-tuple-element.78), channel_id=1, source_target_pairs={{0,6},{32,56},{2,0},{34,58},{4,2},{36,60},{6,4},{38,62},{8,14},{40... | collective-permute-start | bytes 552968 | tf_op jit(solution)/shard_map/ppermute | solution.py:27
  79.7 0.6 collective-permute-done.23
  80.4 3.0 %collective-permute-done.17 = f32[40,1152]{1,0:T(8,128)S(1)} collective-permute-done((f32[40,1152]{1,0:T(8,128)S(1)}, f32[40,1152]{1,0:T(8,128)S(1)}, u32[]{:S(2)}, u32[]{:S(2)}) %collective-permute-start.17) | collective-permute-done | bytes 184352 | tf_op jit(solution)/shard_map/ppermute | solution.py:27
  83.5 1.7 %collective-permute-done.18 = f32[40,1152]{1,0:T(8,128)S(1)} collective-permute-done((f32[40,1152]{1,0:T(8,128)S(1)}, f32[40,1152]{1,0:T(8,128)S(1)}, u32[]{:S(2)}, u32[]{:S(2)}) %collective-permute-start.18) | collective-permute-done | bytes 184352 | tf_op jit(solution)/shard_map/ppermute | solution.py:27
  85.1 1.3 %collective-permute-done.19 = f32[40,1152]{1,0:T(8,128)S(1)} collective-permute-done((f32[40,1152]{1,0:T(8,128)S(1)}, f32[40,1152]{1,0:T(8,128)S(1)}, u32[]{:S(2)}, u32[]{:S(2)}) %collective-permute-start.19) | collective-permute-done | bytes 184352 | tf_op jit(solution)/shard_map/ppermute | solution.py:27
  86.6 3.4 %collective-permute-start.20 = (f32[8,128]{1,0:T(8,128)S(1)}, f32[8,128]{1,0:T(8,128)S(1)}, u32[]{:S(2)}, u32[]{:S(2)}) collective-permute-start(f32[8,128]{1,0:T(8,128)S(1)} %pad_maximum_fusion.8), channel_id=1, source_target_pairs={{0,192},{32,96},{2,194},{34,98},{4,196},{36,100},{6,198},{38,102},... | collective-permute-start | bytes 12296 | tf_op jit(solution)/shard_map/ppermute | solution.py:27
  90.0 0.2 multiply_reduce_fusion.2
  90.2 0.8 subtract_multiply_fusion.1
  91.0 0.2 multiply_reduce_fusion
  91.2 0.8 subtract_multiply_fusion
  92.0 1.2 %collective-permute-done.26 = f32[8,128]{1,0:T(8,128)S(1)} collective-permute-done((f32[8,128]{1,0:T(8,128)S(1)}, f32[8,128]{1,0:T(8,128)S(1)}, u32[]{:S(2)}, u32[]{:S(2)}) %collective-permute-start.26) | collective-permute-done | bytes 4128 | tf_op jit(solution)/shard_map/ppermute | solution.py:27
  93.2 0.6 fusion.3
  (52 shorter events, 1.9 us)
Async XLA Ops:
  0.6 12.6 %collective-permute-start.2 = (f32[32,1152]{1,0:T(8,128)}, f32[32,1152]{1,0:T(8,128)S(1)}, u32[]{:S(2)}, u32[]{:S(2)}) collective-permute-start(f32[32,1152]{1,0:T(8,128)} %param.4), channel_id=1, source_target_pairs={{0,4},{32,48},{2,6},{34,50},{4,0},{36,52},{6,2},{38,54},{8,12},{40... | collective-permute-start | bytes 442376 | tf_op jit(solution)/shard_map/ppermute | solution.py:27
  3.7 9.4 %collective-permute-start.1 = (f32[32,1152]{1,0:T(8,128)}, f32[32,1152]{1,0:T(8,128)S(1)}, u32[]{:S(2)}, u32[]{:S(2)}) collective-permute-start(f32[32,1152]{1,0:T(8,128)} %param.4), channel_id=1, source_target_pairs={{0,6},{32,56},{2,0},{34,58},{4,2},{36,60},{6,4},{38,62},{8,14},{40... | collective-permute-start | bytes 442376 | tf_op jit(solution)/shard_map/ppermute | solution.py:27
  4.9 8.3 %collective-permute-start = (f32[32,1152]{1,0:T(8,128)}, f32[32,1152]{1,0:T(8,128)S(1)}, u32[]{:S(2)}, u32[]{:S(2)}) collective-permute-start(f32[32,1152]{1,0:T(8,128)} %param.4), channel_id=1, source_target_pairs={{0,2},{32,40},{2,4},{34,42},{4,6},{36,44},{6,0},{38,46},{8,10},{40... | collective-permute-start | bytes 442376 | tf_op jit(solution)/shard_map/ppermute | solution.py:27
  5.8 2.1 %collective-permute-start.6 = (f32[32,1152]{1,0:T(8,128)}, f32[32,1152]{1,0:T(8,128)S(1)}, u32[]{:S(2)}, u32[]{:S(2)}) collective-permute-start(f32[32,1152]{1,0:T(8,128)} %refs_1_.1), channel_id=1, source_target_pairs={{0,32},{32,0},{2,34},{34,2},{4,36},{36,4},{6,38},{38,6},{8,40},{40... | collective-permute-start | bytes 442376 | tf_op jit(solution)/shard_map/ppermute | solution.py:27
  7.8 19.8 %copy-start = (f32[32,1152]{1,0:T(8,128)S(1)}, f32[32,1152]{1,0:T(8,128)}, u32[]{:S(2)}) copy-start(f32[32,1152]{1,0:T(8,128)} %refs_1_.1) | copy-start | bytes 442372
  7.9 11.7 %collective-permute-start.8 = (f32[64,1152]{1,0:T(8,128)S(1)}, f32[64,1152]{1,0:T(8,128)S(1)}, u32[]{:S(2)}, u32[]{:S(2)}) collective-permute-start(f32[64,1152]{1,0:T(8,128)S(1)} %constant_dynamic-update-slice_fusion.4), channel_id=1, source_target_pairs={{0,64},{32,224},{2,66},{34,226},{4,68},{36,228},{6,70},{38,230},{8... | collective-permute-start | bytes 884744 | tf_op jit(solution)/shard_map/ppermute | solution.py:27
  11.2 13.6 %collective-permute-start.7 = (f32[64,1152]{1,0:T(8,128)S(1)}, f32[64,1152]{1,0:T(8,128)S(1)}, u32[]{:S(2)}, u32[]{:S(2)}) collective-permute-start(f32[64,1152]{1,0:T(8,128)S(1)} %constant_dynamic-update-slice_fusion.4), channel_id=1, source_target_pairs={{0,1},{32,225},{2,3},{34,227},{4,5},{36,229},{6,7},{38,231},{8,9},... | collective-permute-start | bytes 884744 | tf_op jit(solution)/shard_map/ppermute | solution.py:27
  13.2 16.7 %collective-permute-start.5 = (f32[128,1152]{1,0:T(8,128)S(1)}, f32[128,1152]{1,0:T(8,128)S(1)}, u32[]{:S(2)}, u32[]{:S(2)}) collective-permute-start(f32[128,1152]{1,0:T(8,128)S(1)} %constant_dynamic-update-slice_fusion.refs_0_), channel_id=1, source_target_pairs={{0,16},{32,36},{2,18},{34,38},{4,20},{36,32},{6,22},{38,34},{8,24}... | collective-permute-start | bytes 1769480 | tf_op jit(solution)/shard_map/ppermute | solution.py:27
  15.6 15.4 %collective-permute-start.4 = (f32[128,1152]{1,0:T(8,128)S(1)}, f32[128,1152]{1,0:T(8,128)S(1)}, u32[]{:S(2)}, u32[]{:S(2)}) collective-permute-start(f32[128,1152]{1,0:T(8,128)S(1)} %constant_dynamic-update-slice_fusion.refs_0_), channel_id=1, source_target_pairs={{0,24},{32,38},{2,26},{34,32},{4,28},{36,34},{6,30},{38,36},{8,0},... | collective-permute-start | bytes 1769480 | tf_op jit(solution)/shard_map/ppermute | solution.py:27
  17.0 14.2 %collective-permute-start.3 = (f32[128,1152]{1,0:T(8,128)S(1)}, f32[128,1152]{1,0:T(8,128)S(1)}, u32[]{:S(2)}, u32[]{:S(2)}) collective-permute-start(f32[128,1152]{1,0:T(8,128)S(1)} %constant_dynamic-update-slice_fusion.refs_0_), channel_id=1, source_target_pairs={{0,8},{32,34},{2,10},{34,36},{4,12},{36,38},{6,14},{38,32},{8,16},... | collective-permute-start | bytes 1769480 | tf_op jit(solution)/shard_map/ppermute | solution.py:27
  24.9 14.5 %collective-permute-start.9 = (f32[96,1152]{1,0:T(8,128)S(1)}, f32[96,1152]{1,0:T(8,128)S(1)}, u32[]{:S(2)}, u32[]{:S(2)}) collective-permute-start(f32[96,1152]{1,0:T(8,128)S(1)} %pad_maximum_fusion.5), channel_id=1, source_target_pairs={{0,64},{32,224},{2,66},{34,226},{4,68},{36,228},{6,70},{38,230},{8... | collective-permute-start | bytes 1327112 | tf_op jit(solution)/shard_map/ppermute | solution.py:27
  39.5 2.9 %collective-permute-start.10 = (f32[224,1152]{1,0:T(8,128)S(1)}, f32[224,1152]{1,0:T(8,128)S(1)}, u32[]{:S(2)}, u32[]{:S(2)}) collective-permute-start(f32[224,1152]{1,0:T(8,128)S(1)} %pad_maximum_fusion.4), channel_id=1, source_target_pairs={{0,32},{32,0},{2,34},{34,2},{4,36},{36,4},{6,38},{38,6},{8,40},{40... | collective-permute-start | bytes 3096584 | tf_op jit(solution)/shard_map/ppermute | solution.py:27
  45.3 9.1 %collective-permute-start.13 = (f32[256,1152]{1,0:T(8,128)S(1)}, f32[256,1152]{1,0:T(8,128)S(1)}, u32[]{:S(2)}, u32[]{:S(2)}) collective-permute-start(f32[256,1152]{1,0:T(8,128)S(1)} %shard_map.71), channel_id=1, source_target_pairs={{0,32},{32,0},{2,34},{34,2},{4,36},{36,4},{6,38},{38,6},{8,40},{40... | collective-permute-start | bytes 3538952 | tf_op jit(solution)/shard_map/ppermute | solution.py:27
  45.5 7.5 %collective-permute-start.11 = (f32[8,128]{1,0:T(8,128)S(1)}, f32[8,128]{1,0:T(8,128)S(1)}, u32[]{:S(2)}, u32[]{:S(2)}) collective-permute-start(f32[8,128]{1,0:T(8,128)S(1)} %get-tuple-element.70), channel_id=1, source_target_pairs={{0,128},{32,160},{2,130},{34,162},{4,132},{36,164},{6,134},{38,166... | collective-permute-start | bytes 12296 | tf_op jit(solution)/shard_map/ppermute | solution.py:27
  53.1 1.2 %collective-permute-start.12 = (f32[8,128]{1,0:T(8,128)S(1)}, f32[8,128]{1,0:T(8,128)S(1)}, u32[]{:S(2)}, u32[]{:S(2)}) collective-permute-start(f32[8,128]{1,0:T(8,128)S(1)} %add.71), channel_id=1, source_target_pairs={{0,32},{32,0},{2,34},{34,2},{4,36},{36,4},{6,38},{38,6},{8,40},{40... | collective-permute-start | bytes 12296 | tf_op jit(solution)/shard_map/ppermute | solution.py:27
  54.5 13.8 %collective-permute-start.22 = (f32[96,1152]{1,0:T(8,128)S(1)}, f32[96,1152]{1,0:T(8,128)S(1)}, u32[]{:S(2)}, u32[]{:S(2)}) collective-permute-start(f32[96,1152]{1,0:T(8,128)S(1)} %slice_add_fusion), channel_id=1, source_target_pairs={{0,192},{32,96},{2,194},{34,98},{4,196},{36,100},{6,198},{38,102},... | collective-permute-start | bytes 1327112 | tf_op jit(solution)/shard_map/ppermute | solution.py:27
  57.4 14.5 %collective-permute-start.16 = (f32[136,1152]{1,0:T(8,128)S(1)}, f32[136,1152]{1,0:T(8,128)S(1)}, u32[]{:S(2)}, u32[]{:S(2)}) collective-permute-start(f32[136,1152]{1,0:T(8,128)S(1)} %get-tuple-element.97), channel_id=1, source_target_pairs={{0,16},{32,36},{2,18},{34,38},{4,20},{36,32},{6,22},{38,34},{8,24}... | collective-permute-start | bytes 1880072 | tf_op jit(solution)/shard_map/ppermute | solution.py:27
  59.8 16.2 %collective-permute-start.14 = (f32[136,1152]{1,0:T(8,128)S(1)}, f32[136,1152]{1,0:T(8,128)S(1)}, u32[]{:S(2)}, u32[]{:S(2)}) collective-permute-start(f32[136,1152]{1,0:T(8,128)S(1)} %get-tuple-element.98), channel_id=1, source_target_pairs={{0,24},{32,38},{2,26},{34,32},{4,28},{36,34},{6,30},{38,36},{8,0},... | collective-permute-start | bytes 1880072 | tf_op jit(solution)/shard_map/ppermute | solution.py:27
  61.1 15.0 %collective-permute-start.15 = (f32[136,1152]{1,0:T(8,128)S(1)}, f32[136,1152]{1,0:T(8,128)S(1)}, u32[]{:S(2)}, u32[]{:S(2)}) collective-permute-start(f32[136,1152]{1,0:T(8,128)S(1)} %get-tuple-element.99), channel_id=1, source_target_pairs={{0,8},{32,34},{2,10},{34,36},{4,12},{36,38},{6,14},{38,32},{8,16},... | collective-permute-start | bytes 1880072 | tf_op jit(solution)/shard_map/ppermute | solution.py:27
  68.4 11.3 %collective-permute-start.24 = (f32[64,1152]{1,0:T(8,128)S(1)}, f32[64,1152]{1,0:T(8,128)S(1)}, u32[]{:S(2)}, u32[]{:S(2)}) collective-permute-start(f32[64,1152]{1,0:T(8,128)S(1)} %pad_maximum_fusion.6), channel_id=1, source_target_pairs={{0,192},{32,96},{2,194},{34,98},{4,196},{36,100},{6,198},{38,102},... | collective-permute-start | bytes 884744 | tf_op jit(solution)/shard_map/ppermute | solution.py:27
  71.9 8.4 %collective-permute-start.23 = (f32[64,1152]{1,0:T(8,128)S(1)}, f32[64,1152]{1,0:T(8,128)S(1)}, u32[]{:S(2)}, u32[]{:S(2)}) collective-permute-start(f32[64,1152]{1,0:T(8,128)S(1)} %get-tuple-element.88), channel_id=1, source_target_pairs={{0,193},{32,33},{2,195},{34,35},{4,197},{36,37},{6,199},{38,39},{8... | collective-permute-start | bytes 884744 | tf_op jit(solution)/shard_map/ppermute | solution.py:27
  76.3 13.7 %copy-start.1 = (f32[32,1152]{1,0:T(8,128)S(1)}, f32[32,1152]{1,0:T(8,128)}, u32[]{:S(2)}) copy-start(f32[32,1152]{1,0:T(8,128)} %param.4) | copy-start | bytes 442372
  76.3 7.1 %collective-permute-start.17 = (f32[40,1152]{1,0:T(8,128)S(1)}, f32[40,1152]{1,0:T(8,128)S(1)}, u32[]{:S(2)}, u32[]{:S(2)}) collective-permute-start(f32[40,1152]{1,0:T(8,128)S(1)} %get-tuple-element.77), channel_id=1, source_target_pairs={{0,4},{32,48},{2,6},{34,50},{4,0},{36,52},{6,2},{38,54},{8,12},{40... | collective-permute-start | bytes 552968 | tf_op jit(solution)/shard_map/ppermute | solution.py:27
  77.6 7.6 %collective-permute-start.18 = (f32[40,1152]{1,0:T(8,128)S(1)}, f32[40,1152]{1,0:T(8,128)S(1)}, u32[]{:S(2)}, u32[]{:S(2)}) collective-permute-start(f32[40,1152]{1,0:T(8,128)S(1)} %get-tuple-element.78), channel_id=1, source_target_pairs={{0,6},{32,56},{2,0},{34,58},{4,2},{36,60},{6,4},{38,62},{8,14},{40... | collective-permute-start | bytes 552968 | tf_op jit(solution)/shard_map/ppermute | solution.py:27
  79.7 6.7 %collective-permute-start.19 = (f32[40,1152]{1,0:T(8,128)S(1)}, f32[40,1152]{1,0:T(8,128)S(1)}, u32[]{:S(2)}, u32[]{:S(2)}) collective-permute-start(f32[40,1152]{1,0:T(8,128)S(1)} %get-tuple-element.79), channel_id=1, source_target_pairs={{0,2},{32,40},{2,4},{34,42},{4,6},{36,44},{6,0},{38,46},{8,10},{40... | collective-permute-start | bytes 552968 | tf_op jit(solution)/shard_map/ppermute | solution.py:27
  80.3 10.7 %collective-permute-start.25 = (f32[32,1152]{1,0:T(8,128)S(1)}, f32[32,1152]{1,0:T(8,128)S(1)}, u32[]{:S(2)}, u32[]{:S(2)}) collective-permute-start(f32[32,1152]{1,0:T(8,128)S(1)} %slice.101), channel_id=1, source_target_pairs={{0,32},{32,0},{2,34},{34,2},{4,36},{36,4},{6,38},{38,6},{8,40},{40... | collective-permute-start | bytes 442376 | tf_op jit(solution)/shard_map/ppermute | solution.py:27
  86.6 5.3 %collective-permute-start.21 = (f32[8,128]{1,0:T(8,128)S(1)}, f32[8,128]{1,0:T(8,128)S(1)}, u32[]{:S(2)}, u32[]{:S(2)}) collective-permute-start(f32[8,128]{1,0:T(8,128)S(1)} %pad_maximum_fusion.8), channel_id=1, source_target_pairs={{0,193},{32,33},{2,195},{34,35},{4,197},{36,37},{6,199},{38,39},{8... | collective-permute-start | bytes 12296 | tf_op jit(solution)/shard_map/ppermute | solution.py:27
  86.6 5.3 %collective-permute-start.20 = (f32[8,128]{1,0:T(8,128)S(1)}, f32[8,128]{1,0:T(8,128)S(1)}, u32[]{:S(2)}, u32[]{:S(2)}) collective-permute-start(f32[8,128]{1,0:T(8,128)S(1)} %pad_maximum_fusion.8), channel_id=1, source_target_pairs={{0,192},{32,96},{2,194},{34,98},{4,196},{36,100},{6,198},{38,102},... | collective-permute-start | bytes 12296 | tf_op jit(solution)/shard_map/ppermute | solution.py:27
  92.0 1.2 %collective-permute-start.26 = (f32[8,128]{1,0:T(8,128)S(1)}, f32[8,128]{1,0:T(8,128)S(1)}, u32[]{:S(2)}, u32[]{:S(2)}) collective-permute-start(f32[8,128]{1,0:T(8,128)S(1)} %collective-permute-done.21), channel_id=1, source_target_pairs={{0,32},{32,0},{2,34},{34,2},{4,36},{36,4},{6,38},{38,6},{8,40},{40... | collective-permute-start | bytes 12296 | tf_op jit(solution)/shard_map/ppermute | solution.py:27

commit v7 on v5

--- a/solution.py
+++ b/solution.py
@@ -300,7 +300,8 @@
     text_grad = (
         text_unit_grad - text_unit * jnp.sum(text_unit * text_unit_grad, axis=1, keepdims=True)
     ) * text_inv
-    loss = loss + beside + swap(after(beside, (image_grad, text_grad)))
+    loss = loss + beside + swap(after(beside, text_grad))
+    loss = after(loss, image_grad)
     return ((loss[:1, 0] + loss[:1, 127]) / (rows * 2 * NX * NY * NZ), image_grad, text_grad)
 
 

time: 96.5 us -> 96.5 us (level)
  no operation moved by 1% of the time
where the time goes in v7:
time: 96.5 us; the launch traced here: 96.3 us
  waiting for transfers between devices  36.1 us (37%)
  starting transfers between devices  35.6 us (37%)
  Pallas kernels  14.3 us (15%)
  other arithmetic  4.73 us (5%)
  between operations  4.51 us (5%)
  local copies, waits for them, and re-layouts  1.07 us (1%)
    ppermute x27, waiting for transfers between devices, send(): return lax.ppermute(value, AXES, pairs(target))  36.1 us
    ppermute x27, starting transfers between devices, send(): return lax.ppermute(value, AXES, pairs(target))  35.6 us
    pallas_call x2, Pallas kernels, group_call(): pl.pallas_call(functools.partial(group_kernel, texts[0].shape[0] if start...  6.73 us
    pallas_call x2, Pallas kernels, far_call(): pl.pallas_call(functools.partial(far_kernel, final), out_shape=[b16(rows,...  3.36 us
    pallas_call x1, Pallas kernels, last_call(): pl.pallas_call(last_kernel, out_shape=[f32(rows // 4, width)] * 4, in_spe...  2.15 us
    reduce_sum x2, other arithmetic, normalize(): inverse = lax.rsqrt(jnp.sum(embed * embed, axis=1, keepdims=True) + 1e-06)  2.07 us
  transfers between devices with their start and end apart: 27, of which 16 were waited for; matrix products, arithmetic and copies ran while one was open for 5% of the time, Pallas kernels for 12%

profile of v7, /device:TPU:8, one launch (start us, length us, event | category | flops | bytes accessed | tf_op | source)
XLA Modules:
  0.0 96.3 jit_solution(15437010204350835731)
XLA Ops:
  0.6 3.1 %collective-permute-start.2 = (f32[32,1152]{1,0:T(8,128)}, f32[32,1152]{1,0:T(8,128)S(1)}, u32[]{:S(2)}, u32[]{:S(2)}) collective-permute-start(f32[32,1152]{1,0:T(8,128)} %param.4), channel_id=1, source_target_pairs={{0,4},{32,48},{2,6},{34,50},{4,0},{36,52},{6,2},{38,54},{8,12},{40... | collective-permute-start | bytes 442376 | tf_op jit(solution)/shard_map/ppermute | solution.py:27
  3.7 1.1 %collective-permute-start.1 = (f32[32,1152]{1,0:T(8,128)}, f32[32,1152]{1,0:T(8,128)S(1)}, u32[]{:S(2)}, u32[]{:S(2)}) collective-permute-start(f32[32,1152]{1,0:T(8,128)} %param.4), channel_id=1, source_target_pairs={{0,6},{32,56},{2,0},{34,58},{4,2},{36,60},{6,4},{38,62},{8,14},{40... | collective-permute-start | bytes 442376 | tf_op jit(solution)/shard_map/ppermute | solution.py:27
  4.9 0.9 collective-permute-start
  5.8 1.0 %multiply_reduce_fusion.3 = (f32[32]{0:T(128)S(1)}, f32[64,1152]{1,0:T(8,128)S(1)}) fusion(f32[32,1152]{1,0:T(8,128)} %refs_1_.1), kind=kLoop, calls=%fused_computation.21 | loop fusion | flops 73695 | bytes 295424 | tf_op jit(solution)/shard_map/reduce_sum | solution.py:248
  6.8 1.0 %multiply_reduce_fusion.1 = (f32[32]{0:T(128)S(1)}, f32[128,1152]{1,0:T(8,128)S(1)}) fusion(f32[32,1152]{1,0:T(8,128)} %param.4), kind=kLoop, calls=%fused_computation.18 | loop fusion | flops 73695 | bytes 295424 | tf_op jit(solution)/shard_map/reduce_sum | solution.py:248
  7.9 3.3 %collective-permute-start.8 = (f32[64,1152]{1,0:T(8,128)S(1)}, f32[64,1152]{1,0:T(8,128)S(1)}, u32[]{:S(2)}, u32[]{:S(2)}) collective-permute-start(f32[64,1152]{1,0:T(8,128)S(1)} %constant_dynamic-update-slice_fusion.4), channel_id=1, source_target_pairs={{0,64},{32,224},{2,66},{34,226},{4,68},{36,228},{6,70},{38,230},{8... | collective-permute-start | bytes 884744 | tf_op jit(solution)/shard_map/ppermute | solution.py:27
  11.2 1.9 %collective-permute-start.7 = (f32[64,1152]{1,0:T(8,128)S(1)}, f32[64,1152]{1,0:T(8,128)S(1)}, u32[]{:S(2)}, u32[]{:S(2)}) collective-permute-start(f32[64,1152]{1,0:T(8,128)S(1)} %constant_dynamic-update-slice_fusion.4), channel_id=1, source_target_pairs={{0,1},{32,225},{2,3},{34,227},{4,5},{36,229},{6,7},{38,231},{8,9},... | collective-permute-start | bytes 884744 | tf_op jit(solution)/shard_map/ppermute | solution.py:27
  13.2 2.4 %collective-permute-start.5 = (f32[128,1152]{1,0:T(8,128)S(1)}, f32[128,1152]{1,0:T(8,128)S(1)}, u32[]{:S(2)}, u32[]{:S(2)}) collective-permute-start(f32[128,1152]{1,0:T(8,128)S(1)} %constant_dynamic-update-slice_fusion.refs_0_), channel_id=1, source_target_pairs={{0,16},{32,36},{2,18},{34,38},{4,20},{36,32},{6,22},{38,34},{8,24}... | collective-permute-start | bytes 1769480 | tf_op jit(solution)/shard_map/ppermute | solution.py:27
  15.6 1.3 %collective-permute-start.4 = (f32[128,1152]{1,0:T(8,128)S(1)}, f32[128,1152]{1,0:T(8,128)S(1)}, u32[]{:S(2)}, u32[]{:S(2)}) collective-permute-start(f32[128,1152]{1,0:T(8,128)S(1)} %constant_dynamic-update-slice_fusion.refs_0_), channel_id=1, source_target_pairs={{0,24},{32,38},{2,26},{34,32},{4,28},{36,34},{6,30},{38,36},{8,0},... | collective-permute-start | bytes 1769480 | tf_op jit(solution)/shard_map/ppermute | solution.py:27
  17.0 0.7 collective-permute-start.3
  17.6 1.9 %collective-permute-done.8.refs_4_ = f32[64,1152]{1,0:T(8,128)S(1)} collective-permute-done((f32[64,1152]{1,0:T(8,128)S(1)}, f32[64,1152]{1,0:T(8,128)S(1)}, u32[]{:S(2)}, u32[]{:S(2)}) %collective-permute-start.8) | collective-permute-done | bytes 294944 | tf_op jit(solution)/shard_map/ppermute | solution.py:27
  19.6 5.3 %collective-permute-done.7.refs_3_ = f32[64,1152]{1,0:T(8,128)S(1)} collective-permute-done((f32[64,1152]{1,0:T(8,128)S(1)}, f32[64,1152]{1,0:T(8,128)S(1)}, u32[]{:S(2)}, u32[]{:S(2)}) %collective-permute-start.7) | collective-permute-done | bytes 294944 | tf_op jit(solution)/shard_map/ppermute | solution.py:27
  24.9 1.5 %collective-permute-start.9 = (f32[96,1152]{1,0:T(8,128)S(1)}, f32[96,1152]{1,0:T(8,128)S(1)}, u32[]{:S(2)}, u32[]{:S(2)}) collective-permute-start(f32[96,1152]{1,0:T(8,128)S(1)} %pad_maximum_fusion.5), channel_id=1, source_target_pairs={{0,64},{32,224},{2,66},{34,226},{4,68},{36,228},{6,70},{38,230},{8... | collective-permute-start | bytes 1327112 | tf_op jit(solution)/shard_map/ppermute | solution.py:27
  27.6 2.3 %shard_map.67 = (f32[128,1152]{1,0:T(8,128)S(1)}, bf16[128,1152]{1,0:T(8,128)(2,1)S(1)}, bf16[128,1152]{1,0:T(8,128)(2,1)S(1)}, f32[192,1152]{1,0:T(8,128)S(1)},...) custom-call(f32[1]{0:T(128)S(6)} %copy.11.scale, f32[1]{0:T(128)S(6)} %copy.12.bias, ...), custom_call_target="tpu_custom_call" | custom-call | flops 509607936 | bytes 589824 | tf_op jit(solution)/shard_map/pallas_call | solution.py:187
  29.9 1.1 %collective-permute-done.4.refs_1_ = f32[128,1152]{1,0:T(8,128)S(1)} collective-permute-done((f32[128,1152]{1,0:T(8,128)S(1)}, f32[128,1152]{1,0:T(8,128)S(1)}, u32[]{:S(2)}, u32[]{:S(2)}) %collective-permute-start.4) | collective-permute-done | bytes 589856 | tf_op jit(solution)/shard_map/ppermute | solution.py:27
  31.2 4.4 %shard_map.68 = (f32[384,1152]{1,0:T(8,128)S(1)}, bf16[512,1152]{1,0:T(8,128)(2,1)S(1)}, bf16[512,1152]{1,0:T(8,128)(2,1)S(1)}, f32[192,1152]{1,0:T(8,128)S(1)}, f32[8,128]{1,0:T(8,128)S(1)}) custom-call(f32[1]{0:T(128)S(6)} %copy.11.scale, f32[1]{0:T(128)S(6)} %copy.12.bias, f32[128,1152]{1,0:T(8,128)S(1)} %collective-permute-done.3.refs_0_, ...), custom_call_target="tpu_custom_call" | custom-call | flops 1528823808 | bytes 1769472 | tf_op jit(solution)/shard_map/pallas_call | solution.py:187
  35.6 3.8 %collective-permute-done.9.raw = f32[96,1152]{1,0:T(8,128)S(1)} collective-permute-done((f32[96,1152]{1,0:T(8,128)S(1)}, f32[96,1152]{1,0:T(8,128)S(1)}, u32[]{:S(2)}, u32[]{:S(2)}) %collective-permute-start.9) | collective-permute-done | bytes 442400 | tf_op jit(solution)/shard_map/ppermute | solution.py:27
  39.5 0.3 collective-permute-start.10
  39.8 1.5 %shard_map.69 = (bf16[512,96]{1,0:T(8,128)(2,1)S(1)}, bf16[512,96]{1,0:T(8,128)(2,1)S(1)}, bf16[96,1152]{1,0:T(8,128)(2,1)S(1)}, bf16[96,1152]{1,0:T(8,128)(2,1)S(1)}, f32[8,128]{1,0:T(8,128)S(1)}) custom-call(f32[1]{0:T(128)S(6)} %copy.11.scale, f32[1]{0:T(128)S(6)} %copy.12.bias, bf16[512,1152]{1,0:T(8,128)(2,1)S(1)} %get-tuple-element.50.ihi, ...), custom_call_target="tpu_custom_call" | custom-call | flops 339738624 | bytes 2359296 | tf_op jit(solution)/shard_map/pallas_call | solution.py:200
  41.3 1.1 %collective-permute-done.10.raw = f32[224,1152]{1,0:T(8,128)S(1)} collective-permute-done((f32[224,1152]{1,0:T(8,128)S(1)}, f32[224,1152]{1,0:T(8,128)S(1)}, u32[]{:S(2)}, u32[]{:S(2)}) %collective-permute-start.10) | collective-permute-done | bytes 1032224 | tf_op jit(solution)/shard_map/ppermute | solution.py:27
  42.4 1.8 %shard_map.70 = (bf16[512,224]{1,0:T(8,128)(2,1)S(1)}, bf16[512,224]{1,0:T(8,128)(2,1)S(1)}, bf16[224,1152]{1,0:T(8,128)(2,1)S(1)}, bf16[224,1152]{1,0:T(8,128)(2,1)S(1)}, f32[8,128]{1,0:T(8,128)S(1)}) custom-call(f32[1]{0:T(128)S(6)} %copy.11.scale, f32[1]{0:T(128)S(6)} %copy.12.bias, bf16[512,1152]{1,0:T(8,128)(2,1)S(1)} %get-tuple-element.50.ihi, ...), custom_call_target="tpu_custom_call" | custom-call | flops 792723456 | bytes 2359296 | tf_op jit(solution)/shard_map/pallas_call | solution.py:200
  44.2 1.1 %shard_map.71 = f32[256,1152]{1,0:T(8,128)S(1)} custom-call(bf16[512,1152]{1,0:T(8,128)(2,1)S(1)} %get-tuple-element.50.ihi, bf16[512,1152]{1,0:T(8,128)(2,1)S(1)} %get-tuple-element.51.ilo, bf16[512,224]{1,0:T(8,128)(2,1)S(1)} %get-tuple-element.64.chi, bf16[512,224]{1,0:T(8,128)(2,1)S(1)} %get-tuple-element.65.clo, f32[32,1152]{1,0:T(8,128)S(1)} %slice.67.refs_0_), custom_call_target="tpu_custom_call" | custom-call | flops 792723456 | bytes 2359296 | tf_op jit(solution)/shard_map/pallas_call | solution.py:213
  45.3 0.2 collective-permute-start.13
  45.5 2.1 %shard_map.72 = (f32[128,1152]{1,0:T(8,128)S(1)}, f32[128,1152]{1,0:T(8,128)S(1)}, f32[128,1152]{1,0:T(8,128)S(1)}, f32[128,1152]{1,0:T(8,128)S(1)}) custom-call(bf16[512,96]{1,0:T(8,128)(2,1)S(1)} %get-tuple-element.81.mhi.chi, bf16[512,96]{1,0:T(8,128)(2,1)S(1)} %get-tuple-element.82.mlo.clo, bf16[96,1152]{1,0:T(8,128)(2,1)S(1)} %get-tuple-element.55.uhi, ...), custom_call_target="tpu_custom_call" | custom-call | flops 2378170368 | bytes 2359296 | tf_op jit(solution)/shard_map/pallas_call | solution.py:226
  47.7 1.5 %collective-permute-done.11 = f32[8,128]{1,0:T(8,128)S(1)} collective-permute-done((f32[8,128]{1,0:T(8,128)S(1)}, f32[8,128]{1,0:T(8,128)S(1)}, u32[]{:S(2)}, u32[]{:S(2)}) %collective-permute-start.11) | collective-permute-done | bytes 4128 | tf_op jit(solution)/shard_map/ppermute | solution.py:27
  49.1 0.8 shard_map.74
  49.9 0.4 collective-permute-done.12
  50.6 2.5 %collective-permute-start.22 = (f32[96,1152]{1,0:T(8,128)S(1)}, f32[96,1152]{1,0:T(8,128)S(1)}, u32[]{:S(2)}, u32[]{:S(2)}) collective-permute-start(f32[96,1152]{1,0:T(8,128)S(1)} %slice_add_fusion), channel_id=1, source_target_pairs={{0,192},{32,96},{2,194},{34,98},{4,196},{36,100},{6,198},{38,102},... | collective-permute-start | bytes 1327112 | tf_op jit(solution)/shard_map/ppermute | solution.py:27
  53.5 2.4 %collective-permute-start.16 = (f32[136,1152]{1,0:T(8,128)S(1)}, f32[136,1152]{1,0:T(8,128)S(1)}, u32[]{:S(2)}, u32[]{:S(2)}) collective-permute-start(f32[136,1152]{1,0:T(8,128)S(1)} %get-tuple-element.99), channel_id=1, source_target_pairs={{0,16},{32,36},{2,18},{34,38},{4,20},{36,32},{6,22},{38,34},{8,24}... | collective-permute-start | bytes 1880072 | tf_op jit(solution)/shard_map/ppermute | solution.py:27
  55.9 1.3 %collective-permute-start.14 = (f32[136,1152]{1,0:T(8,128)S(1)}, f32[136,1152]{1,0:T(8,128)S(1)}, u32[]{:S(2)}, u32[]{:S(2)}) collective-permute-start(f32[136,1152]{1,0:T(8,128)S(1)} %get-tuple-element.100), channel_id=1, source_target_pairs={{0,24},{32,38},{2,26},{34,32},{4,28},{36,34},{6,30},{38,36},{8,0},... | collective-permute-start | bytes 1880072 | tf_op jit(solution)/shard_map/ppermute | solution.py:27
  57.2 0.7 collective-permute-start.15
  57.9 6.7 %collective-permute-done.22 = f32[96,1152]{1,0:T(8,128)S(1)} collective-permute-done((f32[96,1152]{1,0:T(8,128)S(1)}, f32[96,1152]{1,0:T(8,128)S(1)}, u32[]{:S(2)}, u32[]{:S(2)}) %collective-permute-start.22) | collective-permute-done | bytes 442400 | tf_op jit(solution)/shard_map/ppermute | solution.py:27
  64.8 3.7 %collective-permute-start.24 = (f32[64,1152]{1,0:T(8,128)S(1)}, f32[64,1152]{1,0:T(8,128)S(1)}, u32[]{:S(2)}, u32[]{:S(2)}) collective-permute-start(f32[64,1152]{1,0:T(8,128)S(1)} %pad_maximum_fusion.6), channel_id=1, source_target_pairs={{0,192},{32,96},{2,194},{34,98},{4,196},{36,100},{6,198},{38,102},... | collective-permute-start | bytes 884744 | tf_op jit(solution)/shard_map/ppermute | solution.py:27
  68.5 3.6 %collective-permute-done.14.in1 = f32[136,1152]{1,0:T(8,128)S(1)} collective-permute-done((f32[136,1152]{1,0:T(8,128)S(1)}, f32[136,1152]{1,0:T(8,128)S(1)}, u32[]{:S(2)}, u32[]{:S(2)}) %collective-permute-start.14) | collective-permute-done | bytes 626720 | tf_op jit(solution)/shard_map/ppermute | solution.py:27
  72.4 1.2 %collective-permute-start.17 = (f32[40,1152]{1,0:T(8,128)S(1)}, f32[40,1152]{1,0:T(8,128)S(1)}, u32[]{:S(2)}, u32[]{:S(2)}) collective-permute-start(f32[40,1152]{1,0:T(8,128)S(1)} %get-tuple-element.78), channel_id=1, source_target_pairs={{0,4},{32,48},{2,6},{34,50},{4,0},{36,52},{6,2},{38,54},{8,12},{40... | collective-permute-start | bytes 552968 | tf_op jit(solution)/shard_map/ppermute | solution.py:27
  73.7 2.1 %collective-permute-start.18 = (f32[40,1152]{1,0:T(8,128)S(1)}, f32[40,1152]{1,0:T(8,128)S(1)}, u32[]{:S(2)}, u32[]{:S(2)}) collective-permute-start(f32[40,1152]{1,0:T(8,128)S(1)} %get-tuple-element.79), channel_id=1, source_target_pairs={{0,6},{32,56},{2,0},{34,58},{4,2},{36,60},{6,4},{38,62},{8,14},{40... | collective-permute-start | bytes 552968 | tf_op jit(solution)/shard_map/ppermute | solution.py:27
  75.8 0.9 collective-permute-done.23
  76.7 0.8 collective-permute-start.25
  77.5 2.0 %collective-permute-done.17 = f32[40,1152]{1,0:T(8,128)S(1)} collective-permute-done((f32[40,1152]{1,0:T(8,128)S(1)}, f32[40,1152]{1,0:T(8,128)S(1)}, u32[]{:S(2)}, u32[]{:S(2)}) %collective-permute-start.17) | collective-permute-done | bytes 184352 | tf_op jit(solution)/shard_map/ppermute | solution.py:27
  79.6 1.7 %collective-permute-done.18 = f32[40,1152]{1,0:T(8,128)S(1)} collective-permute-done((f32[40,1152]{1,0:T(8,128)S(1)}, f32[40,1152]{1,0:T(8,128)S(1)}, u32[]{:S(2)}, u32[]{:S(2)}) %collective-permute-start.18) | collective-permute-done | bytes 184352 | tf_op jit(solution)/shard_map/ppermute | solution.py:27
  81.2 1.3 %collective-permute-done.19 = f32[40,1152]{1,0:T(8,128)S(1)} collective-permute-done((f32[40,1152]{1,0:T(8,128)S(1)}, f32[40,1152]{1,0:T(8,128)S(1)}, u32[]{:S(2)}, u32[]{:S(2)}) %collective-permute-start.19) | collective-permute-done | bytes 184352 | tf_op jit(solution)/shard_map/ppermute | solution.py:27
  82.7 3.1 %collective-permute-start.21 = (f32[8,128]{1,0:T(8,128)S(1)}, f32[8,128]{1,0:T(8,128)S(1)}, u32[]{:S(2)}, u32[]{:S(2)}) collective-permute-start(f32[8,128]{1,0:T(8,128)S(1)} %pad_maximum_fusion.8), channel_id=1, source_target_pairs={{0,192},{32,96},{2,194},{34,98},{4,196},{36,100},{6,198},{38,102},... | collective-permute-start | bytes 12296 | tf_op jit(solution)/shard_map/ppermute | solution.py:27
  85.8 1.0 %collective-permute-start.20 = (f32[8,128]{1,0:T(8,128)S(1)}, f32[8,128]{1,0:T(8,128)S(1)}, u32[]{:S(2)}, u32[]{:S(2)}) collective-permute-start(f32[8,128]{1,0:T(8,128)S(1)} %pad_maximum_fusion.8), channel_id=1, source_target_pairs={{0,128},{32,160},{2,130},{34,162},{4,132},{36,164},{6,134},{38,166... | collective-permute-start | bytes 12296 | tf_op jit(solution)/shard_map/ppermute | solution.py:27
  87.0 0.2 multiply_reduce_fusion.2
  87.1 0.8 subtract_multiply_fusion.1
  87.9 0.8 subtract_multiply_fusion
  88.7 4.6 %collective-permute-done.20 = f32[8,128]{1,0:T(8,128)S(1)} collective-permute-done((f32[8,128]{1,0:T(8,128)S(1)}, f32[8,128]{1,0:T(8,128)S(1)}, u32[]{:S(2)}, u32[]{:S(2)}) %collective-permute-start.20) | collective-permute-done | bytes 4128 | tf_op jit(solution)/shard_map/ppermute | solution.py:27
  93.4 0.6 fusion.3
  (52 shorter events, 2.0 us)
Async XLA Ops:
  0.6 12.6 %collective-permute-start.2 = (f32[32,1152]{1,0:T(8,128)}, f32[32,1152]{1,0:T(8,128)S(1)}, u32[]{:S(2)}, u32[]{:S(2)}) collective-permute-start(f32[32,1152]{1,0:T(8,128)} %param.4), channel_id=1, source_target_pairs={{0,4},{32,48},{2,6},{34,50},{4,0},{36,52},{6,2},{38,54},{8,12},{40... | collective-permute-start | bytes 442376 | tf_op jit(solution)/shard_map/ppermute | solution.py:27
  3.7 9.4 %collective-permute-start.1 = (f32[32,1152]{1,0:T(8,128)}, f32[32,1152]{1,0:T(8,128)S(1)}, u32[]{:S(2)}, u32[]{:S(2)}) collective-permute-start(f32[32,1152]{1,0:T(8,128)} %param.4), channel_id=1, source_target_pairs={{0,6},{32,56},{2,0},{34,58},{4,2},{36,60},{6,4},{38,62},{8,14},{40... | collective-permute-start | bytes 442376 | tf_op jit(solution)/shard_map/ppermute | solution.py:27
  4.9 8.3 %collective-permute-start = (f32[32,1152]{1,0:T(8,128)}, f32[32,1152]{1,0:T(8,128)S(1)}, u32[]{:S(2)}, u32[]{:S(2)}) collective-permute-start(f32[32,1152]{1,0:T(8,128)} %param.4), channel_id=1, source_target_pairs={{0,2},{32,40},{2,4},{34,42},{4,6},{36,44},{6,0},{38,46},{8,10},{40... | collective-permute-start | bytes 442376 | tf_op jit(solution)/shard_map/ppermute | solution.py:27
  5.8 2.1 %collective-permute-start.6 = (f32[32,1152]{1,0:T(8,128)}, f32[32,1152]{1,0:T(8,128)S(1)}, u32[]{:S(2)}, u32[]{:S(2)}) collective-permute-start(f32[32,1152]{1,0:T(8,128)} %refs_1_.1), channel_id=1, source_target_pairs={{0,32},{32,0},{2,34},{34,2},{4,36},{36,4},{6,38},{38,6},{8,40},{40... | collective-permute-start | bytes 442376 | tf_op jit(solution)/shard_map/ppermute | solution.py:27
  7.8 19.8 %copy-start = (f32[32,1152]{1,0:T(8,128)S(1)}, f32[32,1152]{1,0:T(8,128)}, u32[]{:S(2)}) copy-start(f32[32,1152]{1,0:T(8,128)} %refs_1_.1) | copy-start | bytes 442372
  7.9 11.7 %collective-permute-start.8 = (f32[64,1152]{1,0:T(8,128)S(1)}, f32[64,1152]{1,0:T(8,128)S(1)}, u32[]{:S(2)}, u32[]{:S(2)}) collective-permute-start(f32[64,1152]{1,0:T(8,128)S(1)} %constant_dynamic-update-slice_fusion.4), channel_id=1, source_target_pairs={{0,64},{32,224},{2,66},{34,226},{4,68},{36,228},{6,70},{38,230},{8... | collective-permute-start | bytes 884744 | tf_op jit(solution)/shard_map/ppermute | solution.py:27
  11.2 13.6 %collective-permute-start.7 = (f32[64,1152]{1,0:T(8,128)S(1)}, f32[64,1152]{1,0:T(8,128)S(1)}, u32[]{:S(2)}, u32[]{:S(2)}) collective-permute-start(f32[64,1152]{1,0:T(8,128)S(1)} %constant_dynamic-update-slice_fusion.4), channel_id=1, source_target_pairs={{0,1},{32,225},{2,3},{34,227},{4,5},{36,229},{6,7},{38,231},{8,9},... | collective-permute-start | bytes 884744 | tf_op jit(solution)/shard_map/ppermute | solution.py:27
  13.2 16.7 %collective-permute-start.5 = (f32[128,1152]{1,0:T(8,128)S(1)}, f32[128,1152]{1,0:T(8,128)S(1)}, u32[]{:S(2)}, u32[]{:S(2)}) collective-permute-start(f32[128,1152]{1,0:T(8,128)S(1)} %constant_dynamic-update-slice_fusion.refs_0_), channel_id=1, source_target_pairs={{0,16},{32,36},{2,18},{34,38},{4,20},{36,32},{6,22},{38,34},{8,24}... | collective-permute-start | bytes 1769480 | tf_op jit(solution)/shard_map/ppermute | solution.py:27
  15.6 15.4 %collective-permute-start.4 = (f32[128,1152]{1,0:T(8,128)S(1)}, f32[128,1152]{1,0:T(8,128)S(1)}, u32[]{:S(2)}, u32[]{:S(2)}) collective-permute-start(f32[128,1152]{1,0:T(8,128)S(1)} %constant_dynamic-update-slice_fusion.refs_0_), channel_id=1, source_target_pairs={{0,24},{32,38},{2,26},{34,32},{4,28},{36,34},{6,30},{38,36},{8,0},... | collective-permute-start | bytes 1769480 | tf_op jit(solution)/shard_map/ppermute | solution.py:27
  17.0 14.2 %collective-permute-start.3 = (f32[128,1152]{1,0:T(8,128)S(1)}, f32[128,1152]{1,0:T(8,128)S(1)}, u32[]{:S(2)}, u32[]{:S(2)}) collective-permute-start(f32[128,1152]{1,0:T(8,128)S(1)} %constant_dynamic-update-slice_fusion.refs_0_), channel_id=1, source_target_pairs={{0,8},{32,34},{2,10},{34,36},{4,12},{36,38},{6,14},{38,32},{8,16},... | collective-permute-start | bytes 1769480 | tf_op jit(solution)/shard_map/ppermute | solution.py:27
  24.9 14.5 %collective-permute-start.9 = (f32[96,1152]{1,0:T(8,128)S(1)}, f32[96,1152]{1,0:T(8,128)S(1)}, u32[]{:S(2)}, u32[]{:S(2)}) collective-permute-start(f32[96,1152]{1,0:T(8,128)S(1)} %pad_maximum_fusion.5), channel_id=1, source_target_pairs={{0,64},{32,224},{2,66},{34,226},{4,68},{36,228},{6,70},{38,230},{8... | collective-permute-start | bytes 1327112 | tf_op jit(solution)/shard_map/ppermute | solution.py:27
  39.5 2.9 %collective-permute-start.10 = (f32[224,1152]{1,0:T(8,128)S(1)}, f32[224,1152]{1,0:T(8,128)S(1)}, u32[]{:S(2)}, u32[]{:S(2)}) collective-permute-start(f32[224,1152]{1,0:T(8,128)S(1)} %pad_maximum_fusion.4), channel_id=1, source_target_pairs={{0,32},{32,0},{2,34},{34,2},{4,36},{36,4},{6,38},{38,6},{8,40},{40... | collective-permute-start | bytes 3096584 | tf_op jit(solution)/shard_map/ppermute | solution.py:27
  45.3 5.2 %collective-permute-start.13 = (f32[256,1152]{1,0:T(8,128)S(1)}, f32[256,1152]{1,0:T(8,128)S(1)}, u32[]{:S(2)}, u32[]{:S(2)}) collective-permute-start(f32[256,1152]{1,0:T(8,128)S(1)} %shard_map.71), channel_id=1, source_target_pairs={{0,32},{32,0},{2,34},{34,2},{4,36},{36,4},{6,38},{38,6},{8,40},{40... | collective-permute-start | bytes 3538952 | tf_op jit(solution)/shard_map/ppermute | solution.py:27
  45.5 3.6 %collective-permute-start.11 = (f32[8,128]{1,0:T(8,128)S(1)}, f32[8,128]{1,0:T(8,128)S(1)}, u32[]{:S(2)}, u32[]{:S(2)}) collective-permute-start(f32[8,128]{1,0:T(8,128)S(1)} %get-tuple-element.71), channel_id=1, source_target_pairs={{0,1},{32,33},{2,3},{34,35},{4,5},{36,37},{6,7},{38,39},{8,9},{40,... | collective-permute-start | bytes 12296 | tf_op jit(solution)/shard_map/ppermute | solution.py:27
  49.1 1.2 %collective-permute-start.12 = (f32[8,128]{1,0:T(8,128)S(1)}, f32[8,128]{1,0:T(8,128)S(1)}, u32[]{:S(2)}, u32[]{:S(2)}) collective-permute-start(f32[8,128]{1,0:T(8,128)S(1)} %add.71), channel_id=1, source_target_pairs={{0,32},{32,0},{2,34},{34,2},{4,36},{36,4},{6,38},{38,6},{8,40},{40... | collective-permute-start | bytes 12296 | tf_op jit(solution)/shard_map/ppermute | solution.py:27
  50.6 14.1 %collective-permute-start.22 = (f32[96,1152]{1,0:T(8,128)S(1)}, f32[96,1152]{1,0:T(8,128)S(1)}, u32[]{:S(2)}, u32[]{:S(2)}) collective-permute-start(f32[96,1152]{1,0:T(8,128)S(1)} %slice_add_fusion), channel_id=1, source_target_pairs={{0,192},{32,96},{2,194},{34,98},{4,196},{36,100},{6,198},{38,102},... | collective-permute-start | bytes 1327112 | tf_op jit(solution)/shard_map/ppermute | solution.py:27
  53.5 15.0 %collective-permute-start.16 = (f32[136,1152]{1,0:T(8,128)S(1)}, f32[136,1152]{1,0:T(8,128)S(1)}, u32[]{:S(2)}, u32[]{:S(2)}) collective-permute-start(f32[136,1152]{1,0:T(8,128)S(1)} %get-tuple-element.99), channel_id=1, source_target_pairs={{0,16},{32,36},{2,18},{34,38},{4,20},{36,32},{6,22},{38,34},{8,24}... | collective-permute-start | bytes 1880072 | tf_op jit(solution)/shard_map/ppermute | solution.py:27
  55.9 16.2 %collective-permute-start.14 = (f32[136,1152]{1,0:T(8,128)S(1)}, f32[136,1152]{1,0:T(8,128)S(1)}, u32[]{:S(2)}, u32[]{:S(2)}) collective-permute-start(f32[136,1152]{1,0:T(8,128)S(1)} %get-tuple-element.100), channel_id=1, source_target_pairs={{0,24},{32,38},{2,26},{34,32},{4,28},{36,34},{6,30},{38,36},{8,0},... | collective-permute-start | bytes 1880072 | tf_op jit(solution)/shard_map/ppermute | solution.py:27
  57.2 15.0 %collective-permute-start.15 = (f32[136,1152]{1,0:T(8,128)S(1)}, f32[136,1152]{1,0:T(8,128)S(1)}, u32[]{:S(2)}, u32[]{:S(2)}) collective-permute-start(f32[136,1152]{1,0:T(8,128)S(1)} %get-tuple-element.101), channel_id=1, source_target_pairs={{0,8},{32,34},{2,10},{34,36},{4,12},{36,38},{6,14},{38,32},{8,16},... | collective-permute-start | bytes 1880072 | tf_op jit(solution)/shard_map/ppermute | solution.py:27
  64.8 11.0 %collective-permute-start.24 = (f32[64,1152]{1,0:T(8,128)S(1)}, f32[64,1152]{1,0:T(8,128)S(1)}, u32[]{:S(2)}, u32[]{:S(2)}) collective-permute-start(f32[64,1152]{1,0:T(8,128)S(1)} %pad_maximum_fusion.6), channel_id=1, source_target_pairs={{0,192},{32,96},{2,194},{34,98},{4,196},{36,100},{6,198},{38,102},... | collective-permute-start | bytes 884744 | tf_op jit(solution)/shard_map/ppermute | solution.py:27
  68.5 8.2 %collective-permute-start.23 = (f32[64,1152]{1,0:T(8,128)S(1)}, f32[64,1152]{1,0:T(8,128)S(1)}, u32[]{:S(2)}, u32[]{:S(2)}) collective-permute-start(f32[64,1152]{1,0:T(8,128)S(1)} %get-tuple-element.90), channel_id=1, source_target_pairs={{0,193},{32,33},{2,195},{34,35},{4,197},{36,37},{6,199},{38,39},{8... | collective-permute-start | bytes 884744 | tf_op jit(solution)/shard_map/ppermute | solution.py:27
  72.4 14.3 %copy-start.1 = (f32[32,1152]{1,0:T(8,128)S(1)}, f32[32,1152]{1,0:T(8,128)}, u32[]{:S(2)}) copy-start(f32[32,1152]{1,0:T(8,128)} %param.4) | copy-start | bytes 442372
  72.4 7.1 %collective-permute-start.17 = (f32[40,1152]{1,0:T(8,128)S(1)}, f32[40,1152]{1,0:T(8,128)S(1)}, u32[]{:S(2)}, u32[]{:S(2)}) collective-permute-start(f32[40,1152]{1,0:T(8,128)S(1)} %get-tuple-element.78), channel_id=1, source_target_pairs={{0,4},{32,48},{2,6},{34,50},{4,0},{36,52},{6,2},{38,54},{8,12},{40... | collective-permute-start | bytes 552968 | tf_op jit(solution)/shard_map/ppermute | solution.py:27
  73.7 7.6 %collective-permute-start.18 = (f32[40,1152]{1,0:T(8,128)S(1)}, f32[40,1152]{1,0:T(8,128)S(1)}, u32[]{:S(2)}, u32[]{:S(2)}) collective-permute-start(f32[40,1152]{1,0:T(8,128)S(1)} %get-tuple-element.79), channel_id=1, source_target_pairs={{0,6},{32,56},{2,0},{34,58},{4,2},{36,60},{6,4},{38,62},{8,14},{40... | collective-permute-start | bytes 552968 | tf_op jit(solution)/shard_map/ppermute | solution.py:27
  75.8 6.7 %collective-permute-start.19 = (f32[40,1152]{1,0:T(8,128)S(1)}, f32[40,1152]{1,0:T(8,128)S(1)}, u32[]{:S(2)}, u32[]{:S(2)}) collective-permute-start(f32[40,1152]{1,0:T(8,128)S(1)} %get-tuple-element.80), channel_id=1, source_target_pairs={{0,2},{32,40},{2,4},{34,42},{4,6},{36,44},{6,0},{38,46},{8,10},{40... | collective-permute-start | bytes 552968 | tf_op jit(solution)/shard_map/ppermute | solution.py:27
  76.7 10.2 %collective-permute-start.25 = (f32[32,1152]{1,0:T(8,128)S(1)}, f32[32,1152]{1,0:T(8,128)S(1)}, u32[]{:S(2)}, u32[]{:S(2)}) collective-permute-start(f32[32,1152]{1,0:T(8,128)S(1)} %slice.100), channel_id=1, source_target_pairs={{0,32},{32,0},{2,34},{34,2},{4,36},{36,4},{6,38},{38,6},{8,40},{40... | collective-permute-start | bytes 442376 | tf_op jit(solution)/shard_map/ppermute | solution.py:27
  82.7 5.2 %collective-permute-start.21 = (f32[8,128]{1,0:T(8,128)S(1)}, f32[8,128]{1,0:T(8,128)S(1)}, u32[]{:S(2)}, u32[]{:S(2)}) collective-permute-start(f32[8,128]{1,0:T(8,128)S(1)} %pad_maximum_fusion.8), channel_id=1, source_target_pairs={{0,192},{32,96},{2,194},{34,98},{4,196},{36,100},{6,198},{38,102},... | collective-permute-start | bytes 12296 | tf_op jit(solution)/shard_map/ppermute | solution.py:27
  85.8 7.5 %collective-permute-start.20 = (f32[8,128]{1,0:T(8,128)S(1)}, f32[8,128]{1,0:T(8,128)S(1)}, u32[]{:S(2)}, u32[]{:S(2)}) collective-permute-start(f32[8,128]{1,0:T(8,128)S(1)} %pad_maximum_fusion.8), channel_id=1, source_target_pairs={{0,128},{32,160},{2,130},{34,162},{4,132},{36,164},{6,134},{38,166... | collective-permute-start | bytes 12296 | tf_op jit(solution)/shard_map/ppermute | solution.py:27
  87.9 5.4 %collective-permute-start.26 = (f32[8,128]{1,0:T(8,128)S(1)}, f32[8,128]{1,0:T(8,128)S(1)}, u32[]{:S(2)}, u32[]{:S(2)}) collective-permute-start(f32[8,128]{1,0:T(8,128)S(1)} %collective-permute-done.21), channel_id=1, source_target_pairs={{0,32},{32,0},{2,34},{34,2},{4,36},{36,4},{6,38},{38,6},{8,40},{40... | collective-permute-start | bytes 12296 | tf_op jit(solution)/shard_map/ppermute | solution.py:27
